TPU v7x, 128 devices: a whole 4x4x4 slice. The times are simulated.
128 devices in a mesh: gx: 16 (over z, x), gy: 8 (over y, core).
Axes of the slice: x: 4, y: 4, z: 4, core: 2. Of those that a mesh axis runs over, the one named last changes fastest.
Arguments:
- theta: float32 [80, 1024, 1024], P(None, 'gx', 'gy'), may hold values from -6 to 6
- wind_u: float32 [80, 1024, 1024], P(None, 'gx', 'gy'), may hold values from -1 to 1
- wind_v: float32 [80, 1024, 1024], P(None, 'gx', 'gy'), may hold values from -1 to 1
- level_set: float32 [16, 8, 16, 128, 128], P('gx', 'gy'), may hold values from -6 to 6
- fuel_load: float32 [16, 8, 16, 128, 128], P('gx', 'gy'), may hold values from 0.5 to 1.5
- spread_base: float32 [16, 8, 16, 128, 128], P('gx', 'gy'), may hold values from 0.3 to 3
- tile_owner: int32 [16, 8, 16], P('gx', 'gy'), may hold values from 0 to 15, as said below
- tile_place: int32 [16, 8, 16], P('gx', 'gy'), may hold values from 0 to 511, as said below
Outputs:
- theta_next: float32 [80, 1024, 1024], P(None, 'gx', 'gy')
- level_next: float32 [16, 8, 16, 128, 128], P('gx', 'gy')
- fuel_next: float32 [16, 8, 16, 128, 128], P('gx', 'gy')
Inputs may be any that keep to these rules, and one draw needn't show every extreme that they name: Every tile of device (i, j) lies in the block of a device (tile_owner, j) of the same gy index; at most 2 tiles of one device lie in one owner's block, and in every draw some owner of each gy index holds exactly 2 tiles from every device of that index. `tile_place`: no two computed tiles have the same owner and place.
All inputs are finite; a program needn't handle non-finite values.
Results may differ from a plain program's by a relative error of at most 0.0003.
Values sent between devices are 32-bit elements; how exact they have to be, the bound alone decides.
No kernel may reach another device: no remote copies, remote signals or barrier semaphores. Data moves between devices by JAX's collectives and lax.ppermute only.
A program may use at most 128 MiB of HBM per device.

v0:
```python
import jax
import jax.numpy as jnp
from jax import lax
from jax.sharding import PartitionSpec as P

LZ = 80
TA = 4
R = 32
KSUB = 6
CAP = 2
TPD = 16
S = 128


time_step = 0.03
diffusion = 0.15
burn_rate = 0.15
sharpness = 2.0
regular = 0.01
courant = 0.4
heat_gain = 2.0


def padded_2(cells, sides, width):
    for axis, dim in sides:
        count = lax.axis_size(axis)
        ends = count - 1
        head = lax.slice_in_dim(cells, 0, width, axis=dim)
        tail = lax.slice_in_dim(cells, cells.shape[dim] - width, cells.shape[dim], axis=dim)
        cells = jnp.concatenate(
            [
                lax.ppermute(tail, axis, [(i, (i + 1) % count) for i in range(ends)]),
                cells,
                lax.ppermute(head, axis, [((i + 1) % count, i) for i in range(ends)]),
            ],
            axis=dim,
        )
    return cells


def interp_table():
    where_fine = (jnp.arange(S, dtype=jnp.float32) + 0.5) / R + 0.5
    columns = jnp.arange(TA + 2, dtype=jnp.float32)
    return jnp.maximum(0.0, 1.0 - jnp.abs(where_fine[:, None] - columns[None, :]))


def average_table():
    block_of = jnp.arange(S, dtype=jnp.int32) // R
    coarse = jnp.arange(TA, dtype=jnp.int32)
    return jnp.where(coarse[:, None] == block_of[None, :], 1.0 / R, 0.0).astype(jnp.float32)


def fire_tile(level, fuel, base, wind, average):
    heat = jnp.zeros_like(fuel)
    for substep in range(KSUB):
        padded = jnp.pad(level, 1, mode="edge")
        grad_x = 0.5 * (padded[2:, 1:-1] - padded[:-2, 1:-1])
        grad_y = 0.5 * (padded[1:-1, 2:] - padded[1:-1, :-2])
        laplace = (
            padded[2:, 1:-1]
            + padded[:-2, 1:-1]
            + padded[1:-1, 2:]
            + padded[1:-1, :-2]
            - 4.0 * level
        )
        length = jnp.sqrt(grad_x * grad_x + grad_y * grad_y + regular)
        along = (wind[0] * grad_x + wind[1] * grad_y) / length
        speed = base * jnp.maximum(1.0 + along, 0.0)
        level = level - time_step * speed * length + diffusion * laplace
        used = burn_rate * fuel * jax.nn.sigmoid(-sharpness * level)
        fuel = fuel - used
        heat = heat + used
    flux = jnp.dot(
        jnp.dot(average, heat, precision=lax.Precision.HIGHEST),
        average.T,
        precision=lax.Precision.HIGHEST,
    )
    return (level, fuel, flux)


def body(theta, wind_u, wind_v, level_set, fuel_load, spread_base, tile_owner, tile_place):
    cycle = lax.axis_size("gx")
    cells_x = theta.shape[1]
    cells_y = theta.shape[2]
    tiles_y = cells_y // TA
    interp = interp_table()
    average = average_table()
    owners = tile_owner[0, 0]
    places = tile_place[0, 0]
    same_owner = owners[:, None] == owners[None, :]
    earlier = jnp.arange(TPD)[None, :] < jnp.arange(TPD)[:, None]
    slot_rank = jnp.sum(jnp.logical_and(same_owner, earlier), axis=1)
    slot_index = owners * CAP + slot_rank
    request = jnp.full((cycle * CAP,), -1, jnp.int32).at[slot_index].set(places).reshape(cycle, CAP)
    asked = lax.all_to_all(request, "gx", split_axis=0, concat_axis=0, tiled=True).reshape(
        cycle * CAP
    )
    surface = jnp.stack([wind_u[0], wind_v[0]])
    rimmed = padded_2(surface, (("gx", 1), ("gy", 2)), 1)
    valid = asked >= 0
    safe_place = jnp.maximum(asked, 0)
    start_x = safe_place // tiles_y * TA
    start_y = safe_place % tiles_y * TA

    def cut(left, bottom):
        return lax.dynamic_slice(rimmed, (jnp.int32(0), left, bottom), (2, TA + 2, TA + 2))

    patches = jax.vmap(cut)(start_x, start_y)
    fine_wind = jnp.einsum(
        "ak,tckl,bl->tcab", interp, patches, interp, precision=lax.Precision.HIGHEST
    )
    returned = lax.all_to_all(
        fine_wind.reshape(cycle, CAP, 2, S, S), "gx", split_axis=0, concat_axis=0, tiled=True
    )
    tile_wind = returned.reshape(cycle * CAP, 2, S, S)[slot_index]
    level_out, fuel_out, fluxes = jax.vmap(lambda a, b, c, d: fire_tile(a, b, c, d, average))(
        level_set[0, 0], fuel_load[0, 0], spread_base[0, 0], tile_wind
    )
    outbox = (
        jnp.zeros((cycle * CAP, TA * TA), jnp.float32)
        .at[slot_index]
        .set(fluxes.reshape(TPD, TA * TA))
        .reshape(cycle, CAP, TA * TA)
    )
    padded = padded_2(theta, (("gx", 1), ("gy", 2)), 1)
    advect = courant * (
        jnp.maximum(wind_u, 0.0) * (theta - padded[:, :-2, 1:-1])
        + jnp.minimum(wind_u, 0.0) * (padded[:, 2:, 1:-1] - theta)
        + jnp.maximum(wind_v, 0.0) * (theta - padded[:, 1:-1, :-2])
        + jnp.minimum(wind_v, 0.0) * (padded[:, 1:-1, 2:] - theta)
    )
    inbox = lax.all_to_all(outbox, "gx", split_axis=0, concat_axis=0, tiled=True).reshape(
        cycle * CAP, TA, TA
    )
    offsets = jnp.arange(TA, dtype=jnp.int32)
    row_start = jnp.where(valid, start_x, cells_x + TA)
    index_x = jnp.broadcast_to(
        row_start[:, None, None] + offsets[None, :, None], (cycle * CAP, TA, TA)
    )
    index_y = jnp.broadcast_to(
        start_y[:, None, None] + offsets[None, None, :], (cycle * CAP, TA, TA)
    )
    field = jnp.zeros((cells_x, cells_y), jnp.float32).at[index_x, index_y].add(inbox, mode="drop")
    profile = jnp.exp(-(jnp.arange(LZ, dtype=jnp.float32) + 0.5) / (LZ / 4.0))
    theta_next = theta - advect + heat_gain * field[None, :, :] * profile[:, None, None]
    return (theta_next, level_out[None, None], fuel_out[None, None])


def solution(mesh):
    in_specs = (
        P(None, "gx", "gy"),
        P(None, "gx", "gy"),
        P(None, "gx", "gy"),
        P("gx", "gy", None, None, None),
        P("gx", "gy", None, None, None),
        P("gx", "gy", None, None, None),
        P("gx", "gy", None),
        P("gx", "gy", None),
    )
    out_specs = (
        P(None, "gx", "gy"),
        P("gx", "gy", None, None, None),
        P("gx", "gy", None, None, None),
    )
    return jax.shard_map(body, mesh=mesh, in_specs=in_specs, out_specs=out_specs, check_vma=False)
```

profile of v0, /device:TPU:16, one launch (start us, length us, event | category | flops | bytes accessed | tf_op | source)
XLA Modules:
  0.0 268.7 jit_solution(15603853782876521297)
XLA Ops:
  2.2 3.4 %collective-permute-start.4 = (f32[2,1,128]{2,0,1:T(2,128)S(1)}, f32[2,1,128]{2,0,1:T(2,128)S(1)}, u32[]{:S(2)}, u32[]{:S(2)}) collective-permute-start(f32[2,1,128]{2,0,1:T(2,128)S(1)} %get-tuple-element.63), channel_id=1, source_target_pairs={{0,8},{8,16},{16,24},{24,32},{32,40},{40,48},{48,56},{56,64},{64,7... | collective-permute-start | bytes 3080 | tf_op jit(solution)/shard_map/ppermute | solution.py:32
  9.9 9.0 %all-to-all-start = ((s32[16,1,2]{2,1,0:T(1,128)}), s32[16,1,2]{2,1,0:T(1,128)S(1)}, u32[]{:S(2)}, u32[]{:S(2)}) async-start(s32[16,1,2]{2,1,0:T(1,128)} %bitcast.5), calls=%async_computation | async-start | bytes 16384 | tf_op jit(solution)/shard_map/all_to_all | solution.py:95
  19.0 7.5 %all-to-all-done = s32[16,1,2]{2,1,0:T(1,128)S(1)} async-done(((s32[16,1,2]{2,1,0:T(1,128)}), s32[16,1,2]{2,1,0:T(1,128)S(1)}, u32[]{:S(2)}, u32[]{:S(2)}) %all-to-all-start) | async-done | bytes 160 | tf_op jit(solution)/shard_map/all_to_all | solution.py:95
  27.1 1.9 collective-permute-start.6
  29.0 3.6 %collective-permute-start.7 = (f32[2,66,1]{2,0,1:T(2,128)S(1)}, f32[2,66,1]{2,0,1:T(2,128)S(1)}, u32[]{:S(2)}, u32[]{:S(2)}) collective-permute-start(f32[2,66,1]{2,0,1:T(2,128)S(1)} %get-tuple-element.62), channel_id=1, source_target_pairs={{1,0},{2,1},{3,2},{4,3},{5,4},{6,5},{7,6},{9,8},{10,9},{11,10},{12... | collective-permute-start | bytes 1592 | tf_op jit(solution)/shard_map/ppermute | solution.py:34
  32.7 1.9 collective-permute-done.7
  35.0 63.2 %while.1 = (s32[]{:T(128)}, f32[2,66,130]{2,0,1:T(2,128)S(1)}, s32[32,3]{0,1:T(4,128)S(1)}, f32[32,2,6,6]{3,1,2,0:T(2,128)S(1)}, s32[]{:T(128)}) while((s32[]{:T(128)}, f32[2,66,130]{2,0,1:T(2,128)S(1)}, s32[32,3]{0,1:T(4,128)S(1)}, f32[32,2,6,6]{3,1,2,0:T(2,128)S(1)}, s32[]{:T(128)}) %tuple.54), condition=%wide.while_cond, body=%wide.while_body.sunk | while | flops 2 | bytes 12405 | solution.py:106
  35.6 1.4 bitcast_dynamic-update-slice_fusion.2
  37.5 1.4 bitcast_dynamic-update-slice_fusion.2
  98.9 8.3 %fusion.49 = f32[32,2,128,128]{3,2,1,0:T(8,128)} fusion(f32[32,2,6,128]{3,0,2,1:T(8,128)S(1)} %fusion.64, f32[128]{0:T(128)S(1)} %multiply_add_fusion), kind=kOutput, calls=%fused_computation.133 | convolution fusion | flops 75500544 | bytes 4391424 | tf_op jit(solution)/shard_map/ak,tckl,bl->tcab/dot_general | solution.py:109
  107.2 4.8 %all-to-all-start.1 = ((f32[16,2,2,128,128]{4,3,2,1,0:T(8,128)}), f32[16,2,2,128,128]{4,3,2,1,0:T(8,128)}, u32[]{:S(2)}, u32[]{:S(2)}) async-start(f32[16,2,2,128,128]{4,3,2,1,0:T(8,128)} %bitcast.162), calls=%async_computation.1 | async-start | bytes 8388608 | tf_op jit(solution)/shard_map/all_to_all | solution.py:112
  112.1 3.6 %collective-permute-start = (f32[80,1,128]{2,1,0:T(1,128)S(1)}, f32[80,1,128]{2,1,0:T(1,128)S(1)}, u32[]{:S(2)}, u32[]{:S(2)}) collective-permute-start(f32[80,1,128]{2,1,0:T(1,128)S(1)} %get-tuple-element.35), channel_id=1, source_target_pairs={{0,8},{8,16},{16,24},{24,32},{32,40},{40,48},{48,56},{56,64},{64,7... | collective-permute-start | bytes 122888 | tf_op jit(solution)/shard_map/ppermute | solution.py:32
  119.3 1.7 fusion.110
  121.6 47.7 %collective-permute-done = f32[80,1,128]{2,1,0:T(1,128)S(1)} collective-permute-done((f32[80,1,128]{2,1,0:T(1,128)S(1)}, f32[80,1,128]{2,1,0:T(1,128)S(1)}, u32[]{:S(2)}, u32[]{:S(2)}) %collective-permute-start) | collective-permute-done | bytes 40992 | tf_op jit(solution)/shard_map/ppermute | solution.py:32
  169.3 6.9 %collective-permute-done.1 = f32[80,1,128]{2,1,0:T(1,128)S(1)} collective-permute-done((f32[80,1,128]{2,1,0:T(1,128)S(1)}, f32[80,1,128]{2,1,0:T(1,128)S(1)}, u32[]{:S(2)}, u32[]{:S(2)}) %collective-permute-start.1) | collective-permute-done | bytes 40992 | tf_op jit(solution)/shard_map/ppermute | solution.py:34
  176.7 2.6 fusion.103
  179.3 2.7 %copy.65 = f32[80,66,1]{0,1,2:T(8,128)S(1)} copy(f32[80,66,1]{2,1,0:T(8,128)} %get-tuple-element.33) | data formatting | bytes 42240 | tf_op jit(solution)/shard_map/slice | solution.py:29
  182.1 2.5 collective-permute-start.2
  185.6 3.2 %collective-permute-start.3 = (f32[80,66,1]{0,1,2:T(8,128)S(1)}, f32[80,66,1]{0,1,2:T(8,128)S(1)}, u32[]{:S(2)}, u32[]{:S(2)}) collective-permute-start(f32[80,66,1]{0,1,2:T(8,128)S(1)} %copy.67), channel_id=1, source_target_pairs={{1,0},{2,1},{3,2},{4,3},{5,4},{6,5},{7,6},{9,8},{10,9},{11,10},{12... | collective-permute-start | bytes 63368 | tf_op jit(solution)/shard_map/ppermute | solution.py:34
  188.8 3.0 %gather_fusion = f32[16,2,128,128]{3,2,1,0:T(8,128)S(1)} fusion(f32[32,2,128,128]{3,2,1,0:T(8,128)} %bitcast.15, s32[1024]{0:T(1024)S(1)} %pad_clamp_fusion), kind=kCustom, calls=%fused_computation | custom fusion | bytes 4194368 | tf_op jit(solution)/shard_map/gather | solution.py:115
  191.8 5.5 %fusion.17 = f32[16,128,128]{2,1,0:T(8,128)S(1)} fusion(f32[16,128,128]{2,1,0:T(8,128)} %bitcast.165, f32[1,1,16,128,128]{4,3,2,1,0:T(8,128)S(1)} %copy-done, f32[16,130,1]{2,1,0:T(8,128)} %get-tuple-element.48, f32[16,1,128]{2,1,0:T(1,128)S(1)} %get-tuple-element.60, f32[16,1,128]{2,1,0:T(1,128)S(1)} %get-tuple-element.59, ...), kind=kLoop, calls=%fused_computation.94 | loop fusion | flops 8650752 | bytes 5275904 | tf_op jit(solution)/shard_map/vmap()/add | solution.py:69
  197.7 2.2 fusion.21
  200.4 2.2 fusion.25
  203.1 2.2 fusion.29
  205.8 2.2 fusion.33
  209.3 4.5 %subtract_bitcast_fusion = (f32[1,1,16,128,128]{4,3,2,1,0:T(8,128)}, f32[16,128,128]{2,1,0:T(8,128)S(1)}) fusion(f32[16,128,128]{2,1,0:T(8,128)S(1)} %fusion.33, f32[16,128,128]{2,1,0:T(8,128)S(1)} %fusion.29, f32[16,128,128]{2,1,0:T(8,128)S(1)} %fusion.25, f32[16,128,128]{2,1,0:T(8,128)S(1)} %fusion.21, f32[16,128,128]{2,1,0:T(8,128)S(1)} %fusion.17, ...), kind=kLoop, calls=%fused_computation.118 | loop fusion | flops 19660800 | bytes 11567360 | tf_op jit(solution)/shard_map/broadcast_in_dim | solution.py:146
  213.8 2.5 fusion.39
  217.9 6.0 %all-to-all-start.2 = ((f32[16,2,16]{2,1,0:T(2,128)}), f32[16,2,16]{2,1,0:T(2,128)S(1)}, u32[]{:S(2)}, u32[]{:S(2)}) async-start(f32[16,2,16]{2,1,0:T(2,128)} %bitcast.20), calls=%async_computation.2 | async-start | bytes 32768 | tf_op jit(solution)/shard_map/all_to_all | solution.py:132
  225.3 2.5 copy.68
  227.8 3.7 %all-to-all-done.2 = f32[16,2,16]{2,1,0:T(2,128)S(1)} async-done(((f32[16,2,16]{2,1,0:T(2,128)}), f32[16,2,16]{2,1,0:T(2,128)S(1)}, u32[]{:S(2)}, u32[]{:S(2)}) %all-to-all-start.2) | async-done | bytes 2080 | tf_op jit(solution)/shard_map/all_to_all | solution.py:132
  231.6 25.4 %scatter_fusion = f32[64,128]{1,0:T(8,128)S(1)} fusion(f32[64,128]{1,0:T(8,128)S(1)} %broadcast_in_dim.36, s32[512]{0:T(512)S(1)} %reshape.317, f32[512]{0:T(512)S(1)} %reshape.319), kind=kCustom, calls=%fused_computation.3 | custom fusion | flops 512 | bytes 10240 | tf_op jit(solution)/shard_map/scatter-add | solution.py:143
  257.0 11.7 %fusion.5 = f32[80,64,128]{2,1,0:T(8,128)} fusion(f32[80,64,128]{2,1,0:T(8,128)} %param.8, f32[80,66,1]{2,1,0:T(8,128)} %copy.68, f32[80,1,128]{2,1,0:T(1,128)S(1)} %collective-permute-done.1, f32[80,1,128]{2,1,0:T(1,128)S(1)} %collective-permute-done, f32[80,66,1]{2,1,0:T(8,128)S(1)} %copy.66, f32[80,64,128]{2,1,0:T(8,128)} %param.10, ...), kind=kLoop, calls=%fused_computation.13 | loop fusion | flops 17694720 | bytes 10643008 | tf_op jit(solution)/shard_map/add | solution.py:145
  (171 shorter events, 79.7 us)
Async XLA Ops:
  2.2 24.7 %collective-permute-start.4 = (f32[2,1,128]{2,0,1:T(2,128)S(1)}, f32[2,1,128]{2,0,1:T(2,128)S(1)}, u32[]{:S(2)}, u32[]{:S(2)}) collective-permute-start(f32[2,1,128]{2,0,1:T(2,128)S(1)} %get-tuple-element.63), channel_id=1, source_target_pairs={{0,8},{8,16},{16,24},{24,32},{32,40},{40,48},{48,56},{56,64},{64,7... | collective-permute-start | bytes 3080 | tf_op jit(solution)/shard_map/ppermute | solution.py:32
  5.6 21.3 %collective-permute-start.5 = (f32[2,1,128]{2,0,1:T(2,128)S(1)}, f32[2,1,128]{2,0,1:T(2,128)S(1)}, u32[]{:S(2)}, u32[]{:S(2)}) collective-permute-start(f32[2,1,128]{2,0,1:T(2,128)S(1)} %get-tuple-element.64), channel_id=1, source_target_pairs={{8,0},{16,8},{24,16},{32,24},{40,32},{48,40},{56,48},{64,56},{72,6... | collective-permute-start | bytes 3080 | tf_op jit(solution)/shard_map/ppermute | solution.py:34
  9.9 16.5 %all-to-all-start = ((s32[16,1,2]{2,1,0:T(1,128)}), s32[16,1,2]{2,1,0:T(1,128)S(1)}, u32[]{:S(2)}, u32[]{:S(2)}) async-start(s32[16,1,2]{2,1,0:T(1,128)} %bitcast.5), calls=%async_computation | async-start | bytes 16384 | tf_op jit(solution)/shard_map/all_to_all | solution.py:95
  27.1 5.6 %collective-permute-start.6 = (f32[2,66,1]{2,0,1:T(2,128)S(1)}, f32[2,66,1]{2,0,1:T(2,128)S(1)}, u32[]{:S(2)}, u32[]{:S(2)}) collective-permute-start(f32[2,66,1]{2,0,1:T(2,128)S(1)} %get-tuple-element.61), channel_id=1, source_target_pairs={{0,1},{1,2},{2,3},{3,4},{4,5},{5,6},{6,7},{8,9},{9,10},{10,11},{11... | collective-permute-start | bytes 1592 | tf_op jit(solution)/shard_map/ppermute | solution.py:32
  29.0 5.6 %collective-permute-start.7 = (f32[2,66,1]{2,0,1:T(2,128)S(1)}, f32[2,66,1]{2,0,1:T(2,128)S(1)}, u32[]{:S(2)}, u32[]{:S(2)}) collective-permute-start(f32[2,66,1]{2,0,1:T(2,128)S(1)} %get-tuple-element.62), channel_id=1, source_target_pairs={{1,0},{2,1},{3,2},{4,3},{5,4},{6,5},{7,6},{9,8},{10,9},{11,10},{12... | collective-permute-start | bytes 1592 | tf_op jit(solution)/shard_map/ppermute | solution.py:34
  107.2 4.8 %copy-start.1 = (f32[80,64,128]{2,1,0:T(8,128)S(1)}, f32[80,64,128]{2,1,0:T(8,128)}, u32[]{:S(2)}) copy-start(f32[80,64,128]{2,1,0:T(8,128)} %param.8) | copy-start | bytes 7864324
  107.2 81.6 %all-to-all-start.1 = ((f32[16,2,2,128,128]{4,3,2,1,0:T(8,128)}), f32[16,2,2,128,128]{4,3,2,1,0:T(8,128)}, u32[]{:S(2)}, u32[]{:S(2)}) async-start(f32[16,2,2,128,128]{4,3,2,1,0:T(8,128)} %bitcast.162), calls=%async_computation.1 | async-start | bytes 8388608 | tf_op jit(solution)/shard_map/all_to_all | solution.py:112
  112.1 57.2 %collective-permute-start = (f32[80,1,128]{2,1,0:T(1,128)S(1)}, f32[80,1,128]{2,1,0:T(1,128)S(1)}, u32[]{:S(2)}, u32[]{:S(2)}) collective-permute-start(f32[80,1,128]{2,1,0:T(1,128)S(1)} %get-tuple-element.35), channel_id=1, source_target_pairs={{0,8},{8,16},{16,24},{24,32},{32,40},{40,48},{48,56},{56,64},{64,7... | collective-permute-start | bytes 122888 | tf_op jit(solution)/shard_map/ppermute | solution.py:32
  115.8 60.5 %collective-permute-start.1 = (f32[80,1,128]{2,1,0:T(1,128)S(1)}, f32[80,1,128]{2,1,0:T(1,128)S(1)}, u32[]{:S(2)}, u32[]{:S(2)}) collective-permute-start(f32[80,1,128]{2,1,0:T(1,128)S(1)} %get-tuple-element.36), channel_id=1, source_target_pairs={{8,0},{16,8},{24,16},{32,24},{40,32},{48,40},{56,48},{64,56},{72,6... | collective-permute-start | bytes 122888 | tf_op jit(solution)/shard_map/ppermute | solution.py:34
  182.1 42.1 %collective-permute-start.2 = (f32[80,66,1]{0,1,2:T(8,128)S(1)}, f32[80,66,1]{0,1,2:T(8,128)S(1)}, u32[]{:S(2)}, u32[]{:S(2)}) collective-permute-start(f32[80,66,1]{0,1,2:T(8,128)S(1)} %copy.65), channel_id=1, source_target_pairs={{0,1},{1,2},{2,3},{3,4},{4,5},{5,6},{6,7},{8,9},{9,10},{10,11},{11... | collective-permute-start | bytes 63368 | tf_op jit(solution)/shard_map/ppermute | solution.py:32
  185.6 39.7 %collective-permute-start.3 = (f32[80,66,1]{0,1,2:T(8,128)S(1)}, f32[80,66,1]{0,1,2:T(8,128)S(1)}, u32[]{:S(2)}, u32[]{:S(2)}) collective-permute-start(f32[80,66,1]{0,1,2:T(8,128)S(1)} %copy.67), channel_id=1, source_target_pairs={{1,0},{2,1},{3,2},{4,3},{5,4},{6,5},{7,6},{9,8},{10,9},{11,10},{12... | collective-permute-start | bytes 63368 | tf_op jit(solution)/shard_map/ppermute | solution.py:34
  188.8 3.0 %copy-start = (f32[1,1,16,128,128]{4,3,2,1,0:T(8,128)S(1)}, f32[1,1,16,128,128]{4,3,2,1,0:T(8,128)}, u32[]{:S(2)}) copy-start(f32[1,1,16,128,128]{4,3,2,1,0:T(8,128)} %param.13) | copy-start | bytes 3145732
  208.1 1.2 copy-start.2
  213.8 2.5 copy-start.3
  217.9 13.6 %all-to-all-start.2 = ((f32[16,2,16]{2,1,0:T(2,128)}), f32[16,2,16]{2,1,0:T(2,128)S(1)}, u32[]{:S(2)}, u32[]{:S(2)}) async-start(f32[16,2,16]{2,1,0:T(2,128)} %bitcast.20), calls=%async_computation.2 | async-start | bytes 32768 | tf_op jit(solution)/shard_map/all_to_all | solution.py:132
where the time goes:
time: 270 us; the launch traced here: 269 us
  local copies, waits for them, and re-layouts  86.8 us (32%)
  waiting for transfers between devices  67.7 us (25%)
  other arithmetic  60.6 us (22%)
  starting transfers between devices  40.7 us (15%)
  matrix products  11.6 us (4%)
    gather x96, local copies, waits for them, and re-layouts  63.2 us
    ppermute x4, waiting for transfers between devices, padded_2(): lax.ppermute(tail, axis, [(i, (i + 1) % count) for i in range(ends)])  47.8 us
    scatter-add x1, other arithmetic, body(): jnp.zeros((cells_x, cells_y), jnp.float32).at[index_x, index_y]  25.4 us
    add x5, other arithmetic, fire_tile(): level = level - time_step * speed * length + diffusion * laplace  14.2 us
    add x1, other arithmetic, body(): theta - advect + heat_gain * field[None, :, :] * profile[:, None, None]  11.7 us
    ppermute x4, starting transfers between devices, padded_2(): lax.ppermute(tail, axis, [(i, (i + 1) % count) for i in range(ends)])  11.5 us
    ppermute x4, starting transfers between devices, padded_2(): lax.ppermute(head, axis, [((i + 1) % count, i) for i in range(ends)])  9.45 us
    all_to_all x1, starting transfers between devices, body(): lax.all_to_all(request, 'gx', split_axis=0, concat_axis=0, tiled=True)  9.03 us
  transfers between devices with their start and end apart: 11, of which 5 were waited for; matrix products, arithmetic and copies ran while one was open for 17% of the time, Pallas kernels for 0%

commit v1 on v0

v1 whole, which is shorter than its diff:
```python
import functools

import jax
import jax.numpy as jnp
from jax import lax
from jax.experimental import pallas as pl
from jax.experimental.pallas import tpu as pltpu
from jax.sharding import PartitionSpec as P

LZ = 80
TA = 4
R = 32
KSUB = 6
CAP = 2
TPD = 16
S = 128
CX = 64
CY = 128
ROWS = S // 8
BLOCK = 2 * CX + 8
RIM = 8

time_step = 0.03
diffusion = 0.15
burn_rate = 0.15
regular = 0.01
courant = 0.4
heat_gain = 2.0

F32 = jnp.float32


def iota(dim, shape=(8, 128)):
    return lax.broadcasted_iota(jnp.int32, shape, dim)


def wind_edge_kernel(u_ref, v_ref, up_ref, down_ref):
    columns = jnp.transpose(jnp.concatenate([u_ref[0], v_ref[0]], axis=0))
    row = iota(0)
    last = jnp.broadcast_to(columns[CY - 1 : CY], (8, 128))
    first = jnp.broadcast_to(columns[0:1], (8, 128))
    up_ref[...] = jnp.where(row == 0, last, 0.0)
    down_ref[...] = jnp.where(row == TA + 1, first, 0.0)


def wind_edges(wind_u, wind_v):
    surface = pl.BlockSpec((1, CX, CY), lambda i: (0, 0, 0))
    edge = pl.BlockSpec((8, 128), lambda i: (0, 0))
    return pl.pallas_call(
        wind_edge_kernel,
        grid=(1,),
        in_specs=[surface, surface],
        out_specs=[edge, edge],
        out_shape=[jax.ShapeDtypeStruct((8, 128), F32)] * 2,
        name="wind_edges",
    )(wind_u, wind_v)


def pack_kernel(u_ref, v_ref, low_ref, high_ref, out_ref):
    block = jnp.concatenate([u_ref[0], v_ref[0], low_ref[...] + high_ref[...]], axis=0)
    for peer in range(out_ref.shape[0]):
        out_ref[peer] = block


def pack_winds(wind_u, wind_v, low, high, peers):
    surface = pl.BlockSpec((1, CX, CY), lambda i: (0, 0, 0))
    edge = pl.BlockSpec((8, 128), lambda i: (0, 0))
    return pl.pallas_call(
        pack_kernel,
        grid=(1,),
        in_specs=[surface, surface, edge, edge],
        out_specs=pl.BlockSpec((peers, BLOCK, 128), lambda i: (0, 0, 0)),
        out_shape=jax.ShapeDtypeStruct((peers, BLOCK, 128), F32),
        name="pack_winds",
    )(wind_u, wind_v, low, high)


def theta_edge_kernel(levels, theta_ref, west_ref, east_ref, south_ref, north_ref):
    step = pl.program_id(0)

    @pl.when(step == 0)
    def _():
        south_ref[...] = jnp.zeros_like(south_ref)
        north_ref[...] = jnp.zeros_like(north_ref)

    lane = iota(1, (CX, 128))
    south, north = south_ref[...], north_ref[...]
    for k in range(levels):
        z = step * levels + k
        cells = theta_ref[k]
        west_ref[k : k + 1] = cells[0:1]
        east_ref[k : k + 1] = cells[CX - 1 : CX]
        south = jnp.where(lane == z, pltpu.roll(cells, z, 1), south)
        north = jnp.where(lane == z, pltpu.roll(cells, z + 1, 1), north)
    south_ref[...] = south
    north_ref[...] = north


def theta_edges(theta):
    levels = 16
    row = pl.BlockSpec((levels, 128), lambda i: (i, 0))
    column = pl.BlockSpec((CX, 128), lambda i: (0, 0))
    rows = jax.ShapeDtypeStruct((LZ, 128), F32)
    columns = jax.ShapeDtypeStruct((CX, 128), F32)
    return pl.pallas_call(
        functools.partial(theta_edge_kernel, levels),
        grid=(LZ // levels,),
        in_specs=[pl.BlockSpec((levels, CX, CY), lambda i: (i, 0, 0))],
        out_specs=[row, row, column, column],
        out_shape=[rows, rows, columns, columns],
        name="theta_edges",
        cost_estimate=pl.CostEstimate(flops=4_000_000, bytes_accessed=2_800_000, transcendentals=0),
    )(theta)


def advect_kernel(levels, theta_ref, u_ref, v_ref, west_ref, east_ref, south_ref, north_ref, out_ref):
    step = pl.program_id(0)
    lane = iota(1, (CX, 128))
    row = iota(0, (CX, 128))
    for k in range(levels):
        z = step * levels + k
        t = theta_ref[k]
        u = u_ref[k]
        v = v_ref[k]
        west = jnp.where(row == 0, west_ref[k : k + 1], pltpu.roll(t, 1, 0))
        east = jnp.where(row == CX - 1, east_ref[k : k + 1], pltpu.roll(t, CX - 1, 0))
        back = lax.rem(128 - z, 128)
        south = jnp.where(lane == 0, pltpu.roll(south_ref[...], back, 1), pltpu.roll(t, 1, 1))
        north = jnp.where(lane == CY - 1, pltpu.roll(north_ref[...], 127 - z, 1), pltpu.roll(t, CY - 1, 1))
        change = (
            jnp.maximum(u, 0.0) * (t - west)
            + jnp.minimum(u, 0.0) * (east - t)
            + jnp.maximum(v, 0.0) * (t - south)
            + jnp.minimum(v, 0.0) * (north - t)
        )
        out_ref[k] = t - courant * change


def advect(theta, wind_u, wind_v, west, east, south, north):
    levels = 8
    cells = pl.BlockSpec((levels, CX, CY), lambda i: (i, 0, 0))
    row = pl.BlockSpec((levels, 128), lambda i: (i, 0))
    column = pl.BlockSpec((CX, 128), lambda i: (0, 0))
    return pl.pallas_call(
        functools.partial(advect_kernel, levels),
        grid=(LZ // levels,),
        in_specs=[cells, cells, cells, row, row, column, column],
        out_specs=cells,
        out_shape=jax.ShapeDtypeStruct((LZ, CX, CY), F32),
        name="advect",
        cost_estimate=pl.CostEstimate(flops=14_000_000, bytes_accessed=10_500_000, transcendentals=0),
    )(theta, wind_u, wind_v, west, east, south, north)


def fire_kernel(
    peers, owner_ref, place_ref, winds_ref, level_ref, fuel_ref, base_ref,
    level_out, fuel_out, outbox, surface, edges, wind, count,
):
    step = pl.program_id(0)
    lane = iota(1)
    row = iota(0)

    @pl.when(step == 0)
    def _():
        for c in range(2):
            surface[c, 0:RIM] = jnp.zeros((RIM, 128), F32)
            surface[c, RIM + peers * CX :] = jnp.zeros((RIM, 128), F32)
            edges[c, 0:RIM] = jnp.zeros((RIM, 128), F32)
            edges[c, RIM + peers * CX :] = jnp.zeros((RIM, 128), F32)
        for d in range(peers):
            count[d] = 0
            turned = jnp.transpose(
                jnp.concatenate([winds_ref[d, 2 * CX :], jnp.zeros((120, 128), F32)], axis=0)
            )
            for c in range(2):
                surface[c, RIM + d * CX : RIM + (d + 1) * CX] = winds_ref[d, c * CX : (c + 1) * CX]
                edges[c, RIM + d * CX : RIM + (d + 1) * CX] = turned[c * CX : (c + 1) * CX]
        for d in range(peers * CAP):
            outbox[d] = jnp.where(row < TA, 0.0, -1.0)

    owner = owner_ref[step]
    place = place_ref[step]
    tiles_y = CY // TA
    x_own = place // tiles_y * TA
    y_own = lax.rem(place, tiles_y) * TA
    first = owner * CX + x_own + (RIM - 1)

    low_row = (row + 1) // 2
    low_lane = (lane + R // 2) // R
    part_row = jnp.where(row % 2 == 0, 0.5, 0.0) + 0.5 / R
    part_lane = (lane.astype(F32) + 0.5) / R + 0.5 - low_lane.astype(F32)
    outside = jnp.logical_or(
        jnp.logical_and(lane == 0, y_own == 0), jnp.logical_and(lane == TA + 1, y_own == CY - TA)
    )
    back = lax.rem(CY + 1 - y_own, CY)
    for c in range(2):
        patch = pltpu.roll(surface[c, pl.ds(first, 8), :], back, 1)
        patch = jnp.where(outside, edges[c, pl.ds(first, 8), :], patch)
        left = jnp.take_along_axis(patch, low_lane, axis=1)
        right = jnp.take_along_axis(patch, low_lane + 1, axis=1)
        fine = left + (right - left) * part_lane
        below = jnp.take_along_axis(fine, low_row, axis=0)
        above = jnp.take_along_axis(fine, low_row + 1, axis=0)
        rise = above - below
        begin = below + rise * part_row
        slope = rise * (1.0 / R)
        for k in range(ROWS):
            wind[c, k] = begin + slope * float(k)

    level = [level_ref[0, pl.ds(k, 8, stride=ROWS), :] for k in range(ROWS)]
    fuel = [fuel_ref[0, pl.ds(k, 8, stride=ROWS), :] for k in range(ROWS)]
    heat = sum(fuel[1:], fuel[0])
    rate = [base_ref[0, pl.ds(k, 8, stride=ROWS), :] * (0.5 * time_step) for k in range(ROWS)]
    for _ in range(KSUB):
        before = jnp.where(row == 0, level[0], pltpu.roll(level[-1], 1, 0))
        after = jnp.where(row == 7, level[-1], pltpu.roll(level[0], 7, 0))
        rimmed = [before, *level, after]
        new = []
        for k in range(ROWS):
            cell = rimmed[k + 1]
            west, east = rimmed[k], rimmed[k + 2]
            south = jnp.where(lane == 0, cell, pltpu.roll(cell, 1, 1))
            north = jnp.where(lane == S - 1, cell, pltpu.roll(cell, S - 1, 1))
            dx = east - west
            dy = north - south
            square = dx * dx + dy * dy + 4.0 * regular
            length = square * lax.rsqrt(square)
            move = jnp.maximum(length + (wind[0, k] * dx + wind[1, k] * dy), 0.0)
            around = (east + west) + (north + south)
            cell = cell * (1.0 - 4.0 * diffusion) + around * diffusion - rate[k] * move
            fuel[k] = fuel[k] * ((1.0 - 0.5 * burn_rate) + (0.5 * burn_rate) * jnp.tanh(cell))
            new.append(cell)
        level = new
    for k in range(ROWS):
        level_out[0, pl.ds(k, 8, stride=ROWS), :] = level[k]
        fuel_out[0, pl.ds(k, 8, stride=ROWS), :] = fuel[k]
    heat = (heat - sum(fuel[1:], fuel[0])) * (1.0 / (R * R))
    heat = heat + pltpu.roll(heat, 7, 0)

    message = jnp.where(row < TA, 0.0, (x_own + row - TA).astype(F32))
    rows = jnp.take_along_axis(heat, jnp.minimum(2 * row, 7), axis=0)
    for b in range(TA):
        total = jnp.sum(jnp.where(lane // R == b, rows, 0.0), axis=1, keepdims=True)
        message = jnp.where(jnp.logical_and(row < TA, lane == y_own + b), total, message)
    rank = count[owner]
    count[owner] = rank + 1
    outbox[owner * CAP + rank] = message


def fire(owners, places, winds, level_set, fuel_load, spread_base, peers):
    tile = pl.BlockSpec((1, S, S), lambda i: (i, 0, 0))
    scalars = pl.BlockSpec(memory_space=pltpu.SMEM)
    rows = peers * CX + 2 * RIM
    return pl.pallas_call(
        functools.partial(fire_kernel, peers),
        grid=(TPD,),
        in_specs=[
            scalars,
            scalars,
            pl.BlockSpec((peers, BLOCK, 128), lambda i: (0, 0, 0)),
            tile,
            tile,
            tile,
        ],
        out_specs=[tile, tile, pl.BlockSpec((peers * CAP, 8, 128), lambda i: (0, 0, 0))],
        out_shape=[
            jax.ShapeDtypeStruct((TPD, S, S), F32),
            jax.ShapeDtypeStruct((TPD, S, S), F32),
            jax.ShapeDtypeStruct((peers * CAP, 8, 128), F32),
        ],
        scratch_shapes=[
            pltpu.VMEM((2, rows, 128), F32),
            pltpu.VMEM((2, rows, 128), F32),
            pltpu.VMEM((2, ROWS, 8, 128), F32),
            pltpu.SMEM((peers,), jnp.int32),
        ],
        name="fire",
        compiler_params=pltpu.CompilerParams(vmem_limit_bytes=24 * 1024 * 1024),
        cost_estimate=pl.CostEstimate(
            flops=50_000_000, bytes_accessed=6_500_000, transcendentals=3_200_000
        ),
    )(owners, places, winds, level_set, fuel_load, spread_base)


def final_kernel(levels, inbox_ref, part_ref, out_ref, field):
    step = pl.program_id(0)

    @pl.when(step == 0)
    def _():
        inbox = inbox_ref[...]
        slots = inbox.shape[0]
        position = pltpu.roll(inbox, TA, 1).reshape(slots * 8, 128)
        values = inbox.reshape(slots * 8, 128)
        lane = iota(1, (slots * 8, 128)).astype(F32)
        valid = iota(0, (slots * 8, 128)) % 8 < TA
        hot = jnp.where(jnp.logical_and(valid, lane == position), 1.0, 0.0)
        total = lax.dot_general(
            hot, values, (((0,), (0,)), ((), ())),
            precision=lax.Precision.HIGHEST, preferred_element_type=F32,
        )
        field[...] = total[:CX]

    for k in range(levels):
        z = (jnp.full((8, 128), step * levels + k, jnp.int32)).astype(F32)
        gain = heat_gain * jnp.exp((z + 0.5) * (-4.0 / LZ))
        out_ref[k] = part_ref[k] + field[...] * jnp.concatenate([gain] * (CX // 8), axis=0)


def finish(inbox, part):
    levels = 16
    cells = pl.BlockSpec((levels, CX, CY), lambda i: (i, 0, 0))
    return pl.pallas_call(
        functools.partial(final_kernel, levels),
        grid=(LZ // levels,),
        in_specs=[pl.BlockSpec(inbox.shape, lambda i: (0, 0, 0)), cells],
        out_specs=cells,
        out_shape=jax.ShapeDtypeStruct((LZ, CX, CY), F32),
        scratch_shapes=[pltpu.VMEM((CX, CY), F32)],
        name="finish",
        cost_estimate=pl.CostEstimate(flops=3_000_000, bytes_accessed=5_300_000, transcendentals=0),
    )(inbox, part)


def shifted(cells, axis, up):
    ends = lax.axis_size(axis) - 1
    pairs = [(i, i + 1) if up else (i + 1, i) for i in range(ends)]
    return lax.ppermute(cells, axis, pairs)


def exchange(cells, peers):
    return lax.all_to_all(cells, "gx", split_axis=0, concat_axis=0, tiled=True)


def body(theta, wind_u, wind_v, level_set, fuel_load, spread_base, tile_owner, tile_place):
    peers = lax.axis_size("gx")
    up, down = wind_edges(wind_u, wind_v)
    low = shifted(up, "gy", True)
    high = shifted(down, "gy", False)
    winds = exchange(pack_winds(wind_u, wind_v, low, high, peers), peers)

    first_x, last_x, first_y, last_y = theta_edges(theta)
    west = shifted(last_x, "gx", True)
    east = shifted(first_x, "gx", False)
    south = shifted(last_y, "gy", True)
    north = shifted(first_y, "gy", False)
    part = advect(theta, wind_u, wind_v, west, east, south, north)

    level_out, fuel_out, outbox = fire(
        tile_owner[0, 0], tile_place[0, 0], winds, level_set[0, 0], fuel_load[0, 0], spread_base[0, 0], peers
    )
    inbox = exchange(outbox, peers)
    theta_next = finish(inbox, part)
    return (theta_next, level_out[None, None], fuel_out[None, None])


def solution(mesh):
    in_specs = (
        P(None, "gx", "gy"),
        P(None, "gx", "gy"),
        P(None, "gx", "gy"),
        P("gx", "gy", None, None, None),
        P("gx", "gy", None, None, None),
        P("gx", "gy", None, None, None),
        P("gx", "gy", None),
        P("gx", "gy", None),
    )
    out_specs = (
        P(None, "gx", "gy"),
        P("gx", "gy", None, None, None),
        P("gx", "gy", None, None, None),
    )
    return jax.shard_map(body, mesh=mesh, in_specs=in_specs, out_specs=out_specs, check_vma=False)
```

time: 270 us -> 96.2 us (0.36)
  the two profiles are of different devices: /device:TPU:16 before, /device:TPU:41 now
where the time goes in v1:
time: 96.2 us; the launch traced here: 95.3 us
  Pallas kernels  36.4 us (38%)
  starting transfers between devices  24.9 us (26%)
  blocking collectives  24 us (25%)
  waiting for transfers between devices  6.69 us (7%)
  local copies, waits for them, and re-layouts  2.53 us (3%)
    all_to_all x1, blocking collectives, exchange(): return lax.all_to_all(cells, 'gx', split_axis=0, concat_axis=0, tiled=True)  24 us
    ppermute x6, starting transfers between devices, shifted(): return lax.ppermute(cells, axis, pairs)  20.4 us
    pallas_call x1, Pallas kernels, fire(): pl.pallas_call(functools.partial(fire_kernel, peers), grid=(TPD,), in_spe...  13.8 us
    pallas_call x1, Pallas kernels, advect(): pl.pallas_call(functools.partial(advect_kernel, levels), grid=(LZ // leve...  9.36 us
    ppermute x6, waiting for transfers between devices, shifted(): return lax.ppermute(cells, axis, pairs)  6.69 us
    pallas_call x1, Pallas kernels, finish(): pl.pallas_call(functools.partial(final_kernel, levels), grid=(LZ // level...  5.06 us
    pallas_call x1, Pallas kernels, theta_edges(): pl.pallas_call(functools.partial(theta_edge_kernel, levels), grid=(LZ //...  4.83 us
    all_to_all x1, starting transfers between devices, exchange(): return lax.all_to_all(cells, 'gx', split_axis=0, concat_axis=0, tiled=True)  4.54 us
  transfers between devices with their start and end apart: 7, of which 2 were waited for; matrix products, arithmetic and copies ran while one was open for 0% of the time, Pallas kernels for 15%

profile of v1, /device:TPU:41, one launch (start us, length us, event | category | flops | bytes accessed | tf_op | source)
XLA Modules:
  0.0 95.3 jit_solution(5481660465721099397)
XLA Ops:
  0.6 1.5 %wind_edges.1 = (f32[8,128]{1,0:T(8,128)}, f32[8,128]{1,0:T(8,128)}) custom-call(f32[80,64,128]{2,1,0:T(8,128)} %u_ref.5, f32[80,64,128]{2,1,0:T(8,128)} %v_ref.5), custom_call_target="tpu_custom_call" | custom-call | tf_op jit(solution)/shard_map/wind_edges/pallas_call | solution.py:49
  2.1 3.8 %collective-permute-start = (f32[8,128]{1,0:T(8,128)}, f32[8,128]{1,0:T(8,128)S(1)}, u32[]{:S(2)}, u32[]{:S(2)}) collective-permute-start(f32[8,128]{1,0:T(8,128)} %get-tuple-element.12), channel_id=1, source_target_pairs={{0,1},{1,2},{2,3},{3,4},{4,5},{5,6},{6,7},{8,9},{9,10},{10,11},{11... | collective-permute-start | bytes 12296 | tf_op jit(solution)/shard_map/ppermute | solution.py:327
  5.9 0.0 copy-start
  5.9 0.0 copy-start.1
  5.9 0.0 copy-start.2
  5.9 0.0 copy-start.3
  5.9 0.0 copy-start.4
  5.9 2.2 %collective-permute-start.1 = (f32[8,128]{1,0:T(8,128)}, f32[8,128]{1,0:T(8,128)S(1)}, u32[]{:S(2)}, u32[]{:S(2)}) collective-permute-start(f32[8,128]{1,0:T(8,128)} %get-tuple-element.13), channel_id=1, source_target_pairs={{1,0},{2,1},{3,2},{4,3},{5,4},{6,5},{7,6},{9,8},{10,9},{11,10},{12... | collective-permute-start | bytes 12296 | tf_op jit(solution)/shard_map/ppermute | solution.py:327
  8.1 0.0 collective-permute-done.low_ref
  8.1 0.0 copy-start.10
  8.1 3.2 %collective-permute-done.1.high_ref = f32[8,128]{1,0:T(8,128)S(1)} collective-permute-done((f32[8,128]{1,0:T(8,128)}, f32[8,128]{1,0:T(8,128)S(1)}, u32[]{:S(2)}, u32[]{:S(2)}) %collective-permute-start.1) | collective-permute-done | bytes 4128 | tf_op jit(solution)/shard_map/ppermute | solution.py:327
  11.3 0.6 copy-done.11
  11.9 1.8 %pack_winds.1 = f32[16,136,128]{2,1,0:T(8,128)} custom-call(f32[80,64,128]{2,1,0:T(8,128)} %u_ref.5, f32[80,64,128]{2,1,0:T(8,128)} %v_ref.5, f32[8,128]{1,0:T(8,128)} %copy-done.10, f32[8,128]{1,0:T(8,128)} %copy-done.11), custom_call_target="tpu_custom_call" | custom-call | tf_op jit(solution)/shard_map/pack_winds/pallas_call | solution.py:68
  13.8 24.0 %all_to_all.10.winds_ref = f32[16,136,128]{2,1,0:T(8,128)S(1)} all-to-all(f32[16,136,128]{2,1,0:T(8,128)} %pack_winds.1), channel_id=1, replica_groups=mesh['gx'=16,'gy'=8] {'gx'}, dimensions={0} | all-to-all | bytes 2228224 | tf_op jit(solution)/shard_map/all_to_all | solution.py:331
  37.8 13.8 %fire.1 = (f32[16,128,128]{2,1,0:T(8,128)}, f32[16,128,128]{2,1,0:T(8,128)}, f32[32,8,128]{2,1,0:T(8,128)}) custom-call(s32[16]{0:T(128)S(1)} %bitcast.10, s32[16]{0:T(128)S(1)} %bitcast.11, f32[16,136,128]{2,1,0:T(8,128)S(1)} %all_to_all.10.winds_ref, f32[16,128,128]{2,1,0:T(8,128)S(1)} %bitcast.7, f32[16,128,128]{2,1,0:T(8,128)S(1)} %bitcast.8, ...), custom_call_target="tpu_custom_call" | custom-call | flops 50000000 | bytes 6500000 | tf_op jit(solution)/shard_map/fire/pallas_call | solution.py:254
  51.6 4.5 %all-to-all-start.1 = ((f32[32,8,128]{2,1,0:T(8,128)}), f32[32,8,128]{2,1,0:T(8,128)S(1)}, u32[]{:S(2)}, u32[]{:S(2)}) async-start(f32[32,8,128]{2,1,0:T(8,128)} %get-tuple-element.14), calls=%async_computation.1 | async-start | bytes 262144 | tf_op jit(solution)/shard_map/all_to_all | solution.py:331
  56.1 4.8 %theta_edges.1 = (f32[80,128]{1,0:T(8,128)}, f32[80,128]{1,0:T(8,128)}, f32[64,128]{1,0:T(8,128)}, f32[64,128]{1,0:T(8,128)}) custom-call(f32[80,64,128]{2,1,0:T(8,128)} %theta_ref.3), custom_call_target="tpu_custom_call" | custom-call | flops 4000000 | bytes 2800000 | tf_op jit(solution)/shard_map/theta_edges/pallas_call | solution.py:105
  61.0 3.1 %collective-permute-start.2 = (f32[80,128]{1,0:T(8,128)}, f32[80,128]{1,0:T(8,128)S(1)}, u32[]{:S(2)}, u32[]{:S(2)}) collective-permute-start(f32[80,128]{1,0:T(8,128)} %get-tuple-element.15), channel_id=1, source_target_pairs={{0,8},{8,16},{16,24},{24,32},{32,40},{40,48},{48,56},{56,64},{64,7... | collective-permute-start | bytes 122888 | tf_op jit(solution)/shard_map/ppermute | solution.py:327
  64.1 4.3 %collective-permute-start.3 = (f32[80,128]{1,0:T(8,128)}, f32[80,128]{1,0:T(8,128)S(1)}, u32[]{:S(2)}, u32[]{:S(2)}) collective-permute-start(f32[80,128]{1,0:T(8,128)} %get-tuple-element.16), channel_id=1, source_target_pairs={{8,0},{16,8},{24,16},{32,24},{40,32},{48,40},{56,48},{64,56},{72,6... | collective-permute-start | bytes 122888 | tf_op jit(solution)/shard_map/ppermute | solution.py:327
  68.4 5.1 %collective-permute-start.4 = (f32[64,128]{1,0:T(8,128)}, f32[64,128]{1,0:T(8,128)S(1)}, u32[]{:S(2)}, u32[]{:S(2)}) collective-permute-start(f32[64,128]{1,0:T(8,128)} %get-tuple-element.17), channel_id=1, source_target_pairs={{0,1},{1,2},{2,3},{3,4},{4,5},{5,6},{6,7},{8,9},{9,10},{10,11},{11... | collective-permute-start | bytes 98312 | tf_op jit(solution)/shard_map/ppermute | solution.py:327
  73.5 1.9 %collective-permute-start.5 = (f32[64,128]{1,0:T(8,128)}, f32[64,128]{1,0:T(8,128)S(1)}, u32[]{:S(2)}, u32[]{:S(2)}) collective-permute-start(f32[64,128]{1,0:T(8,128)} %get-tuple-element.18), channel_id=1, source_target_pairs={{1,0},{2,1},{3,2},{4,3},{5,4},{6,5},{7,6},{9,8},{10,9},{11,10},{12... | collective-permute-start | bytes 98312 | tf_op jit(solution)/shard_map/ppermute | solution.py:327
  75.4 0.0 collective-permute-done.4.south_ref
  75.5 3.5 %collective-permute-done.5.north_ref = f32[64,128]{1,0:T(8,128)S(1)} collective-permute-done((f32[64,128]{1,0:T(8,128)}, f32[64,128]{1,0:T(8,128)S(1)}, u32[]{:S(2)}, u32[]{:S(2)}) %collective-permute-start.5) | collective-permute-done | bytes 32800 | tf_op jit(solution)/shard_map/ppermute | solution.py:327
  79.0 0.0 collective-permute-done.2.west_ref
  79.0 0.0 collective-permute-done.3.east_ref
  79.0 0.6 copy-done.9
  79.6 0.0 copy-done.6
  79.6 0.6 copy-done.7
  80.2 9.4 %advect.1.part_ref = f32[80,64,128]{2,1,0:T(8,128)} custom-call(f32[80,64,128]{2,1,0:T(8,128)} %theta_ref.3, f32[80,64,128]{2,1,0:T(8,128)} %u_ref.5, f32[80,64,128]{2,1,0:T(8,128)} %v_ref.5, f32[80,128]{1,0:T(8,128)} %copy-done.6, f32[80,128]{1,0:T(8,128)} %copy-done.7, f32[64,128]{1,0:T(8,128)} %copy-done.8, f32[64,128]{1,0:T(8,128)} %copy-done.9), custom_call_target="tpu_custom_call" | custom-call | flops 14000000 | bytes 10500000 | tf_op jit(solution)/shard_map/advect/pallas_call | solution.py:144
  89.6 0.0 all-to-all-done.1.inbox_ref
  89.6 0.6 copy-done.5
  90.2 5.1 %finish.1 = f32[80,64,128]{2,1,0:T(8,128)} custom-call(f32[32,8,128]{2,1,0:T(8,128)} %copy-done.5, f32[80,64,128]{2,1,0:T(8,128)} %advect.1.part_ref), custom_call_target="tpu_custom_call" | custom-call | flops 3000000 | bytes 5300000 | tf_op jit(solution)/shard_map/finish/pallas_call | solution.py:312
  (13 shorter events, 0.0 us)
Async XLA Ops:
  2.1 6.0 %collective-permute-start = (f32[8,128]{1,0:T(8,128)}, f32[8,128]{1,0:T(8,128)S(1)}, u32[]{:S(2)}, u32[]{:S(2)}) collective-permute-start(f32[8,128]{1,0:T(8,128)} %get-tuple-element.12), channel_id=1, source_target_pairs={{0,1},{1,2},{2,3},{3,4},{4,5},{5,6},{6,7},{8,9},{9,10},{10,11},{11... | collective-permute-start | bytes 12296 | tf_op jit(solution)/shard_map/ppermute | solution.py:327
  5.9 31.9 %copy-start = (f32[1,1,16,128,128]{4,3,2,1,0:T(8,128)S(1)}, f32[1,1,16,128,128]{4,3,2,1,0:T(8,128)}, u32[]{:S(2)}) copy-start(f32[1,1,16,128,128]{4,3,2,1,0:T(8,128)} %param.11) | copy-start | bytes 3145732
  5.9 31.9 %copy-start.1 = (f32[1,1,16,128,128]{4,3,2,1,0:T(8,128)S(1)}, f32[1,1,16,128,128]{4,3,2,1,0:T(8,128)}, u32[]{:S(2)}) copy-start(f32[1,1,16,128,128]{4,3,2,1,0:T(8,128)} %param.12) | copy-start | bytes 3145732
  5.9 31.9 %copy-start.2 = (f32[1,1,16,128,128]{4,3,2,1,0:T(8,128)S(1)}, f32[1,1,16,128,128]{4,3,2,1,0:T(8,128)}, u32[]{:S(2)}) copy-start(f32[1,1,16,128,128]{4,3,2,1,0:T(8,128)} %param.13) | copy-start | bytes 3145732
  5.9 31.9 %copy-start.3 = (s32[1,1,16]{2,1,0:T(1,128)S(1)}, s32[1,1,16]{2,1,0:T(1,128)}, u32[]{:S(2)}) copy-start(s32[1,1,16]{2,1,0:T(1,128)} %param.14) | copy-start | bytes 196
  5.9 31.9 %copy-start.4 = (s32[1,1,16]{2,1,0:T(1,128)S(1)}, s32[1,1,16]{2,1,0:T(1,128)}, u32[]{:S(2)}) copy-start(s32[1,1,16]{2,1,0:T(1,128)} %param.15) | copy-start | bytes 196
  5.9 5.4 %collective-permute-start.1 = (f32[8,128]{1,0:T(8,128)}, f32[8,128]{1,0:T(8,128)S(1)}, u32[]{:S(2)}, u32[]{:S(2)}) collective-permute-start(f32[8,128]{1,0:T(8,128)} %get-tuple-element.13), channel_id=1, source_target_pairs={{1,0},{2,1},{3,2},{4,3},{5,4},{6,5},{7,6},{9,8},{10,9},{11,10},{12... | collective-permute-start | bytes 12296 | tf_op jit(solution)/shard_map/ppermute | solution.py:327
  8.1 3.2 %copy-start.10 = (f32[8,128]{1,0:T(8,128)}, f32[8,128]{1,0:T(8,128)S(1)}, u32[]{:S(2)}) copy-start(f32[8,128]{1,0:T(8,128)S(1)} %collective-permute-done.low_ref) | copy-start | bytes 12292
  11.3 0.6 copy-start.11
  51.6 38.0 %all-to-all-start.1 = ((f32[32,8,128]{2,1,0:T(8,128)}), f32[32,8,128]{2,1,0:T(8,128)S(1)}, u32[]{:S(2)}, u32[]{:S(2)}) async-start(f32[32,8,128]{2,1,0:T(8,128)} %get-tuple-element.14), calls=%async_computation.1 | async-start | bytes 262144 | tf_op jit(solution)/shard_map/all_to_all | solution.py:331
  61.0 18.0 %collective-permute-start.2 = (f32[80,128]{1,0:T(8,128)}, f32[80,128]{1,0:T(8,128)S(1)}, u32[]{:S(2)}, u32[]{:S(2)}) collective-permute-start(f32[80,128]{1,0:T(8,128)} %get-tuple-element.15), channel_id=1, source_target_pairs={{0,8},{8,16},{16,24},{24,32},{32,40},{40,48},{48,56},{56,64},{64,7... | collective-permute-start | bytes 122888 | tf_op jit(solution)/shard_map/ppermute | solution.py:327
  64.1 14.9 %collective-permute-start.3 = (f32[80,128]{1,0:T(8,128)}, f32[80,128]{1,0:T(8,128)S(1)}, u32[]{:S(2)}, u32[]{:S(2)}) collective-permute-start(f32[80,128]{1,0:T(8,128)} %get-tuple-element.16), channel_id=1, source_target_pairs={{8,0},{16,8},{24,16},{32,24},{40,32},{48,40},{56,48},{64,56},{72,6... | collective-permute-start | bytes 122888 | tf_op jit(solution)/shard_map/ppermute | solution.py:327
  68.4 7.1 %collective-permute-start.4 = (f32[64,128]{1,0:T(8,128)}, f32[64,128]{1,0:T(8,128)S(1)}, u32[]{:S(2)}, u32[]{:S(2)}) collective-permute-start(f32[64,128]{1,0:T(8,128)} %get-tuple-element.17), channel_id=1, source_target_pairs={{0,1},{1,2},{2,3},{3,4},{4,5},{5,6},{6,7},{8,9},{9,10},{10,11},{11... | collective-permute-start | bytes 98312 | tf_op jit(solution)/shard_map/ppermute | solution.py:327
  73.5 5.4 %collective-permute-start.5 = (f32[64,128]{1,0:T(8,128)}, f32[64,128]{1,0:T(8,128)S(1)}, u32[]{:S(2)}, u32[]{:S(2)}) collective-permute-start(f32[64,128]{1,0:T(8,128)} %get-tuple-element.18), channel_id=1, source_target_pairs={{1,0},{2,1},{3,2},{4,3},{5,4},{6,5},{7,6},{9,8},{10,9},{11,10},{12... | collective-permute-start | bytes 98312 | tf_op jit(solution)/shard_map/ppermute | solution.py:327
  75.5 3.5 %copy-start.8 = (f32[64,128]{1,0:T(8,128)}, f32[64,128]{1,0:T(8,128)S(1)}, u32[]{:S(2)}) copy-start(f32[64,128]{1,0:T(8,128)S(1)} %collective-permute-done.4.south_ref) | copy-start | bytes 98308
  79.0 0.6 copy-start.9
  79.0 0.6 copy-start.6
  79.6 0.6 copy-start.7
  89.6 0.7 copy-start.5

commit v2 on v0

v2 whole, which is shorter than its diff:
```python
import functools

import jax
import jax.numpy as jnp
from jax import lax
from jax.experimental import pallas as pl
from jax.experimental.pallas import tpu as pltpu
from jax.sharding import PartitionSpec as P

LZ = 80
TA = 4
R = 32
KSUB = 6
CAP = 2
TPD = 16
S = 128
CX = 64
CY = 128
ROWS = S // 8
BLOCK = 2 * CX + 8
RIM = 8
GROUP = 8
GROUPS = LZ // GROUP

time_step = 0.03
diffusion = 0.15
burn_rate = 0.15
regular = 0.01
courant = 0.4
heat_gain = 2.0

F32 = jnp.float32
LOCAL = pl.BlockSpec(memory_space=pltpu.VMEM)
ANYWHERE = pl.BlockSpec(memory_space=pl.ANY)
SCALARS = pl.BlockSpec(memory_space=pltpu.SMEM)


def iota(dim, shape=(8, 128)):
    return lax.broadcasted_iota(jnp.int32, shape, dim)


def near(cells):
    return pltpu.with_memory_space_constraint(cells, pltpu.VMEM)


def params(mib):
    return pltpu.CompilerParams(vmem_limit_bytes=mib * 1024 * 1024)


def wind_edge_kernel(u_ref, v_ref, block_ref, up_ref, down_ref, sems):
    copies = [
        pltpu.make_async_copy(ref.at[0], block_ref.at[c * CX : (c + 1) * CX], sems.at[c])
        for c, ref in enumerate((u_ref, v_ref))
    ]
    for copy in copies:
        copy.start()
    for copy in copies:
        copy.wait()
    columns = jnp.transpose(block_ref[...])
    row = iota(0)
    last = jnp.broadcast_to(columns[CY - 1 : CY], (8, 128))
    first = jnp.broadcast_to(columns[0:1], (8, 128))
    up_ref[...] = jnp.where(row == 0, last, 0.0)
    down_ref[...] = jnp.where(row == TA + 1, first, 0.0)


def wind_edges(wind_u, wind_v):
    return pl.pallas_call(
        wind_edge_kernel,
        in_specs=[ANYWHERE, ANYWHERE],
        out_specs=[LOCAL, LOCAL, LOCAL],
        out_shape=[pltpu.VMEM((2 * CX, 128), F32), pltpu.VMEM((8, 128), F32), pltpu.VMEM((8, 128), F32)],
        scratch_shapes=[pltpu.SemaphoreType.DMA((2,))],
        name="wind_edges",
        compiler_params=params(4),
    )(wind_u, wind_v)


def pack_kernel(block_ref, low_ref, high_ref, out_ref):
    edge = low_ref[...] + high_ref[...]
    for peer in range(out_ref.shape[0]):
        out_ref[peer, : 2 * CX] = block_ref[...]
        out_ref[peer, 2 * CX :] = edge


def pack_winds(block, low, high, peers):
    return pl.pallas_call(
        pack_kernel,
        in_specs=[LOCAL, LOCAL, LOCAL],
        out_specs=LOCAL,
        out_shape=pltpu.VMEM((peers, BLOCK, 128), F32),
        name="pack_winds",
        compiler_params=params(4),
    )(near(block), near(low), near(high))


def theta_edge_kernel(
    after_ref, theta_ref, u_ref, v_ref,
    theta_out, u_out, v_out, first_x_ref, last_x_ref, first_y_ref, last_y_ref, sems,
):
    def copy(c, g):
        source, target = ((theta_ref, theta_out), (u_ref, u_out), (v_ref, v_out))[c]
        part = pl.ds(g * GROUP, GROUP)
        return pltpu.make_async_copy(source.at[part], target.at[part], sems.at[c, g])

    for g in reversed(range(GROUPS)):
        copy(0, g).start()
    for c in (1, 2):
        for g in range(GROUPS):
            copy(c, g).start()
    lane = iota(1, (CX, 128))

    def one(i, carry):
        first, last = carry
        g = GROUPS - 1 - i
        copy(0, g).wait()
        first = pltpu.roll(first, GROUP, 1)
        last = pltpu.roll(last, GROUP, 1)
        for k in range(GROUP):
            z = g * GROUP + k
            cells = theta_out[z]
            first_x_ref[pl.ds(z, 1)] = cells[0:1]
            last_x_ref[pl.ds(z, 1)] = cells[CX - 1 : CX]
            turned = pltpu.roll(cells, k + 1, 1)
            first = jnp.where(lane == k + 1, turned, first)
            last = jnp.where(lane == k, turned, last)
        return first, last

    zero = jnp.zeros((CX, 128), F32)
    first, last = lax.fori_loop(0, GROUPS, one, (zero, zero))
    first_y_ref[...] = first
    last_y_ref[...] = last
    for c in (1, 2):
        for g in range(GROUPS):
            copy(c, g).wait()


def theta_edges(after, theta, wind_u, wind_v):
    whole = pltpu.VMEM((LZ, CX, CY), F32)
    row = pltpu.VMEM((LZ, 128), F32)
    column = pltpu.VMEM((CX, 128), F32)
    return pl.pallas_call(
        theta_edge_kernel,
        in_specs=[ANYWHERE] * 4,
        out_specs=[LOCAL] * 7,
        out_shape=[whole, whole, whole, row, row, column, column],
        scratch_shapes=[pltpu.SemaphoreType.DMA((3, GROUPS))],
        name="theta_edges",
        compiler_params=params(4),
        cost_estimate=pl.CostEstimate(flops=4_000_000, bytes_accessed=8_000_000, transcendentals=0),
    )(after, theta, wind_u, wind_v)


def advect_kernel(theta_ref, u_ref, v_ref, west_ref, east_ref, south_ref, north_ref, out_ref):
    lane = iota(1, (CX, 128))
    row = iota(0, (CX, 128))

    def one(g, carry):
        south_all, north_all = carry
        for k in range(GROUP):
            z = g * GROUP + k
            t = theta_ref[z]
            u = u_ref[z]
            v = v_ref[z]
            west = jnp.where(row == 0, west_ref[pl.ds(z, 1)], pltpu.roll(t, 1, 0))
            east = jnp.where(row == CX - 1, east_ref[pl.ds(z, 1)], pltpu.roll(t, CX - 1, 0))
            south = pltpu.roll(jnp.where(lane == CY - 1, pltpu.roll(south_all, 127 - k, 1), t), 1, 1)
            north = pltpu.roll(jnp.where(lane == 0, pltpu.roll(north_all, 127 - k, 1), t), CY - 1, 1)
            change = jnp.abs(u) * (t - jnp.where(u > 0, west, east)) + jnp.abs(v) * (
                t - jnp.where(v > 0, south, north)
            )
            out_ref[z] = t - courant * change
        return pltpu.roll(south_all, 128 - GROUP, 1), pltpu.roll(north_all, 128 - GROUP, 1)

    lax.fori_loop(0, GROUPS, one, (south_ref[...], north_ref[...]))


def advect(*args):
    return pl.pallas_call(
        advect_kernel,
        in_specs=[LOCAL] * 7,
        out_specs=LOCAL,
        out_shape=pltpu.VMEM((LZ, CX, CY), F32),
        name="advect",
        compiler_params=params(4),
        cost_estimate=pl.CostEstimate(flops=14_000_000, bytes_accessed=1_000_000, transcendentals=0),
    )(*(near(a) for a in args))


def fire_kernel(
    peers, waits, owner_ref, place_ref, winds_ref, level_ref, fuel_ref, base_ref, *rest
):
    level_out, fuel_out, outbox, surface, edges, wind, level_own, fuel_own, count, sems = rest[waits:]
    lane = iota(1)
    row = iota(0)

    for c in range(2):
        for ref in (surface, edges):
            ref[c, 0:RIM] = jnp.zeros((RIM, 128), F32)
            ref[c, RIM + peers * CX :] = jnp.zeros((RIM, 128), F32)
    for d in range(peers):
        count[d] = 0
        turned = jnp.transpose(
            jnp.concatenate([winds_ref[d, 2 * CX :], jnp.zeros((120, 128), F32)], axis=0)
        )
        for c in range(2):
            surface[c, RIM + d * CX : RIM + (d + 1) * CX] = winds_ref[d, c * CX : (c + 1) * CX]
            edges[c, RIM + d * CX : RIM + (d + 1) * CX] = turned[c * CX : (c + 1) * CX]
    for d in range(peers * CAP):
        outbox[d] = jnp.where(row < TA, 0.0, -1.0)

    tiles_y = CY // TA
    low_row = (row + 1) // 2
    low_lane = (lane + R // 2) // R
    part_row = jnp.where(row % 2 == 0, 0.5, 0.0) + 0.5 / R
    part_lane = (lane.astype(F32) + 0.5) / R + 0.5 - low_lane.astype(F32)

    def results(t):
        return (
            pltpu.make_async_copy(level_own.at[t], level_out.at[t], sems.at[0, t]),
            pltpu.make_async_copy(fuel_own.at[t], fuel_out.at[t], sems.at[1, t]),
        )

    def one(tile, carry):
        owner = owner_ref[tile]
        place = place_ref[tile]
        x_own = place // tiles_y * TA
        y_own = lax.rem(place, tiles_y) * TA
        first = owner * CX + x_own + (RIM - 1)
        outside = jnp.logical_or(
            jnp.logical_and(lane == 0, y_own == 0), jnp.logical_and(lane == TA + 1, y_own == CY - TA)
        )
        back = lax.rem(CY + 1 - y_own, CY)
        for c in range(2):
            patch = pltpu.roll(surface[c, pl.ds(first, 8), :], back, 1)
            patch = jnp.where(outside, edges[c, pl.ds(first, 8), :], patch)
            left = jnp.take_along_axis(patch, low_lane, axis=1)
            right = jnp.take_along_axis(patch, low_lane + 1, axis=1)
            fine = left + (right - left) * part_lane
            below = jnp.take_along_axis(fine, low_row, axis=0)
            above = jnp.take_along_axis(fine, low_row + 1, axis=0)
            rise = above - below
            begin = below + rise * part_row
            slope = rise * (1.0 / R)
            for k in range(ROWS):
                wind[c, k] = begin + slope * float(k)

        level = [level_ref[tile, pl.ds(k, 8, stride=ROWS), :] for k in range(ROWS)]
        fuel = [fuel_ref[tile, pl.ds(k, 8, stride=ROWS), :] for k in range(ROWS)]
        heat = sum(fuel[1:], fuel[0])
        rate = [base_ref[tile, pl.ds(k, 8, stride=ROWS), :] * (0.5 * time_step) for k in range(ROWS)]
        for _ in range(KSUB):
            before = jnp.where(row == 0, level[0], pltpu.roll(level[-1], 1, 0))
            after = jnp.where(row == 7, level[-1], pltpu.roll(level[0], 7, 0))
            rimmed = [before, *level, after]
            new = []
            for k in range(ROWS):
                cell = rimmed[k + 1]
                west, east = rimmed[k], rimmed[k + 2]
                south = jnp.where(lane == 0, cell, pltpu.roll(cell, 1, 1))
                north = jnp.where(lane == S - 1, cell, pltpu.roll(cell, S - 1, 1))
                dx = east - west
                dy = north - south
                square = dx * dx + dy * dy + 4.0 * regular
                length = square * lax.rsqrt(square)
                move = jnp.maximum(length + (wind[0, k] * dx + wind[1, k] * dy), 0.0)
                around = (east + west) + (north + south)
                cell = cell * (1.0 - 4.0 * diffusion) + around * diffusion - rate[k] * move
                fuel[k] = fuel[k] * ((1.0 - 0.5 * burn_rate) + (0.5 * burn_rate) * jnp.tanh(cell))
                new.append(cell)
            level = new
        for k in range(ROWS):
            level_own[tile, pl.ds(k, 8, stride=ROWS), :] = level[k]
            fuel_own[tile, pl.ds(k, 8, stride=ROWS), :] = fuel[k]
        for copy in results(tile):
            copy.start()
        heat = (heat - sum(fuel[1:], fuel[0])) * (1.0 / (R * R))
        heat = heat + pltpu.roll(heat, 7, 0)

        message = jnp.where(row < TA, 0.0, (x_own + row - TA).astype(F32))
        rows = jnp.take_along_axis(heat, jnp.minimum(2 * row, 7), axis=0)
        for b in range(TA):
            total = jnp.sum(jnp.where(lane // R == b, rows, 0.0), axis=1, keepdims=True)
            message = jnp.where(jnp.logical_and(row < TA, lane == y_own + b), total, message)
        rank = count[owner]
        count[owner] = rank + 1
        outbox[owner * CAP + rank] = message
        return carry

    lax.fori_loop(0, TPD, one, 0)
    for t in range(TPD):
        for copy in results(t):
            copy.wait()


def fire(owners, places, winds, level_set, fuel_load, spread_base, peers, waits):
    rows = peers * CX + 2 * RIM
    tiles = (TPD, S, S)
    return pl.pallas_call(
        functools.partial(fire_kernel, peers, len(waits)),
        in_specs=[SCALARS, SCALARS] + [LOCAL] * 4 + [ANYWHERE] * len(waits),
        out_specs=[ANYWHERE, ANYWHERE, LOCAL],
        out_shape=[
            jax.ShapeDtypeStruct(tiles, F32),
            jax.ShapeDtypeStruct(tiles, F32),
            pltpu.VMEM((peers * CAP, 8, 128), F32),
        ],
        scratch_shapes=[
            pltpu.VMEM((2, rows, 128), F32),
            pltpu.VMEM((2, rows, 128), F32),
            pltpu.VMEM((2, ROWS, 8, 128), F32),
            pltpu.VMEM(tiles, F32),
            pltpu.VMEM(tiles, F32),
            pltpu.SMEM((peers,), jnp.int32),
            pltpu.SemaphoreType.DMA((2, TPD)),
        ],
        name="fire",
        compiler_params=params(12),
        cost_estimate=pl.CostEstimate(
            flops=50_000_000, bytes_accessed=6_500_000, transcendentals=3_200_000
        ),
    )(owners, places, *(near(a) for a in (winds, level_set, fuel_load, spread_base)), *waits)


def final_kernel(inbox_ref, part_ref, out_ref, field, result, sems):
    inbox = inbox_ref[...]
    slots = inbox.shape[0]
    position = pltpu.roll(inbox, TA, 1).reshape(slots * 8, 128)
    values = inbox.reshape(slots * 8, 128)
    lane = iota(1, (slots * 8, 128)).astype(F32)
    valid = iota(0, (slots * 8, 128)) % 8 < TA
    hot = jnp.where(jnp.logical_and(valid, lane == position), 1.0, 0.0)
    total = lax.dot_general(
        hot, values, (((0,), (0,)), ((), ())),
        precision=lax.Precision.HIGHEST, preferred_element_type=F32,
    )
    field[...] = total[:CX]

    def copy(g):
        part = pl.ds(g * GROUP, GROUP)
        return pltpu.make_async_copy(result.at[part], out_ref.at[part], sems.at[g])

    def one(g, carry):
        for k in range(GROUP):
            z = g * GROUP + k
            height = jnp.full((8, 128), z, jnp.int32).astype(F32)
            gain = heat_gain * jnp.exp((height + 0.5) * (-4.0 / LZ))
            result[z] = part_ref[z] + field[...] * jnp.concatenate([gain] * (CX // 8), axis=0)
        copy(g).start()
        return carry

    lax.fori_loop(0, GROUPS, one, 0)
    for g in range(GROUPS):
        copy(g).wait()


def finish(inbox, part):
    return pl.pallas_call(
        final_kernel,
        in_specs=[LOCAL, LOCAL],
        out_specs=ANYWHERE,
        out_shape=jax.ShapeDtypeStruct((LZ, CX, CY), F32),
        scratch_shapes=[
            pltpu.VMEM((CX, CY), F32),
            pltpu.VMEM((LZ, CX, CY), F32),
            pltpu.SemaphoreType.DMA((GROUPS,)),
        ],
        name="finish",
        compiler_params=params(8),
        cost_estimate=pl.CostEstimate(flops=3_000_000, bytes_accessed=2_700_000, transcendentals=0),
    )(near(inbox), near(part))


def shifted(cells, axis, up):
    ends = lax.axis_size(axis) - 1
    pairs = [(i, i + 1) if up else (i + 1, i) for i in range(ends)]
    return lax.ppermute(cells, axis, pairs)


def exchange(cells):
    return lax.all_to_all(cells, "gx", split_axis=0, concat_axis=0, tiled=True)


def body(theta, wind_u, wind_v, level_set, fuel_load, spread_base, tile_owner, tile_place):
    peers = lax.axis_size("gx")
    block, up, down = wind_edges(wind_u, wind_v)
    low = shifted(up, "gy", True)
    high = shifted(down, "gy", False)
    packed = pack_winds(block, low, high, peers)
    winds = exchange(packed)

    theta_near, u_near, v_near, first_x, last_x, first_y, last_y = theta_edges(packed, theta, wind_u, wind_v)
    west = shifted(last_x, "gx", True)
    east = shifted(first_x, "gx", False)
    south = shifted(last_y, "gy", True)
    north = shifted(first_y, "gy", False)

    level_out, fuel_out, outbox = fire(
        tile_owner[0, 0], tile_place[0, 0], winds, level_set[0, 0], fuel_load[0, 0], spread_base[0, 0], peers,
        (west, east, south, north),
    )
    part = advect(theta_near, u_near, v_near, west, east, south, north)
    inbox = exchange(outbox)
    theta_next = finish(inbox, part)
    return (theta_next, level_out[None, None], fuel_out[None, None])


def solution(mesh):
    in_specs = (
        P(None, "gx", "gy"),
        P(None, "gx", "gy"),
        P(None, "gx", "gy"),
        P("gx", "gy", None, None, None),
        P("gx", "gy", None, None, None),
        P("gx", "gy", None, None, None),
        P("gx", "gy", None),
        P("gx", "gy", None),
    )
    out_specs = (
        P(None, "gx", "gy"),
        P("gx", "gy", None, None, None),
        P("gx", "gy", None, None, None),
    )
    return jax.shard_map(body, mesh=mesh, in_specs=in_specs, out_specs=out_specs, check_vma=False)
```

time: 270 us -> 90.3 us (0.33)
  the two profiles are of different devices: /device:TPU:16 before, /device:TPU:1 now
where the time goes in v2:
time: 90.3 us; the launch traced here: 89.5 us
  starting transfers between devices  31.3 us (35%)
  Pallas kernels  28.4 us (31%)
  local copies, waits for them, and re-layouts  22.6 us (25%)
  waiting for transfers between devices  6.3 us (7%)
    unnamed x36, local copies, waits for them, and re-layouts  22.6 us
    ppermute x6, starting transfers between devices, shifted(): return lax.ppermute(cells, axis, pairs)  16 us
    all_to_all x2, starting transfers between devices, exchange(): return lax.all_to_all(cells, 'gx', split_axis=0, concat_axis=0, tiled=True)  15.3 us
    pallas_call x1, Pallas kernels, fire(): pl.pallas_call(functools.partial(fire_kernel, peers, len(waits)), in_spec...  15.1 us
    pallas_call x1, Pallas kernels, advect(): pl.pallas_call(advect_kernel, in_specs=[LOCAL] * 7, out_specs=LOCAL, out_...  8.78 us
    ppermute x6, waiting for transfers between devices, shifted(): return lax.ppermute(cells, axis, pairs)  6.29 us
    pallas_call x1, Pallas kernels, theta_edges(): pl.pallas_call(theta_edge_kernel, in_specs=[ANYWHERE] * 4, out_specs=[LOC...  2.38 us
    pallas_call x1, Pallas kernels, finish(): pl.pallas_call(final_kernel, in_specs=[LOCAL, LOCAL], out_specs=ANYWHERE,...  1.92 us
  transfers between devices with their start and end apart: 8, of which 2 were waited for; matrix products, arithmetic and copies ran while one was open for 0% of the time, Pallas kernels for 12%

profile of v2, /device:TPU:1, one launch (start us, length us, event | category | flops | bytes accessed | tf_op | source)
XLA Modules:
  0.0 89.5 jit_solution(15095404491072715121)
XLA Ops:
  0.6 1.7 %copy-done = f32[80,64,128]{2,1,0:T(8,128)S(1)} copy-done((f32[80,64,128]{2,1,0:T(8,128)S(1)}, f32[80,64,128]{2,1,0:T(8,128)}, u32[]{:S(2)}) %copy-start) | copy-done | bytes 2621464
  2.4 1.7 %copy-done.2 = f32[80,64,128]{2,1,0:T(8,128)S(1)} copy-done((f32[80,64,128]{2,1,0:T(8,128)S(1)}, f32[80,64,128]{2,1,0:T(8,128)}, u32[]{:S(2)}) %copy-start.2) | copy-done | bytes 2621464
  4.1 0.2 wind_edges.1
  4.3 0.0 copy-start.1
  4.3 4.9 %collective-permute-start = (f32[8,128]{1,0:T(8,128)S(1)}, f32[8,128]{1,0:T(8,128)S(1)}, u32[]{:S(2)}, u32[]{:S(2)}) collective-permute-start(f32[8,128]{1,0:T(8,128)S(1)} %get-tuple-element.17), channel_id=1, source_target_pairs={{0,1},{1,2},{2,3},{3,4},{4,5},{5,6},{6,7},{8,9},{9,10},{10,11},{11... | collective-permute-start | bytes 12296 | tf_op jit(solution)/shard_map/ppermute | solution.py:377
  9.2 1.9 %collective-permute-start.1 = (f32[8,128]{1,0:T(8,128)S(1)}, f32[8,128]{1,0:T(8,128)S(1)}, u32[]{:S(2)}, u32[]{:S(2)}) collective-permute-start(f32[8,128]{1,0:T(8,128)S(1)} %get-tuple-element.18), channel_id=1, source_target_pairs={{1,0},{2,1},{3,2},{4,3},{5,4},{6,5},{7,6},{9,8},{10,9},{11,10},{12... | collective-permute-start | bytes 12296 | tf_op jit(solution)/shard_map/ppermute | solution.py:377
  11.1 3.0 %collective-permute-done.1.high_ref = f32[8,128]{1,0:T(8,128)S(1)} collective-permute-done((f32[8,128]{1,0:T(8,128)S(1)}, f32[8,128]{1,0:T(8,128)S(1)}, u32[]{:S(2)}, u32[]{:S(2)}) %collective-permute-start.1) | collective-permute-done | bytes 4128 | tf_op jit(solution)/shard_map/ppermute | solution.py:377
  14.1 0.1 pack_winds.1.after_ref
  14.2 1.0 %copy-done.4 = f32[16,136,128]{2,1,0:T(8,128)} copy-done((f32[16,136,128]{2,1,0:T(8,128)}, f32[16,136,128]{2,1,0:T(8,128)S(1)}, u32[]{:S(2)}) %copy-start.4) | copy-done | bytes 1114136
  15.2 7.6 %all-to-all-start = ((f32[16,136,128]{2,1,0:T(8,128)}), f32[16,136,128]{2,1,0:T(8,128)}, u32[]{:S(2)}, u32[]{:S(2)}) async-start(f32[16,136,128]{2,1,0:T(8,128)} %copy-done.4), calls=%async_computation | async-start | bytes 2228224 | tf_op jit(solution)/shard_map/all_to_all | solution.py:381
  22.8 1.7 %copy-done.3 = f32[80,64,128]{2,1,0:T(8,128)S(1)} copy-done((f32[80,64,128]{2,1,0:T(8,128)S(1)}, f32[80,64,128]{2,1,0:T(8,128)}, u32[]{:S(2)}) %copy-start.3) | copy-done | bytes 2621464
  24.6 1.2 %copy-done.5 = f32[16,136,128]{2,1,0:T(8,128)S(1)} copy-done((f32[16,136,128]{2,1,0:T(8,128)S(1)}, f32[16,136,128]{2,1,0:T(8,128)}, u32[]{:S(2)}) %copy-start.5) | copy-done | bytes 1114136
  25.8 1.7 %copy-done.6 = f32[80,64,128]{2,1,0:T(8,128)S(1)} copy-done((f32[80,64,128]{2,1,0:T(8,128)S(1)}, f32[80,64,128]{2,1,0:T(8,128)}, u32[]{:S(2)}) %copy-start.6) | copy-done | bytes 2621464
  27.6 2.4 %theta_edges.1 = (f32[80,64,128]{2,1,0:T(8,128)S(1)}, f32[80,64,128]{2,1,0:T(8,128)S(1)}, f32[80,64,128]{2,1,0:T(8,128)S(1)}, f32[80,128]{1,0:T(8,128)S(1)}, f32...) custom-call(f32[16,136,128]{2,1,0:T(8,128)S(1)} %copy-done.5, f32[80,64,128]{2,1,0:T(8,128)S(1)} %copy-done.6, ...), custom_call_target="tpu_custom_call" | custom-call | flops 4000000 | bytes 8000000 | tf_op jit(solution)/shard_map/theta_edges/pallas_call | solution.py:142
  30.0 1.5 %copy-done.7 = f32[80,64,128]{2,1,0:T(8,128)} copy-done((f32[80,64,128]{2,1,0:T(8,128)}, f32[80,64,128]{2,1,0:T(8,128)S(1)}, u32[]{:S(2)}) %copy-start.7) | copy-done | bytes 2621464
  31.4 1.5 %copy-done.9 = f32[80,64,128]{2,1,0:T(8,128)} copy-done((f32[80,64,128]{2,1,0:T(8,128)}, f32[80,64,128]{2,1,0:T(8,128)S(1)}, u32[]{:S(2)}) %copy-start.9) | copy-done | bytes 2621464
  33.0 1.5 %copy-done.11 = f32[80,64,128]{2,1,0:T(8,128)} copy-done((f32[80,64,128]{2,1,0:T(8,128)}, f32[80,64,128]{2,1,0:T(8,128)S(1)}, u32[]{:S(2)}) %copy-start.11) | copy-done | bytes 2621464
  34.5 3.2 %collective-permute-start.2 = (f32[80,128]{1,0:T(8,128)S(1)}, f32[80,128]{1,0:T(8,128)S(1)}, u32[]{:S(2)}, u32[]{:S(2)}) collective-permute-start(f32[80,128]{1,0:T(8,128)S(1)} %get-tuple-element.19), channel_id=1, source_target_pairs={{0,8},{8,16},{16,24},{24,32},{32,40},{40,48},{48,56},{56,64},{64,7... | collective-permute-start | bytes 122888 | tf_op jit(solution)/shard_map/ppermute | solution.py:377
  37.7 1.3 %collective-permute-start.3 = (f32[80,128]{1,0:T(8,128)S(1)}, f32[80,128]{1,0:T(8,128)S(1)}, u32[]{:S(2)}, u32[]{:S(2)}) collective-permute-start(f32[80,128]{1,0:T(8,128)S(1)} %get-tuple-element.20), channel_id=1, source_target_pairs={{8,0},{16,8},{24,16},{32,24},{40,32},{48,40},{56,48},{64,56},{72,6... | collective-permute-start | bytes 122888 | tf_op jit(solution)/shard_map/ppermute | solution.py:377
  39.0 2.8 %collective-permute-start.4 = (f32[64,128]{1,0:T(8,128)S(1)}, f32[64,128]{1,0:T(8,128)S(1)}, u32[]{:S(2)}, u32[]{:S(2)}) collective-permute-start(f32[64,128]{1,0:T(8,128)S(1)} %get-tuple-element.21), channel_id=1, source_target_pairs={{0,1},{1,2},{2,3},{3,4},{4,5},{5,6},{6,7},{8,9},{9,10},{10,11},{11... | collective-permute-start | bytes 98312 | tf_op jit(solution)/shard_map/ppermute | solution.py:377
  41.8 1.9 %collective-permute-start.5 = (f32[64,128]{1,0:T(8,128)S(1)}, f32[64,128]{1,0:T(8,128)S(1)}, u32[]{:S(2)}, u32[]{:S(2)}) collective-permute-start(f32[64,128]{1,0:T(8,128)S(1)} %get-tuple-element.22), channel_id=1, source_target_pairs={{1,0},{2,1},{3,2},{4,3},{5,4},{6,5},{7,6},{9,8},{10,9},{11,10},{12... | collective-permute-start | bytes 98312 | tf_op jit(solution)/shard_map/ppermute | solution.py:377
  43.7 3.3 %collective-permute-done.5.rest_3_.north_ref = f32[64,128]{1,0:T(8,128)S(1)} collective-permute-done((f32[64,128]{1,0:T(8,128)S(1)}, f32[64,128]{1,0:T(8,128)S(1)}, u32[]{:S(2)}, u32[]{:S(2)}) %collective-permute-start.5) | collective-permute-done | bytes 32800 | tf_op jit(solution)/shard_map/ppermute | solution.py:377
  47.1 1.2 %copy-done.13 = f32[1,1,16,128,128]{4,3,2,1,0:T(8,128)S(1)} copy-done((f32[1,1,16,128,128]{4,3,2,1,0:T(8,128)S(1)}, f32[1,1,16,128,128]{4,3,2,1,0:T(8,128)}, u32[]{:S(2)}) %copy-start.13) | copy-done | bytes 1048600
  48.3 1.2 %copy-done.14 = f32[1,1,16,128,128]{4,3,2,1,0:T(8,128)S(1)} copy-done((f32[1,1,16,128,128]{4,3,2,1,0:T(8,128)S(1)}, f32[1,1,16,128,128]{4,3,2,1,0:T(8,128)}, u32[]{:S(2)}) %copy-start.14) | copy-done | bytes 1048600
  49.5 1.2 %copy-done.15 = f32[1,1,16,128,128]{4,3,2,1,0:T(8,128)S(1)} copy-done((f32[1,1,16,128,128]{4,3,2,1,0:T(8,128)S(1)}, f32[1,1,16,128,128]{4,3,2,1,0:T(8,128)}, u32[]{:S(2)}) %copy-start.15) | copy-done | bytes 1048600
  50.8 15.1 %fire.1 = (f32[16,128,128]{2,1,0:T(8,128)}, f32[16,128,128]{2,1,0:T(8,128)}, f32[32,8,128]{2,1,0:T(8,128)}) custom-call(s32[16]{0:T(128)S(1)} %bitcast.10, s32[16]{0:T(128)S(1)} %bitcast.11, f32[16,136,128]{2,1,0:T(8,128)} %all-to-all-done.winds_ref, f32[16,128,128]{2,1,0:T(8,128)S(1)} %bitcast.7, f32[16,128,128]{2,1,0:T(8,128)S(1)} %bitcast.8, ...), custom_call_target="tpu_custom_call" | custom-call | flops 50000000 | bytes 6500000 | tf_op jit(solution)/shard_map/fire/pallas_call | solution.py:299
  65.8 7.7 %all-to-all-start.1 = ((f32[32,8,128]{2,1,0:T(8,128)}), f32[32,8,128]{2,1,0:T(8,128)S(1)}, u32[]{:S(2)}, u32[]{:S(2)}) async-start(f32[32,8,128]{2,1,0:T(8,128)} %get-tuple-element.23), calls=%async_computation.1 | async-start | bytes 262144 | tf_op jit(solution)/shard_map/all_to_all | solution.py:381
  73.5 1.7 %copy-done.8 = f32[80,64,128]{2,1,0:T(8,128)S(1)} copy-done((f32[80,64,128]{2,1,0:T(8,128)S(1)}, f32[80,64,128]{2,1,0:T(8,128)}, u32[]{:S(2)}) %copy-start.8) | copy-done | bytes 2621464
  75.3 1.7 %copy-done.10 = f32[80,64,128]{2,1,0:T(8,128)S(1)} copy-done((f32[80,64,128]{2,1,0:T(8,128)S(1)}, f32[80,64,128]{2,1,0:T(8,128)}, u32[]{:S(2)}) %copy-start.10) | copy-done | bytes 2621464
  77.0 1.7 %copy-done.12 = f32[80,64,128]{2,1,0:T(8,128)S(1)} copy-done((f32[80,64,128]{2,1,0:T(8,128)S(1)}, f32[80,64,128]{2,1,0:T(8,128)}, u32[]{:S(2)}) %copy-start.12) | copy-done | bytes 2621464
  78.7 8.8 %advect.1.part_ref = f32[80,64,128]{2,1,0:T(8,128)S(1)} custom-call(f32[80,64,128]{2,1,0:T(8,128)S(1)} %copy-done.8, f32[80,64,128]{2,1,0:T(8,128)S(1)} %copy-done.10, f32[80,64,128]{2,1,0:T(8,128)S(1)} %copy-done.12, f32[80,128]{1,0:T(8,128)S(1)} %collective-permute-done.2.rest_0_.west_ref, f32[80,128]{1,0:T(8,128)S(1)} %collective-permute-done.3.rest_1_.east_ref, ...), custom_call_target="tpu_custom_call" | custom-call | flops 14000000 | bytes 1000000 | tf_op jit(solution)/shard_map/advect/pallas_call | solution.py:179
  87.5 1.9 %finish.1 = f32[80,64,128]{2,1,0:T(8,128)} custom-call(f32[32,8,128]{2,1,0:T(8,128)S(1)} %all-to-all-done.1.inbox_ref, f32[80,64,128]{2,1,0:T(8,128)S(1)} %advect.1.part_ref), custom_call_target="tpu_custom_call" | custom-call | flops 3000000 | bytes 2700000 | tf_op jit(solution)/shard_map/finish/pallas_call | solution.py:358
  (26 shorter events, 0.1 us)
Async XLA Ops:
  0.6 1.7 %copy-start = (f32[80,64,128]{2,1,0:T(8,128)S(1)}, f32[80,64,128]{2,1,0:T(8,128)}, u32[]{:S(2)}) copy-start(f32[80,64,128]{2,1,0:T(8,128)} %u_ref.3) | copy-start | bytes 7864324
  2.4 1.7 %copy-start.2 = (f32[80,64,128]{2,1,0:T(8,128)S(1)}, f32[80,64,128]{2,1,0:T(8,128)}, u32[]{:S(2)}) copy-start(f32[80,64,128]{2,1,0:T(8,128)} %v_ref.3) | copy-start | bytes 7864324
  4.3 18.5 %copy-start.1 = (f32[80,64,128]{2,1,0:T(8,128)S(1)}, f32[80,64,128]{2,1,0:T(8,128)}, u32[]{:S(2)}) copy-start(f32[80,64,128]{2,1,0:T(8,128)} %u_ref.3) | copy-start | bytes 7864324
  4.3 6.8 %collective-permute-start = (f32[8,128]{1,0:T(8,128)S(1)}, f32[8,128]{1,0:T(8,128)S(1)}, u32[]{:S(2)}, u32[]{:S(2)}) collective-permute-start(f32[8,128]{1,0:T(8,128)S(1)} %get-tuple-element.17), channel_id=1, source_target_pairs={{0,1},{1,2},{2,3},{3,4},{4,5},{5,6},{6,7},{8,9},{9,10},{10,11},{11... | collective-permute-start | bytes 12296 | tf_op jit(solution)/shard_map/ppermute | solution.py:377
  9.2 4.9 %collective-permute-start.1 = (f32[8,128]{1,0:T(8,128)S(1)}, f32[8,128]{1,0:T(8,128)S(1)}, u32[]{:S(2)}, u32[]{:S(2)}) collective-permute-start(f32[8,128]{1,0:T(8,128)S(1)} %get-tuple-element.18), channel_id=1, source_target_pairs={{1,0},{2,1},{3,2},{4,3},{5,4},{6,5},{7,6},{9,8},{10,9},{11,10},{12... | collective-permute-start | bytes 12296 | tf_op jit(solution)/shard_map/ppermute | solution.py:377
  14.2 1.0 %copy-start.4 = (f32[16,136,128]{2,1,0:T(8,128)}, f32[16,136,128]{2,1,0:T(8,128)S(1)}, u32[]{:S(2)}) copy-start(f32[16,136,128]{2,1,0:T(8,128)S(1)} %pack_winds.1.after_ref) | copy-start | bytes 3342340
  15.2 31.9 %all-to-all-start = ((f32[16,136,128]{2,1,0:T(8,128)}), f32[16,136,128]{2,1,0:T(8,128)}, u32[]{:S(2)}, u32[]{:S(2)}) async-start(f32[16,136,128]{2,1,0:T(8,128)} %copy-done.4), calls=%async_computation | async-start | bytes 2228224 | tf_op jit(solution)/shard_map/all_to_all | solution.py:381
  22.8 1.7 %copy-start.3 = (f32[80,64,128]{2,1,0:T(8,128)S(1)}, f32[80,64,128]{2,1,0:T(8,128)}, u32[]{:S(2)}) copy-start(f32[80,64,128]{2,1,0:T(8,128)} %v_ref.3) | copy-start | bytes 7864324
  24.6 1.2 %copy-start.5 = (f32[16,136,128]{2,1,0:T(8,128)S(1)}, f32[16,136,128]{2,1,0:T(8,128)}, u32[]{:S(2)}) copy-start(f32[16,136,128]{2,1,0:T(8,128)} %copy-done.4) | copy-start | bytes 3342340
  25.8 1.7 %copy-start.6 = (f32[80,64,128]{2,1,0:T(8,128)S(1)}, f32[80,64,128]{2,1,0:T(8,128)}, u32[]{:S(2)}) copy-start(f32[80,64,128]{2,1,0:T(8,128)} %theta_ref.1) | copy-start | bytes 7864324
  27.6 19.5 %copy-start.16 = (s32[1,1,16]{2,1,0:T(1,128)S(1)}, s32[1,1,16]{2,1,0:T(1,128)}, u32[]{:S(2)}) copy-start(s32[1,1,16]{2,1,0:T(1,128)} %param.14) | copy-start | bytes 196
  27.6 19.5 %copy-start.17 = (s32[1,1,16]{2,1,0:T(1,128)S(1)}, s32[1,1,16]{2,1,0:T(1,128)}, u32[]{:S(2)}) copy-start(s32[1,1,16]{2,1,0:T(1,128)} %param.15) | copy-start | bytes 196
  29.9 1.5 %copy-start.7 = (f32[80,64,128]{2,1,0:T(8,128)}, f32[80,64,128]{2,1,0:T(8,128)S(1)}, u32[]{:S(2)}) copy-start(f32[80,64,128]{2,1,0:T(8,128)S(1)} %get-tuple-element.24.theta_ref) | copy-start | bytes 7864324
  31.4 1.5 %copy-start.9 = (f32[80,64,128]{2,1,0:T(8,128)}, f32[80,64,128]{2,1,0:T(8,128)S(1)}, u32[]{:S(2)}) copy-start(f32[80,64,128]{2,1,0:T(8,128)S(1)} %get-tuple-element.25.u_ref) | copy-start | bytes 7864324
  33.0 1.5 %copy-start.11 = (f32[80,64,128]{2,1,0:T(8,128)}, f32[80,64,128]{2,1,0:T(8,128)S(1)}, u32[]{:S(2)}) copy-start(f32[80,64,128]{2,1,0:T(8,128)S(1)} %get-tuple-element.26.v_ref) | copy-start | bytes 7864324
  34.5 12.6 %collective-permute-start.2 = (f32[80,128]{1,0:T(8,128)S(1)}, f32[80,128]{1,0:T(8,128)S(1)}, u32[]{:S(2)}, u32[]{:S(2)}) collective-permute-start(f32[80,128]{1,0:T(8,128)S(1)} %get-tuple-element.19), channel_id=1, source_target_pairs={{0,8},{8,16},{16,24},{24,32},{32,40},{40,48},{48,56},{56,64},{64,7... | collective-permute-start | bytes 122888 | tf_op jit(solution)/shard_map/ppermute | solution.py:377
  37.7 9.3 %collective-permute-start.3 = (f32[80,128]{1,0:T(8,128)S(1)}, f32[80,128]{1,0:T(8,128)S(1)}, u32[]{:S(2)}, u32[]{:S(2)}) collective-permute-start(f32[80,128]{1,0:T(8,128)S(1)} %get-tuple-element.20), channel_id=1, source_target_pairs={{8,0},{16,8},{24,16},{32,24},{40,32},{48,40},{56,48},{64,56},{72,6... | collective-permute-start | bytes 122888 | tf_op jit(solution)/shard_map/ppermute | solution.py:377
  39.0 4.7 %collective-permute-start.4 = (f32[64,128]{1,0:T(8,128)S(1)}, f32[64,128]{1,0:T(8,128)S(1)}, u32[]{:S(2)}, u32[]{:S(2)}) collective-permute-start(f32[64,128]{1,0:T(8,128)S(1)} %get-tuple-element.21), channel_id=1, source_target_pairs={{0,1},{1,2},{2,3},{3,4},{4,5},{5,6},{6,7},{8,9},{9,10},{10,11},{11... | collective-permute-start | bytes 98312 | tf_op jit(solution)/shard_map/ppermute | solution.py:377
  41.8 5.2 %collective-permute-start.5 = (f32[64,128]{1,0:T(8,128)S(1)}, f32[64,128]{1,0:T(8,128)S(1)}, u32[]{:S(2)}, u32[]{:S(2)}) collective-permute-start(f32[64,128]{1,0:T(8,128)S(1)} %get-tuple-element.22), channel_id=1, source_target_pairs={{1,0},{2,1},{3,2},{4,3},{5,4},{6,5},{7,6},{9,8},{10,9},{11,10},{12... | collective-permute-start | bytes 98312 | tf_op jit(solution)/shard_map/ppermute | solution.py:377
  47.1 1.2 %copy-start.13 = (f32[1,1,16,128,128]{4,3,2,1,0:T(8,128)S(1)}, f32[1,1,16,128,128]{4,3,2,1,0:T(8,128)}, u32[]{:S(2)}) copy-start(f32[1,1,16,128,128]{4,3,2,1,0:T(8,128)} %param.11) | copy-start | bytes 3145732
  48.3 1.2 %copy-start.14 = (f32[1,1,16,128,128]{4,3,2,1,0:T(8,128)S(1)}, f32[1,1,16,128,128]{4,3,2,1,0:T(8,128)}, u32[]{:S(2)}) copy-start(f32[1,1,16,128,128]{4,3,2,1,0:T(8,128)} %param.12) | copy-start | bytes 3145732
  49.5 1.2 %copy-start.15 = (f32[1,1,16,128,128]{4,3,2,1,0:T(8,128)S(1)}, f32[1,1,16,128,128]{4,3,2,1,0:T(8,128)}, u32[]{:S(2)}) copy-start(f32[1,1,16,128,128]{4,3,2,1,0:T(8,128)} %param.13) | copy-start | bytes 3145732
  65.8 21.7 %all-to-all-start.1 = ((f32[32,8,128]{2,1,0:T(8,128)}), f32[32,8,128]{2,1,0:T(8,128)S(1)}, u32[]{:S(2)}, u32[]{:S(2)}) async-start(f32[32,8,128]{2,1,0:T(8,128)} %get-tuple-element.23), calls=%async_computation.1 | async-start | bytes 262144 | tf_op jit(solution)/shard_map/all_to_all | solution.py:381
  73.5 1.7 %copy-start.8 = (f32[80,64,128]{2,1,0:T(8,128)S(1)}, f32[80,64,128]{2,1,0:T(8,128)}, u32[]{:S(2)}) copy-start(f32[80,64,128]{2,1,0:T(8,128)} %copy-done.7) | copy-start | bytes 7864324
  75.3 1.7 %copy-start.10 = (f32[80,64,128]{2,1,0:T(8,128)S(1)}, f32[80,64,128]{2,1,0:T(8,128)}, u32[]{:S(2)}) copy-start(f32[80,64,128]{2,1,0:T(8,128)} %copy-done.9) | copy-start | bytes 7864324
  77.0 1.7 %copy-start.12 = (f32[80,64,128]{2,1,0:T(8,128)S(1)}, f32[80,64,128]{2,1,0:T(8,128)}, u32[]{:S(2)}) copy-start(f32[80,64,128]{2,1,0:T(8,128)} %copy-done.11) | copy-start | bytes 7864324

commit v3 on v2

v3 whole, which is shorter than its diff:
```python
import functools

import jax
import jax.numpy as jnp
from jax import lax
from jax.experimental import pallas as pl
from jax.experimental.pallas import tpu as pltpu
from jax.sharding import PartitionSpec as P

LZ = 80
TA = 4
R = 32
KSUB = 6
CAP = 2
TPD = 16
S = 128
CX = 64
CY = 128
ROWS = S // 8
BLOCK = 2 * CX + 8
RIM = 8
GROUP = 8
GROUPS = LZ // GROUP
SIDE = 2
AHEAD = 2

time_step = 0.03
diffusion = 0.15
burn_rate = 0.15
regular = 0.01
courant = 0.4
heat_gain = 2.0

F32 = jnp.float32
LOCAL = pl.BlockSpec(memory_space=pltpu.VMEM)
FAR = pl.BlockSpec(memory_space=pltpu.HBM)
ANYWHERE = pl.BlockSpec(memory_space=pl.ANY)
SCALARS = pl.BlockSpec(memory_space=pltpu.SMEM)


def iota(dim, shape=(8, 128)):
    return lax.broadcasted_iota(jnp.int32, shape, dim)


def near(cells):
    return pltpu.with_memory_space_constraint(cells, pltpu.VMEM)


def far(cells):
    return pltpu.with_memory_space_constraint(cells, pltpu.HBM)


def params(mib):
    return pltpu.CompilerParams(vmem_limit_bytes=mib * 1024 * 1024)


def wind_edge_kernel(u_ref, v_ref, block_ref, up_ref, down_ref, sems):
    copies = [
        pltpu.make_async_copy(ref.at[0], block_ref.at[c * CX : (c + 1) * CX], sems.at[c])
        for c, ref in enumerate((u_ref, v_ref))
    ]
    for copy in copies:
        copy.start()
    for copy in copies:
        copy.wait()
    columns = jnp.transpose(block_ref[...])
    row = iota(0)
    last = jnp.broadcast_to(columns[CY - 1 : CY], (8, 128))
    first = jnp.broadcast_to(columns[0:1], (8, 128))
    up_ref[...] = jnp.where(row == 0, last, 0.0)
    down_ref[...] = jnp.where(row == TA + 1, first, 0.0)


def wind_edges(wind_u, wind_v):
    return pl.pallas_call(
        wind_edge_kernel,
        in_specs=[FAR, FAR],
        out_specs=[LOCAL, LOCAL, LOCAL],
        out_shape=[pltpu.VMEM((2 * CX, 128), F32), pltpu.VMEM((8, 128), F32), pltpu.VMEM((8, 128), F32)],
        scratch_shapes=[pltpu.SemaphoreType.DMA((2,))],
        name="wind_edges",
        compiler_params=params(4),
    )(far(wind_u), far(wind_v))


def pack_kernel(block_ref, low_ref, high_ref, out_ref):
    edge = low_ref[...] + high_ref[...]
    for peer in range(out_ref.shape[0]):
        out_ref[peer, : 2 * CX] = block_ref[...]
        out_ref[peer, 2 * CX :] = edge


def pack_winds(block, low, high, peers):
    return pl.pallas_call(
        pack_kernel,
        in_specs=[LOCAL, LOCAL, LOCAL],
        out_specs=LOCAL,
        out_shape=pltpu.VMEM((peers, BLOCK, 128), F32),
        name="pack_winds",
        compiler_params=params(4),
    )(near(block), near(low), near(high))


def theta_edge_kernel(after_ref, theta_ref, first_x_ref, last_x_ref, first_y_ref, last_y_ref, theta, sems):
    def copy(g):
        part = pl.ds(g * GROUP, GROUP)
        return pltpu.make_async_copy(theta_ref.at[part], theta.at[part], sems.at[g])

    for g in reversed(range(GROUPS)):
        copy(g).start()
    lane = iota(1, (CX, 128))

    def one(i, carry):
        first, last = carry
        g = GROUPS - 1 - i
        copy(g).wait()
        first = pltpu.roll(first, GROUP, 1)
        last = pltpu.roll(last, GROUP, 1)
        for k in range(GROUP):
            z = g * GROUP + k
            cells = theta[z]
            first_x_ref[pl.ds(z, 1)] = cells[0:1]
            last_x_ref[pl.ds(z, 1)] = cells[CX - 1 : CX]
            turned = pltpu.roll(cells, k + 1, 1)
            first = jnp.where(lane == k + 1, turned, first)
            last = jnp.where(lane == k, turned, last)
        return first, last

    zero = jnp.zeros((CX, 128), F32)
    first, last = lax.fori_loop(0, GROUPS, one, (zero, zero))
    first_y_ref[...] = first
    last_y_ref[...] = last


def theta_edges(after, theta):
    row = pltpu.VMEM((LZ, 128), F32)
    column = pltpu.VMEM((CX, 128), F32)
    return pl.pallas_call(
        theta_edge_kernel,
        in_specs=[ANYWHERE, FAR],
        out_specs=[LOCAL] * 4,
        out_shape=[row, row, column, column],
        scratch_shapes=[pltpu.VMEM((LZ, CX, CY), F32), pltpu.SemaphoreType.DMA((GROUPS,))],
        name="theta_edges",
        compiler_params=params(8),
        cost_estimate=pl.CostEstimate(flops=4_000_000, bytes_accessed=2_700_000, transcendentals=0),
    )(after, far(theta))


def advect_kernel(
    theta_ref, u_ref, v_ref, west_ref, east_ref, south_ref, north_ref, out_ref, theta, wind_u, wind_v, sems
):
    def copies(g):
        part = pl.ds(g * GROUP, GROUP)
        pairs = ((theta_ref, theta), (u_ref, wind_u), (v_ref, wind_v))
        return [
            pltpu.make_async_copy(source.at[part], target.at[part], sems.at[c, g])
            for c, (source, target) in enumerate(pairs)
        ]

    for g in range(GROUPS):
        for copy in copies(g):
            copy.start()
    lane = iota(1, (CX, 128))
    row = iota(0, (CX, 128))

    def one(g, carry):
        south_all, north_all = carry
        for copy in copies(g):
            copy.wait()
        def begin(k):
            t = theta[g * GROUP + k]
            rolled = [pltpu.roll(t, 1, 1), pltpu.roll(t, CY - 1, 1)]
            rims = [pltpu.roll(south_all, (128 - k) % 128, 1), pltpu.roll(north_all, 126 - k, 1)]
            return t, rolled, rims

        def end(k, begun):
            z = g * GROUP + k
            t, rolled, rims = begun
            u = wind_u[z]
            v = wind_v[z]
            west = jnp.where(row == 0, west_ref[pl.ds(z, 1)], pltpu.roll(t, 1, 0))
            east = jnp.where(row == CX - 1, east_ref[pl.ds(z, 1)], pltpu.roll(t, CX - 1, 0))
            south = jnp.where(lane == 0, rims[0], rolled[0])
            north = jnp.where(lane == CY - 1, rims[1], rolled[1])
            change = jnp.abs(u) * (t - jnp.where(u > 0, west, east)) + jnp.abs(v) * (
                t - jnp.where(v > 0, south, north)
            )
            out_ref[z] = t - courant * change

        begun = [begin(k) for k in range(AHEAD)]
        for k in range(GROUP):
            if k + AHEAD < GROUP:
                begun.append(begin(k + AHEAD))
            end(k, begun[k])
        return pltpu.roll(south_all, 128 - GROUP, 1), pltpu.roll(north_all, 128 - GROUP, 1)

    lax.fori_loop(0, GROUPS, one, (south_ref[...], north_ref[...]))


def advect(theta, wind_u, wind_v, *rims):
    whole = pltpu.VMEM((LZ, CX, CY), F32)
    return pl.pallas_call(
        advect_kernel,
        in_specs=[FAR] * 3 + [LOCAL] * 4,
        out_specs=LOCAL,
        out_shape=whole,
        scratch_shapes=[whole, whole, whole, pltpu.SemaphoreType.DMA((3, GROUPS))],
        name="advect",
        compiler_params=params(12),
        cost_estimate=pl.CostEstimate(flops=14_000_000, bytes_accessed=8_000_000, transcendentals=0),
    )(far(theta), far(wind_u), far(wind_v), *(near(a) for a in rims))


def fire_kernel(
    peers, waits, owner_ref, place_ref, winds_ref, level_ref, fuel_ref, base_ref, *rest
):
    (
        level_out, fuel_out, outbox, surface, edges, begins, slopes, heats,
        level_own, fuel_own, base_own, count, in_sems, out_sems,
    ) = rest[waits:]
    lane = iota(1)
    row = iota(0)

    def inputs(t):
        pairs = ((level_ref, level_own), (fuel_ref, fuel_own), (base_ref, base_own))
        return [
            pltpu.make_async_copy(source.at[t], target.at[t], in_sems.at[c, t])
            for c, (source, target) in enumerate(pairs)
        ]

    def results(t):
        pairs = ((level_own, level_out), (fuel_own, fuel_out))
        return [
            pltpu.make_async_copy(source.at[t], target.at[t], out_sems.at[c, t])
            for c, (source, target) in enumerate(pairs)
        ]

    for t in range(TPD):
        for copy in inputs(t):
            copy.start()

    for c in range(2):
        for ref in (surface, edges):
            ref[c, 0:RIM] = jnp.zeros((RIM, 128), F32)
            ref[c, RIM + peers * CX :] = jnp.zeros((RIM, 128), F32)
    turned = jnp.transpose(jnp.concatenate([winds_ref[d, 2 * CX :] for d in range(peers)], axis=0))
    for d in range(peers):
        count[d] = 0
        own = pltpu.roll(turned, (128 - 8 * d) % 128, 1)
        for c in range(2):
            surface[c, RIM + d * CX : RIM + (d + 1) * CX] = winds_ref[d, c * CX : (c + 1) * CX]
            edges[c, RIM + d * CX : RIM + (d + 1) * CX] = own[c * CX : (c + 1) * CX]

    tiles_y = CY // TA
    low_row = (row + 1) // 2
    low_lane = (lane + R // 2) // R
    part_row = jnp.where(row % 2 == 0, 0.5, 0.0) + 0.5 / R
    part_lane = (lane.astype(F32) + 0.5) / R + 0.5 - low_lane.astype(F32)

    x_own, y_own, patches = [], [], []
    for t in range(TPD):
        place = place_ref[t]
        x_own.append(place // tiles_y * TA)
        y_own.append(lax.rem(place, tiles_y) * TA)
        first = owner_ref[t] * CX + x_own[t] + (RIM - 1)
        back = lax.rem(CY + 1 - y_own[t], CY)
        outside = jnp.logical_or(
            jnp.logical_and(lane == 0, y_own[t] == 0),
            jnp.logical_and(lane == TA + 1, y_own[t] == CY - TA),
        )
        for c in range(2):
            patch = pltpu.roll(surface[c, pl.ds(first, 8), :], back, 1)
            patches.append(jnp.where(outside, edges[c, pl.ds(first, 8), :], patch))
    left = [jnp.take_along_axis(p, low_lane, axis=1) for p in patches]
    right = [jnp.take_along_axis(p, low_lane + 1, axis=1) for p in patches]
    fine = [p + (q - p) * part_lane for p, q in zip(left, right)]
    below = [jnp.take_along_axis(p, low_row, axis=0) for p in fine]
    above = [jnp.take_along_axis(p, low_row + 1, axis=0) for p in fine]
    for i, (p, q) in enumerate(zip(below, above)):
        begins[i] = p + (q - p) * part_row
        slopes[i] = (q - p) * (1.0 / R)

    def burn(t):
        begin = [begins[2 * t + c] for c in range(2)]
        slope = [slopes[2 * t + c] for c in range(2)]
        level = [level_own[t, pl.ds(k, 8, stride=ROWS), :] for k in range(ROWS)]
        fuel = [fuel_own[t, pl.ds(k, 8, stride=ROWS), :] for k in range(ROWS)]
        heat = sum(fuel[1:], fuel[0])
        rate = [base_own[t, pl.ds(k, 8, stride=ROWS), :] * (0.5 * time_step) for k in range(ROWS)]
        wind = [[begin[c] + slope[c] * float(k) for k in range(ROWS)] for c in range(2)]
        yield
        for _ in range(KSUB):
            before = jnp.where(row == 0, level[0], pltpu.roll(level[-1], 1, 0))
            after = jnp.where(row == 7, level[-1], pltpu.roll(level[0], 7, 0))
            rimmed = [before, *level, after]
            south = [jnp.where(lane == 0, cell, pltpu.roll(cell, 1, 1)) for cell in level]
            north = [jnp.where(lane == S - 1, cell, pltpu.roll(cell, S - 1, 1)) for cell in level]
            yield
            new = []
            for k in range(ROWS):
                cell = rimmed[k + 1]
                west, east = rimmed[k], rimmed[k + 2]
                dx = east - west
                dy = north[k] - south[k]
                square = dx * dx + dy * dy + 4.0 * regular
                length = square * lax.rsqrt(square)
                move = jnp.maximum(length + (wind[0][k] * dx + wind[1][k] * dy), 0.0)
                around = (east + west) + (north[k] + south[k])
                cell = cell * (1.0 - 4.0 * diffusion) + around * diffusion - rate[k] * move
                fuel[k] = fuel[k] * ((1.0 - 0.5 * burn_rate) + (0.5 * burn_rate) * jnp.tanh(cell))
                new.append(cell)
            level = new
        yield
        for k in range(ROWS):
            level_own[t, pl.ds(k, 8, stride=ROWS), :] = level[k]
            fuel_own[t, pl.ds(k, 8, stride=ROWS), :] = fuel[k]
        heats[t] = (heat - sum(fuel[1:], fuel[0])) * (1.0 / (R * R))

    def some(i, carry):
        tiles = [i * SIDE + j for j in range(SIDE)]
        for t in tiles:
            for copy in inputs(t):
                copy.wait()
        works = [burn(t) for t in tiles]
        while works:
            works = [w for w in works if next(w, works) is None]
        for t in tiles:
            for copy in results(t):
                copy.start()
        return carry

    lax.fori_loop(0, TPD // SIDE, some, 0)

    for d in range(peers * CAP):
        outbox[d] = jnp.where(row < TA, 0.0, -1.0)
    pairs = [heats[t] for t in range(TPD)]
    pairs = [h + pltpu.roll(h, 7, 0) for h in pairs]
    pairs = [jnp.take_along_axis(h, jnp.minimum(2 * row, 7), axis=0) for h in pairs]
    sums = [
        [jnp.sum(jnp.where(lane // R == b, h, 0.0), axis=1, keepdims=True) for b in range(TA)] for h in pairs
    ]
    for t in range(TPD):
        message = jnp.where(row < TA, 0.0, (x_own[t] + row - TA).astype(F32))
        for b in range(TA):
            message = jnp.where(jnp.logical_and(row < TA, lane == y_own[t] + b), sums[t][b], message)
        owner = owner_ref[t]
        rank = count[owner]
        count[owner] = rank + 1
        outbox[owner * CAP + rank] = message
    for t in range(TPD):
        for copy in results(t):
            copy.wait()


def fire(owners, places, winds, level_set, fuel_load, spread_base, peers, waits):
    rows = peers * CX + 2 * RIM
    tiles = (TPD, S, S)
    return pl.pallas_call(
        functools.partial(fire_kernel, peers, len(waits)),
        in_specs=[SCALARS, SCALARS, LOCAL] + [FAR] * 3 + [ANYWHERE] * len(waits),
        out_specs=[ANYWHERE, ANYWHERE, LOCAL],
        out_shape=[
            jax.ShapeDtypeStruct(tiles, F32),
            jax.ShapeDtypeStruct(tiles, F32),
            pltpu.VMEM((peers * CAP, 8, 128), F32),
        ],
        scratch_shapes=[
            pltpu.VMEM((2, rows, 128), F32),
            pltpu.VMEM((2, rows, 128), F32),
            pltpu.VMEM((2 * TPD, 8, 128), F32),
            pltpu.VMEM((2 * TPD, 8, 128), F32),
            pltpu.VMEM((TPD, 8, 128), F32),
            pltpu.VMEM(tiles, F32),
            pltpu.VMEM(tiles, F32),
            pltpu.VMEM(tiles, F32),
            pltpu.SMEM((peers,), jnp.int32),
            pltpu.SemaphoreType.DMA((3, TPD)),
            pltpu.SemaphoreType.DMA((2, TPD)),
        ],
        name="fire",
        compiler_params=params(12),
        cost_estimate=pl.CostEstimate(
            flops=50_000_000, bytes_accessed=6_500_000, transcendentals=3_200_000
        ),
    )(owners, places, near(winds), *(far(a) for a in (level_set, fuel_load, spread_base)), *waits)


def final_kernel(inbox_ref, part_ref, out_ref, field, result, sems):
    inbox = inbox_ref[...]
    slots = inbox.shape[0]
    position = pltpu.roll(inbox, TA, 1).reshape(slots * 8, 128)
    values = inbox.reshape(slots * 8, 128)
    lane = iota(1, (slots * 8, 128)).astype(F32)
    valid = iota(0, (slots * 8, 128)) % 8 < TA
    hot = jnp.where(jnp.logical_and(valid, lane == position), 1.0, 0.0)
    total = lax.dot_general(
        hot, values, (((0,), (0,)), ((), ())),
        precision=lax.Precision.HIGHEST, preferred_element_type=F32,
    )
    field[...] = total[:CX]

    def copy(g):
        part = pl.ds(g * GROUP, GROUP)
        return pltpu.make_async_copy(result.at[part], out_ref.at[part], sems.at[g])

    def one(g, carry):
        for k in range(GROUP):
            z = g * GROUP + k
            height = jnp.full((8, 128), z, jnp.int32).astype(F32)
            gain = heat_gain * jnp.exp((height + 0.5) * (-4.0 / LZ))
            result[z] = part_ref[z] + field[...] * jnp.concatenate([gain] * (CX // 8), axis=0)
        copy(g).start()
        return carry

    lax.fori_loop(0, GROUPS, one, 0)
    for g in range(GROUPS):
        copy(g).wait()


def finish(inbox, part):
    return pl.pallas_call(
        final_kernel,
        in_specs=[LOCAL, LOCAL],
        out_specs=ANYWHERE,
        out_shape=jax.ShapeDtypeStruct((LZ, CX, CY), F32),
        scratch_shapes=[
            pltpu.VMEM((CX, CY), F32),
            pltpu.VMEM((LZ, CX, CY), F32),
            pltpu.SemaphoreType.DMA((GROUPS,)),
        ],
        name="finish",
        compiler_params=params(8),
        cost_estimate=pl.CostEstimate(flops=3_000_000, bytes_accessed=2_700_000, transcendentals=0),
    )(near(inbox), near(part))


def shifted(cells, axis, up):
    ends = lax.axis_size(axis) - 1
    pairs = [(i, i + 1) if up else (i + 1, i) for i in range(ends)]
    return lax.ppermute(cells, axis, pairs)


def exchange(cells):
    return lax.all_to_all(cells, "gx", split_axis=0, concat_axis=0, tiled=True)


def body(theta, wind_u, wind_v, level_set, fuel_load, spread_base, tile_owner, tile_place):
    peers = lax.axis_size("gx")
    block, up, down = wind_edges(wind_u, wind_v)
    low = shifted(up, "gy", True)
    high = shifted(down, "gy", False)
    packed = pack_winds(block, low, high, peers)
    winds = exchange(packed)

    first_x, last_x, first_y, last_y = theta_edges(low, theta)
    west = shifted(last_x, "gx", True)
    east = shifted(first_x, "gx", False)
    south = shifted(last_y, "gy", True)
    north = shifted(first_y, "gy", False)

    level_out, fuel_out, outbox = fire(
        tile_owner[0, 0], tile_place[0, 0], winds, level_set[0, 0], fuel_load[0, 0], spread_base[0, 0], peers,
        (west, east, south, north),
    )
    part = advect(theta, wind_u, wind_v, west, east, south, north)
    inbox = exchange(outbox)
    theta_next = finish(inbox, part)
    return (theta_next, level_out[None, None], fuel_out[None, None])


def solution(mesh):
    in_specs = (
        P(None, "gx", "gy"),
        P(None, "gx", "gy"),
        P(None, "gx", "gy"),
        P("gx", "gy", None, None, None),
        P("gx", "gy", None, None, None),
        P("gx", "gy", None, None, None),
        P("gx", "gy", None),
        P("gx", "gy", None),
    )
    out_specs = (
        P(None, "gx", "gy"),
        P("gx", "gy", None, None, None),
        P("gx", "gy", None, None, None),
    )
    return jax.shard_map(body, mesh=mesh, in_specs=in_specs, out_specs=out_specs, check_vma=False)
```

time: 90.3 us -> 65.6 us (0.73)
  the two profiles are of different devices: /device:TPU:1 before, /device:TPU:16 now
where the time goes in v3:
time: 65.6 us; the launch traced here: 65.1 us
  starting transfers between devices  28.3 us (43%)
  Pallas kernels  22.6 us (34%)
  waiting for transfers between devices  13.4 us (20%)
  between operations  0.75 us (1%)
    ppermute x6, starting transfers between devices, shifted(): return lax.ppermute(cells, axis, pairs)  16.2 us
    all_to_all x2, starting transfers between devices, exchange(): return lax.all_to_all(cells, 'gx', split_axis=0, concat_axis=0, tiled=True)  12.1 us
    pallas_call x1, Pallas kernels, fire(): pl.pallas_call(functools.partial(fire_kernel, peers, len(waits)), in_spec...  11.2 us
    all_to_all x2, waiting for transfers between devices, exchange(): return lax.all_to_all(cells, 'gx', split_axis=0, concat_axis=0, tiled=True)  8.18 us
    ppermute x6, waiting for transfers between devices, shifted(): return lax.ppermute(cells, axis, pairs)  5.2 us
    pallas_call x1, Pallas kernels, advect(): pl.pallas_call(advect_kernel, in_specs=[FAR] * 3 + [LOCAL] * 4, out_specs...  4.93 us
    pallas_call x1, Pallas kernels, theta_edges(): pl.pallas_call(theta_edge_kernel, in_specs=[ANYWHERE, FAR], out_specs=[LO...  2.57 us
    pallas_call x1, Pallas kernels, finish(): pl.pallas_call(final_kernel, in_specs=[LOCAL, LOCAL], out_specs=ANYWHERE,...  1.91 us
  transfers between devices with their start and end apart: 8, of which 6 were waited for; matrix products, arithmetic and copies ran while one was open for 0% of the time, Pallas kernels for 12%

profile of v3, /device:TPU:16, one launch (start us, length us, event | category | flops | bytes accessed | tf_op | source)
XLA Modules:
  0.0 65.1 jit_solution(9119113103467592637)
XLA Ops:
  0.6 0.9 %wind_edges.1 = (f32[128,128]{1,0:T(8,128)S(1)}, f32[8,128]{1,0:T(8,128)S(1)}, f32[8,128]{1,0:T(8,128)S(1)}) custom-call(f32[80,64,128]{2,1,0:T(8,128)} %u_ref.3, f32[80,64,128]{2,1,0:T(8,128)} %v_ref.3), custom_call_target="tpu_custom_call" | custom-call | tf_op jit(solution)/shard_map/wind_edges/pallas_call | solution.py:75
  1.5 1.9 %collective-permute-start = (f32[8,128]{1,0:T(8,128)S(1)}, f32[8,128]{1,0:T(8,128)S(1)}, u32[]{:S(2)}, u32[]{:S(2)}) collective-permute-start(f32[8,128]{1,0:T(8,128)S(1)} %get-tuple-element.14), channel_id=1, source_target_pairs={{0,1},{1,2},{2,3},{3,4},{4,5},{5,6},{6,7},{8,9},{9,10},{10,11},{11... | collective-permute-start | bytes 12296 | tf_op jit(solution)/shard_map/ppermute | solution.py:441
  3.5 3.6 %collective-permute-start.1 = (f32[8,128]{1,0:T(8,128)S(1)}, f32[8,128]{1,0:T(8,128)S(1)}, u32[]{:S(2)}, u32[]{:S(2)}) collective-permute-start(f32[8,128]{1,0:T(8,128)S(1)} %get-tuple-element.15), channel_id=1, source_target_pairs={{1,0},{2,1},{3,2},{4,3},{5,4},{6,5},{7,6},{9,8},{10,9},{11,10},{12... | collective-permute-start | bytes 12296 | tf_op jit(solution)/shard_map/ppermute | solution.py:441
  7.1 0.0 collective-permute-done.low_ref.after_ref
  7.1 1.3 %collective-permute-done.1.high_ref = f32[8,128]{1,0:T(8,128)S(1)} collective-permute-done((f32[8,128]{1,0:T(8,128)S(1)}, f32[8,128]{1,0:T(8,128)S(1)}, u32[]{:S(2)}, u32[]{:S(2)}) %collective-permute-start.1) | collective-permute-done | bytes 4128 | tf_op jit(solution)/shard_map/ppermute | solution.py:441
  8.4 1.1 %pack_winds.1 = f32[16,136,128]{2,1,0:T(8,128)} custom-call(f32[128,128]{1,0:T(8,128)S(1)} %get-tuple-element.13.block_ref, f32[8,128]{1,0:T(8,128)S(1)} %collective-permute-done.low_ref.after_ref, f32[8,128]{1,0:T(8,128)S(1)} %collective-permute-done.1.high_ref), custom_call_target="tpu_custom_call" | custom-call | tf_op jit(solution)/shard_map/pack_winds/pallas_call | solution.py:94
  9.5 0.0 copy-start
  9.5 0.0 copy-start.1
  9.5 8.0 %all-to-all-start = ((f32[16,136,128]{2,1,0:T(8,128)}), f32[16,136,128]{2,1,0:T(8,128)S(1)}, u32[]{:S(2)}, u32[]{:S(2)}) async-start(f32[16,136,128]{2,1,0:T(8,128)} %pack_winds.1), calls=%async_computation | async-start | bytes 2228224 | tf_op jit(solution)/shard_map/all_to_all | solution.py:445
  17.5 2.6 %theta_edges.1 = (f32[80,128]{1,0:T(8,128)S(1)}, f32[80,128]{1,0:T(8,128)S(1)}, f32[64,128]{1,0:T(8,128)S(1)}, f32[64,128]{1,0:T(8,128)S(1)}) custom-call(f32[8,128]{1,0:T(8,128)S(1)} %collective-permute-done.low_ref.after_ref, f32[80,64,128]{2,1,0:T(8,128)} %theta_ref.3), custom_call_target="tpu_custom_call" | custom-call | flops 4000000 | bytes 2700000 | tf_op jit(solution)/shard_map/theta_edges/pallas_call | solution.py:138
  20.1 3.8 %collective-permute-start.2 = (f32[80,128]{1,0:T(8,128)S(1)}, f32[80,128]{1,0:T(8,128)S(1)}, u32[]{:S(2)}, u32[]{:S(2)}) collective-permute-start(f32[80,128]{1,0:T(8,128)S(1)} %get-tuple-element.16), channel_id=1, source_target_pairs={{0,8},{8,16},{16,24},{24,32},{32,40},{40,48},{48,56},{56,64},{64,7... | collective-permute-start | bytes 122888 | tf_op jit(solution)/shard_map/ppermute | solution.py:441
  23.9 1.3 %collective-permute-start.3 = (f32[80,128]{1,0:T(8,128)S(1)}, f32[80,128]{1,0:T(8,128)S(1)}, u32[]{:S(2)}, u32[]{:S(2)}) collective-permute-start(f32[80,128]{1,0:T(8,128)S(1)} %get-tuple-element.17), channel_id=1, source_target_pairs={{8,0},{16,8},{24,16},{32,24},{40,32},{48,40},{56,48},{64,56},{72,6... | collective-permute-start | bytes 122888 | tf_op jit(solution)/shard_map/ppermute | solution.py:441
  25.2 2.4 %collective-permute-start.4 = (f32[64,128]{1,0:T(8,128)S(1)}, f32[64,128]{1,0:T(8,128)S(1)}, u32[]{:S(2)}, u32[]{:S(2)}) collective-permute-start(f32[64,128]{1,0:T(8,128)S(1)} %get-tuple-element.18), channel_id=1, source_target_pairs={{0,1},{1,2},{2,3},{3,4},{4,5},{5,6},{6,7},{8,9},{9,10},{10,11},{11... | collective-permute-start | bytes 98312 | tf_op jit(solution)/shard_map/ppermute | solution.py:441
  27.6 3.1 %collective-permute-start.5 = (f32[64,128]{1,0:T(8,128)S(1)}, f32[64,128]{1,0:T(8,128)S(1)}, u32[]{:S(2)}, u32[]{:S(2)}) collective-permute-start(f32[64,128]{1,0:T(8,128)S(1)} %get-tuple-element.19), channel_id=1, source_target_pairs={{1,0},{2,1},{3,2},{4,3},{5,4},{6,5},{7,6},{9,8},{10,9},{11,10},{12... | collective-permute-start | bytes 98312 | tf_op jit(solution)/shard_map/ppermute | solution.py:441
  30.8 0.0 collective-permute-done.4.rest_2_.south_ref
  30.8 1.6 %collective-permute-done.5.rest_3_.north_ref = f32[64,128]{1,0:T(8,128)S(1)} collective-permute-done((f32[64,128]{1,0:T(8,128)S(1)}, f32[64,128]{1,0:T(8,128)S(1)}, u32[]{:S(2)}, u32[]{:S(2)}) %collective-permute-start.5) | collective-permute-done | bytes 32800 | tf_op jit(solution)/shard_map/ppermute | solution.py:441
  32.4 1.1 %collective-permute-done.2.rest_0_.west_ref = f32[80,128]{1,0:T(8,128)S(1)} collective-permute-done((f32[80,128]{1,0:T(8,128)S(1)}, f32[80,128]{1,0:T(8,128)S(1)}, u32[]{:S(2)}, u32[]{:S(2)}) %collective-permute-start.2) | collective-permute-done | bytes 40992 | tf_op jit(solution)/shard_map/ppermute | solution.py:441
  33.4 1.3 %collective-permute-done.3.rest_1_.east_ref = f32[80,128]{1,0:T(8,128)S(1)} collective-permute-done((f32[80,128]{1,0:T(8,128)S(1)}, f32[80,128]{1,0:T(8,128)S(1)}, u32[]{:S(2)}, u32[]{:S(2)}) %collective-permute-start.3) | collective-permute-done | bytes 40992 | tf_op jit(solution)/shard_map/ppermute | solution.py:441
  34.7 5.1 %all-to-all-done.winds_ref = f32[16,136,128]{2,1,0:T(8,128)S(1)} async-done(((f32[16,136,128]{2,1,0:T(8,128)}), f32[16,136,128]{2,1,0:T(8,128)S(1)}, u32[]{:S(2)}, u32[]{:S(2)}) %all-to-all-start) | async-done | bytes 1114144 | tf_op jit(solution)/shard_map/all_to_all | solution.py:445
  39.8 0.0 copy-done
  39.8 0.0 copy-done.1
  39.8 11.2 %fire.1 = (f32[16,128,128]{2,1,0:T(8,128)}, f32[16,128,128]{2,1,0:T(8,128)}, f32[32,8,128]{2,1,0:T(8,128)}) custom-call(s32[16]{0:T(128)S(1)} %bitcast.7, s32[16]{0:T(128)S(1)} %bitcast.8, f32[16,136,128]{2,1,0:T(8,128)S(1)} %all-to-all-done.winds_ref, f32[16,128,128]{2,1,0:T(8,128)} %bitcast.9, f32[16,128,128]{2,1,0:T(8,128)} %bitcast.10, ...), custom_call_target="tpu_custom_call" | custom-call | flops 50000000 | bytes 6500000 | tf_op jit(solution)/shard_map/fire/pallas_call | solution.py:359
  51.1 4.1 %all-to-all-start.1 = ((f32[32,8,128]{2,1,0:T(8,128)}), f32[32,8,128]{2,1,0:T(8,128)S(1)}, u32[]{:S(2)}, u32[]{:S(2)}) async-start(f32[32,8,128]{2,1,0:T(8,128)} %get-tuple-element.20), calls=%async_computation.1 | async-start | bytes 262144 | tf_op jit(solution)/shard_map/all_to_all | solution.py:445
  55.1 4.9 %advect.1.part_ref = f32[80,64,128]{2,1,0:T(8,128)S(1)} custom-call(f32[80,64,128]{2,1,0:T(8,128)} %theta_ref.3, f32[80,64,128]{2,1,0:T(8,128)} %u_ref.3, f32[80,64,128]{2,1,0:T(8,128)} %v_ref.3, f32[80,128]{1,0:T(8,128)S(1)} %collective-permute-done.2.rest_0_.west_ref, f32[80,128]{1,0:T(8,128)S(1)} %collective-permute-done.3.rest_1_.east_ref, ...), custom_call_target="tpu_custom_call" | custom-call | flops 14000000 | bytes 8000000 | tf_op jit(solution)/shard_map/advect/pallas_call | solution.py:203
  60.1 3.1 %all-to-all-done.1.inbox_ref = f32[32,8,128]{2,1,0:T(8,128)S(1)} async-done(((f32[32,8,128]{2,1,0:T(8,128)}), f32[32,8,128]{2,1,0:T(8,128)S(1)}, u32[]{:S(2)}, u32[]{:S(2)}) %all-to-all-start.1) | async-done | bytes 131104 | tf_op jit(solution)/shard_map/all_to_all | solution.py:445
  63.1 1.9 %finish.1 = f32[80,64,128]{2,1,0:T(8,128)} custom-call(f32[32,8,128]{2,1,0:T(8,128)S(1)} %all-to-all-done.1.inbox_ref, f32[80,64,128]{2,1,0:T(8,128)S(1)} %advect.1.part_ref), custom_call_target="tpu_custom_call" | custom-call | flops 3000000 | bytes 2700000 | tf_op jit(solution)/shard_map/finish/pallas_call | solution.py:422
Async XLA Ops:
  1.5 5.6 %collective-permute-start = (f32[8,128]{1,0:T(8,128)S(1)}, f32[8,128]{1,0:T(8,128)S(1)}, u32[]{:S(2)}, u32[]{:S(2)}) collective-permute-start(f32[8,128]{1,0:T(8,128)S(1)} %get-tuple-element.14), channel_id=1, source_target_pairs={{0,1},{1,2},{2,3},{3,4},{4,5},{5,6},{6,7},{8,9},{9,10},{10,11},{11... | collective-permute-start | bytes 12296 | tf_op jit(solution)/shard_map/ppermute | solution.py:441
  3.5 5.0 %collective-permute-start.1 = (f32[8,128]{1,0:T(8,128)S(1)}, f32[8,128]{1,0:T(8,128)S(1)}, u32[]{:S(2)}, u32[]{:S(2)}) collective-permute-start(f32[8,128]{1,0:T(8,128)S(1)} %get-tuple-element.15), channel_id=1, source_target_pairs={{1,0},{2,1},{3,2},{4,3},{5,4},{6,5},{7,6},{9,8},{10,9},{11,10},{12... | collective-permute-start | bytes 12296 | tf_op jit(solution)/shard_map/ppermute | solution.py:441
  9.5 30.4 %copy-start = (s32[1,1,16]{2,1,0:T(1,128)S(1)}, s32[1,1,16]{2,1,0:T(1,128)}, u32[]{:S(2)}) copy-start(s32[1,1,16]{2,1,0:T(1,128)} %param.14) | copy-start | bytes 196
  9.5 30.4 %copy-start.1 = (s32[1,1,16]{2,1,0:T(1,128)S(1)}, s32[1,1,16]{2,1,0:T(1,128)}, u32[]{:S(2)}) copy-start(s32[1,1,16]{2,1,0:T(1,128)} %param.15) | copy-start | bytes 196
  9.5 30.3 %all-to-all-start = ((f32[16,136,128]{2,1,0:T(8,128)}), f32[16,136,128]{2,1,0:T(8,128)S(1)}, u32[]{:S(2)}, u32[]{:S(2)}) async-start(f32[16,136,128]{2,1,0:T(8,128)} %pack_winds.1), calls=%async_computation | async-start | bytes 2228224 | tf_op jit(solution)/shard_map/all_to_all | solution.py:445
  20.1 13.4 %collective-permute-start.2 = (f32[80,128]{1,0:T(8,128)S(1)}, f32[80,128]{1,0:T(8,128)S(1)}, u32[]{:S(2)}, u32[]{:S(2)}) collective-permute-start(f32[80,128]{1,0:T(8,128)S(1)} %get-tuple-element.16), channel_id=1, source_target_pairs={{0,8},{8,16},{16,24},{24,32},{32,40},{40,48},{48,56},{56,64},{64,7... | collective-permute-start | bytes 122888 | tf_op jit(solution)/shard_map/ppermute | solution.py:441
  23.9 10.8 %collective-permute-start.3 = (f32[80,128]{1,0:T(8,128)S(1)}, f32[80,128]{1,0:T(8,128)S(1)}, u32[]{:S(2)}, u32[]{:S(2)}) collective-permute-start(f32[80,128]{1,0:T(8,128)S(1)} %get-tuple-element.17), channel_id=1, source_target_pairs={{8,0},{16,8},{24,16},{32,24},{40,32},{48,40},{56,48},{64,56},{72,6... | collective-permute-start | bytes 122888 | tf_op jit(solution)/shard_map/ppermute | solution.py:441
  25.2 5.6 %collective-permute-start.4 = (f32[64,128]{1,0:T(8,128)S(1)}, f32[64,128]{1,0:T(8,128)S(1)}, u32[]{:S(2)}, u32[]{:S(2)}) collective-permute-start(f32[64,128]{1,0:T(8,128)S(1)} %get-tuple-element.18), channel_id=1, source_target_pairs={{0,1},{1,2},{2,3},{3,4},{4,5},{5,6},{6,7},{8,9},{9,10},{10,11},{11... | collective-permute-start | bytes 98312 | tf_op jit(solution)/shard_map/ppermute | solution.py:441
  27.6 4.7 %collective-permute-start.5 = (f32[64,128]{1,0:T(8,128)S(1)}, f32[64,128]{1,0:T(8,128)S(1)}, u32[]{:S(2)}, u32[]{:S(2)}) collective-permute-start(f32[64,128]{1,0:T(8,128)S(1)} %get-tuple-element.19), channel_id=1, source_target_pairs={{1,0},{2,1},{3,2},{4,3},{5,4},{6,5},{7,6},{9,8},{10,9},{11,10},{12... | collective-permute-start | bytes 98312 | tf_op jit(solution)/shard_map/ppermute | solution.py:441
  51.1 12.1 %all-to-all-start.1 = ((f32[32,8,128]{2,1,0:T(8,128)}), f32[32,8,128]{2,1,0:T(8,128)S(1)}, u32[]{:S(2)}, u32[]{:S(2)}) async-start(f32[32,8,128]{2,1,0:T(8,128)} %get-tuple-element.20), calls=%async_computation.1 | async-start | bytes 262144 | tf_op jit(solution)/shard_map/all_to_all | solution.py:445

commit v4 on v3

--- a/solution.py
+++ b/solution.py
@@ -17,8 +17,9 @@
 CX = 64
 CY = 128
 ROWS = S // 8
-BLOCK = 2 * CX + 8
 RIM = 8
+SIDES = (0, 1, -1)
+WIND = 100
 GROUP = 8
 GROUPS = LZ // GROUP
 SIDE = 2
@@ -54,60 +55,61 @@
     return pltpu.CompilerParams(vmem_limit_bytes=mib * 1024 * 1024)
 
 
-def wind_edge_kernel(u_ref, v_ref, block_ref, up_ref, down_ref, sems):
-    copies = [
-        pltpu.make_async_copy(ref.at[0], block_ref.at[c * CX : (c + 1) * CX], sems.at[c])
-        for c, ref in enumerate((u_ref, v_ref))
-    ]
-    for copy in copies:
-        copy.start()
-    for copy in copies:
-        copy.wait()
-    columns = jnp.transpose(block_ref[...])
-    row = iota(0)
-    last = jnp.broadcast_to(columns[CY - 1 : CY], (8, 128))
-    first = jnp.broadcast_to(columns[0:1], (8, 128))
-    up_ref[...] = jnp.where(row == 0, last, 0.0)
-    down_ref[...] = jnp.where(row == TA + 1, first, 0.0)
-
-
-def wind_edges(wind_u, wind_v):
+def ranks_of(owner_ref, count, peers):
+    for d in range(peers):
+        count[d] = 0
+    ranks = []
+    for t in range(TPD):
+        owner = owner_ref[t]
+        ranks.append(count[owner])
+        count[owner] = ranks[t] + 1
+    return ranks
+
+
+def request_kernel(owner_ref, place_ref, out_ref, table, count):
+    peers = out_ref.shape[0]
+    for i in range((peers + 2) * CAP):
+        table[i] = -1
+    ranks = ranks_of(owner_ref, count, peers)
+    for t in range(TPD):
+        table[(owner_ref[t] + 1) * CAP + ranks[t]] = place_ref[t]
+    lane = iota(1, (1, 128))
+    for peer in range(peers):
+        line = jnp.full((1, 128), -1, jnp.int32)
+        for g, side in enumerate(SIDES):
+            for r in range(CAP):
+                line = jnp.where(lane == g * CAP + r, table[(peer + 1 + side) * CAP + r], line)
+        out_ref[peer] = line
+
+
+def make_requests(owners, places, peers):
     return pl.pallas_call(
-        wind_edge_kernel,
-        in_specs=[FAR, FAR],
-        out_specs=[LOCAL, LOCAL, LOCAL],
-        out_shape=[pltpu.VMEM((2 * CX, 128), F32), pltpu.VMEM((8, 128), F32), pltpu.VMEM((8, 128), F32)],
-        scratch_shapes=[pltpu.SemaphoreType.DMA((2,))],
-        name="wind_edges",
+        request_kernel,
+        in_specs=[SCALARS, SCALARS],
+        out_specs=LOCAL,
+        out_shape=pltpu.VMEM((peers, 1, 128), jnp.int32),
+        scratch_shapes=[pltpu.SMEM(((peers + 2) * CAP,), jnp.int32), pltpu.SMEM((peers,), jnp.int32)],
+        name="make_requests",
         compiler_params=params(4),
-    )(far(wind_u), far(wind_v))
-
-
-def pack_kernel(block_ref, low_ref, high_ref, out_ref):
-    edge = low_ref[...] + high_ref[...]
-    for peer in range(out_ref.shape[0]):
-        out_ref[peer, : 2 * CX] = block_ref[...]
-        out_ref[peer, 2 * CX :] = edge
-
-
-def pack_winds(block, low, high, peers):
-    return pl.pallas_call(
-        pack_kernel,
-        in_specs=[LOCAL, LOCAL, LOCAL],
-        out_specs=LOCAL,
-        out_shape=pltpu.VMEM((peers, BLOCK, 128), F32),
-        name="pack_winds",
-        compiler_params=params(4),
-    )(near(block), near(low), near(high))
-
-
-def theta_edge_kernel(after_ref, theta_ref, first_x_ref, last_x_ref, first_y_ref, last_y_ref, theta, sems):
+    )(owners, places)
+
+
+def edge_kernel(
+    after_ref, theta_ref, u_ref, v_ref,
+    block_ref, first_x_ref, last_x_ref, first_y_ref, last_y_ref, theta, sems, wind_sems,
+):
     def copy(g):
         part = pl.ds(g * GROUP, GROUP)
         return pltpu.make_async_copy(theta_ref.at[part], theta.at[part], sems.at[g])
 
+    winds = [
+        pltpu.make_async_copy(ref.at[0], block_ref.at[c * CX : (c + 1) * CX], wind_sems.at[c])
+        for c, ref in enumerate((u_ref, v_ref))
+    ]
     for g in reversed(range(GROUPS)):
         copy(g).start()
+    for wind in winds:
+        wind.start()
     lane = iota(1, (CX, 128))
 
     def one(i, carry):
@@ -128,23 +130,86 @@
 
     zero = jnp.zeros((CX, 128), F32)
     first, last = lax.fori_loop(0, GROUPS, one, (zero, zero))
+    for wind in winds:
+        wind.wait()
+    for c in range(2):
+        cells = block_ref[c * CX : (c + 1) * CX]
+        first = jnp.where(lane == WIND + c, pltpu.roll(cells, WIND + c, 1), first)
+        last = jnp.where(lane == WIND + c, pltpu.roll(cells, WIND + c + 1, 1), last)
     first_y_ref[...] = first
     last_y_ref[...] = last
 
 
-def theta_edges(after, theta):
+def make_edges(after, theta, wind_u, wind_v):
     row = pltpu.VMEM((LZ, 128), F32)
     column = pltpu.VMEM((CX, 128), F32)
     return pl.pallas_call(
-        theta_edge_kernel,
-        in_specs=[ANYWHERE, FAR],
-        out_specs=[LOCAL] * 4,
-        out_shape=[row, row, column, column],
-        scratch_shapes=[pltpu.VMEM((LZ, CX, CY), F32), pltpu.SemaphoreType.DMA((GROUPS,))],
-        name="theta_edges",
+        edge_kernel,
+        in_specs=[ANYWHERE, FAR, FAR, FAR],
+        out_specs=[LOCAL] * 5,
+        out_shape=[pltpu.VMEM((2 * CX, 128), F32), row, row, column, column],
+        scratch_shapes=[
+            pltpu.VMEM((LZ, CX, CY), F32),
+            pltpu.SemaphoreType.DMA((GROUPS,)),
+            pltpu.SemaphoreType.DMA((2,)),
+        ],
+        name="edges",
         compiler_params=params(8),
         cost_estimate=pl.CostEstimate(flops=4_000_000, bytes_accessed=2_700_000, transcendentals=0),
-    )(after, far(theta))
+    )(after, far(theta), far(wind_u), far(wind_v))
+
+
+def cut_kernel(
+    asked_ref, block_ref, south_ref, north_ref, first_x_ref, last_x_ref,
+    out_ref, first_x_out, last_x_out, surface, edges,
+):
+    first_x_out[...] = first_x_ref[...]
+    last_x_out[...] = last_x_ref[...]
+    wide = iota(1, (CX, 128))
+    lane = iota(1)
+    blank = jnp.zeros((RIM, 128), F32)
+    for c in range(2):
+        low = jnp.broadcast_to(south_ref[:, WIND + c : WIND + c + 1], (CX, 128))
+        high = jnp.broadcast_to(north_ref[:, WIND + c : WIND + c + 1], (CX, 128))
+        surface[c, 0:RIM] = blank
+        surface[c, RIM : RIM + CX] = block_ref[c * CX : (c + 1) * CX]
+        surface[c, RIM + CX :] = blank
+        edges[c, 0:RIM] = blank
+        edges[c, RIM : RIM + CX] = jnp.where(wide % 8 == 0, low, high)
+        edges[c, RIM + CX :] = blank
+    tiles_y = CY // TA
+    for source in range(out_ref.shape[0]):
+        message = jnp.zeros((8, 128), F32)
+        for g, side in enumerate(SIDES):
+            for r in range(CAP):
+                place = asked_ref[source, 0, g * CAP + r]
+                y_own = jnp.bitwise_and(place, tiles_y - 1) * TA
+                first = lax.shift_right_arithmetic(place, 5) * TA - 1 + side * CX
+                first = jnp.where(place < 0, CX, jnp.clip(first, -RIM, CX)) + RIM
+                begin = (g * CAP + r) * 16
+                outside = jnp.where(y_own == 0, 0, jnp.where(y_own == CY - TA, TA + 1, 1000))
+                for c in range(2):
+                    at = begin + 8 * c
+                    turn = jnp.bitwise_and(at + 1 - y_own, 127)
+                    part = pltpu.roll(surface[c, pl.ds(first, 8), :], turn, 1)
+                    part = jnp.where(lane == at + outside, edges[c, pl.ds(first, 8), :], part)
+                    message = jnp.where(lane // 8 == at // 8, part, message)
+        out_ref[source] = message
+
+
+def cut_patches(asked, block, south, north, first_x, last_x):
+    peers = asked.shape[0]
+    row = pltpu.VMEM((LZ, 128), F32)
+    rows = CX + 2 * RIM
+    return pl.pallas_call(
+        cut_kernel,
+        in_specs=[SCALARS] + [LOCAL] * 5,
+        out_specs=[LOCAL] * 3,
+        out_shape=[pltpu.VMEM((peers, 8, 128), F32), row, row],
+        scratch_shapes=[pltpu.VMEM((2, rows, 128), F32), pltpu.VMEM((2, rows, 128), F32)],
+        name="cut_patches",
+        compiler_params=params(4),
+    )(asked, *(near(a) for a in (block, south, north, first_x, last_x)))
 
 
 def advect_kernel(
@@ -216,7 +281,7 @@
     peers, waits, owner_ref, place_ref, winds_ref, level_ref, fuel_ref, base_ref, *rest
 ):
     (
-        level_out, fuel_out, outbox, surface, edges, begins, slopes, heats,
+        level_out, fuel_out, outbox, begins, slopes, heats,
         level_own, fuel_own, base_own, count, in_sems, out_sems,
     ) = rest[waits:]
     lane = iota(1)
@@ -240,38 +305,25 @@
         for copy in inputs(t):
             copy.start()
 
-    for c in range(2):
-        for ref in (surface, edges):
-            ref[c, 0:RIM] = jnp.zeros((RIM, 128), F32)
-            ref[c, RIM + peers * CX :] = jnp.zeros((RIM, 128), F32)
-    turned = jnp.transpose(jnp.concatenate([winds_ref[d, 2 * CX :] for d in range(peers)], axis=0))
-    for d in range(peers):
-        count[d] = 0
-        own = pltpu.roll(turned, (128 - 8 * d) % 128, 1)
-        for c in range(2):
-            surface[c, RIM + d * CX : RIM + (d + 1) * CX] = winds_ref[d, c * CX : (c + 1) * CX]
-            edges[c, RIM + d * CX : RIM + (d + 1) * CX] = own[c * CX : (c + 1) * CX]
-
     tiles_y = CY // TA
     low_row = (row + 1) // 2
     low_lane = (lane + R // 2) // R
     part_row = jnp.where(row % 2 == 0, 0.5, 0.0) + 0.5 / R
     part_lane = (lane.astype(F32) + 0.5) / R + 0.5 - low_lane.astype(F32)
 
-    x_own, y_own, patches = [], [], []
+    ranks = ranks_of(owner_ref, count, peers)
+    patches = []
     for t in range(TPD):
-        place = place_ref[t]
-        x_own.append(place // tiles_y * TA)
-        y_own.append(lax.rem(place, tiles_y) * TA)
-        first = owner_ref[t] * CX + x_own[t] + (RIM - 1)
-        back = lax.rem(CY + 1 - y_own[t], CY)
-        outside = jnp.logical_or(
-            jnp.logical_and(lane == 0, y_own[t] == 0),
-            jnp.logical_and(lane == TA + 1, y_own[t] == CY - TA),
-        )
+        owner = owner_ref[t]
+        parts = []
+        for g, side in enumerate(SIDES):
+            begin = (g * CAP + ranks[t]) * 16
+            inside = jnp.logical_and(owner >= side, owner - side < peers)
+            part = winds_ref[jnp.clip(owner - side, 0, peers - 1)]
+            part = jnp.where(inside, part, 0.0)
+            parts.append([pltpu.roll(part, jnp.bitwise_and(-begin - 8 * c, 127), 1) for c in range(2)])
         for c in range(2):
-            patch = pltpu.roll(surface[c, pl.ds(first, 8), :], back, 1)
-            patches.append(jnp.where(outside, edges[c, pl.ds(first, 8), :], patch))
+            patches.append(parts[0][c] + parts[1][c] + parts[2][c])
     left = [jnp.take_along_axis(p, low_lane, axis=1) for p in patches]
     right = [jnp.take_along_axis(p, low_lane + 1, axis=1) for p in patches]
     fine = [p + (q - p) * part_lane for p, q in zip(left, right)]
@@ -341,20 +393,19 @@
         [jnp.sum(jnp.where(lane // R == b, h, 0.0), axis=1, keepdims=True) for b in range(TA)] for h in pairs
     ]
     for t in range(TPD):
-        message = jnp.where(row < TA, 0.0, (x_own[t] + row - TA).astype(F32))
+        place = place_ref[t]
+        x_own = place // tiles_y * TA
+        y_own = lax.rem(place, tiles_y) * TA
+        message = jnp.where(row < TA, 0.0, (x_own + row - TA).astype(F32))
         for b in range(TA):
-            message = jnp.where(jnp.logical_and(row < TA, lane == y_own[t] + b), sums[t][b], message)
-        owner = owner_ref[t]
-        rank = count[owner]
-        count[owner] = rank + 1
-        outbox[owner * CAP + rank] = message
+            message = jnp.where(jnp.logical_and(row < TA, lane == y_own + b), sums[t][b], message)
+        outbox[owner_ref[t] * CAP + ranks[t]] = message
     for t in range(TPD):
         for copy in results(t):
             copy.wait()
 
 
 def fire(owners, places, winds, level_set, fuel_load, spread_base, peers, waits):
-    rows = peers * CX + 2 * RIM
     tiles = (TPD, S, S)
     return pl.pallas_call(
         functools.partial(fire_kernel, peers, len(waits)),
@@ -366,8 +417,6 @@
             pltpu.VMEM((peers * CAP, 8, 128), F32),
         ],
         scratch_shapes=[
-            pltpu.VMEM((2, rows, 128), F32),
-            pltpu.VMEM((2, rows, 128), F32),
             pltpu.VMEM((2 * TPD, 8, 128), F32),
             pltpu.VMEM((2 * TPD, 8, 128), F32),
             pltpu.VMEM((TPD, 8, 128), F32),
@@ -447,21 +496,21 @@
 
 def body(theta, wind_u, wind_v, level_set, fuel_load, spread_base, tile_owner, tile_place):
     peers = lax.axis_size("gx")
-    block, up, down = wind_edges(wind_u, wind_v)
-    low = shifted(up, "gy", True)
-    high = shifted(down, "gy", False)
-    packed = pack_winds(block, low, high, peers)
-    winds = exchange(packed)
-
-    first_x, last_x, first_y, last_y = theta_edges(low, theta)
+    owners, places = tile_owner[0, 0], tile_place[0, 0]
+    requests = make_requests(owners, places, peers)
+    asked = exchange(requests)
+
+    block, first_x, last_x, first_y, last_y = make_edges(requests, theta, wind_u, wind_v)
+    south = shifted(last_y, "gy", True)
+    north = shifted(first_y, "gy", False)
+
+    patches, first_x, last_x = cut_patches(asked, block, south, north, first_x, last_x)
+    winds = exchange(patches)
     west = shifted(last_x, "gx", True)
     east = shifted(first_x, "gx", False)
-    south = shifted(last_y, "gy", True)
-    north = shifted(first_y, "gy", False)
 
     level_out, fuel_out, outbox = fire(
-        tile_owner[0, 0], tile_place[0, 0], winds, level_set[0, 0], fuel_load[0, 0], spread_base[0, 0], peers,
-        (west, east, south, north),
+        owners, places, winds, level_set[0, 0], fuel_load[0, 0], spread_base[0, 0], peers, ()
     )
     part = advect(theta, wind_u, wind_v, west, east, south, north)
     inbox = exchange(outbox)

time: 65.6 us -> 71.8 us (1.095)
  the two profiles are of different devices: /device:TPU:16 before, /device:TPU:22 now
where the time goes in v4:
time: 71.8 us; the launch traced here: 71.4 us
  blocking collectives  24.3 us (34%)
  Pallas kernels  22.7 us (32%)
  starting transfers between devices  16.8 us (23%)
  waiting for transfers between devices  5.54 us (8%)
  local copies, waits for them, and re-layouts  1.32 us (2%)
  between operations  0.74 us (1%)
    all_to_all x2, blocking collectives, exchange(): return lax.all_to_all(cells, 'gx', split_axis=0, concat_axis=0, tiled=True)  24.3 us
    ppermute x4, starting transfers between devices, shifted(): return lax.ppermute(cells, axis, pairs)  11.4 us
    pallas_call x1, Pallas kernels, fire(): pl.pallas_call(functools.partial(fire_kernel, peers, len(waits)), in_spec...  11.1 us
    ppermute x4, waiting for transfers between devices, shifted(): return lax.ppermute(cells, axis, pairs)  5.54 us
    all_to_all x1, starting transfers between devices, exchange(): return lax.all_to_all(cells, 'gx', split_axis=0, concat_axis=0, tiled=True)  5.39 us
    pallas_call x1, Pallas kernels, advect(): pl.pallas_call(advect_kernel, in_specs=[FAR] * 3 + [LOCAL] * 4, out_specs...  4.93 us
    pallas_call x1, Pallas kernels, make_edges(): pl.pallas_call(edge_kernel, in_specs=[ANYWHERE, FAR, FAR, FAR], out_specs...  2.7 us
    pallas_call x1, Pallas kernels, finish(): pl.pallas_call(final_kernel, in_specs=[LOCAL, LOCAL], out_specs=ANYWHERE,...  1.92 us
  transfers between devices with their start and end apart: 5, of which 1 were waited for; matrix products, arithmetic and copies ran while one was open for 0% of the time, Pallas kernels for 7%

profile of v4, /device:TPU:22, one launch (start us, length us, event | category | flops | bytes accessed | tf_op | source)
XLA Modules:
  0.0 71.4 jit_solution(17424219051126268684)
XLA Ops:
  0.6 0.0 copy-start
  0.6 0.6 copy-done
  1.3 0.0 copy-start.2
  1.3 0.7 copy-done.2
  1.9 0.7 make_requests.1.after_ref
  2.6 0.0 copy-start.1
  2.6 0.0 copy-start.3
  2.6 2.7 %edges.1 = (f32[128,128]{1,0:T(8,128)S(1)}, f32[80,128]{1,0:T(8,128)S(1)}, f32[80,128]{1,0:T(8,128)S(1)}, f32[64,128]{1,0:T(8,128)S(1)}, f32[64,128]{1,0:T(8,128)S(1)}) custom-call(s32[16,1,128]{2,1,0:T(1,128)S(1)} %make_requests.1.after_ref, f32[80,64,128]{2,1,0:T(8,128)} %theta_ref.3, f32[80,64,128]{2,1,0:T(8,128)} %u_ref.3, f32[80,64,128]{2,1,0:T(8,128)} %v_ref.3), custom_call_target="tpu_custom_call" | custom-call | flops 4000000 | bytes 2700000 | tf_op jit(solution)/shard_map/edges/pallas_call | solution.py:146
  5.3 1.9 %collective-permute-start = (f32[64,128]{1,0:T(8,128)S(1)}, f32[64,128]{1,0:T(8,128)S(1)}, u32[]{:S(2)}, u32[]{:S(2)}) collective-permute-start(f32[64,128]{1,0:T(8,128)S(1)} %get-tuple-element.15), channel_id=1, source_target_pairs={{0,1},{1,2},{2,3},{3,4},{4,5},{5,6},{6,7},{8,9},{9,10},{10,11},{11... | collective-permute-start | bytes 98312 | tf_op jit(solution)/shard_map/ppermute | solution.py:490
  7.3 3.6 %collective-permute-start.1 = (f32[64,128]{1,0:T(8,128)S(1)}, f32[64,128]{1,0:T(8,128)S(1)}, u32[]{:S(2)}, u32[]{:S(2)}) collective-permute-start(f32[64,128]{1,0:T(8,128)S(1)} %get-tuple-element.16), channel_id=1, source_target_pairs={{1,0},{2,1},{3,2},{4,3},{5,4},{6,5},{7,6},{9,8},{10,9},{11,10},{12... | collective-permute-start | bytes 98312 | tf_op jit(solution)/shard_map/ppermute | solution.py:490
  10.9 13.7 %all_to_all.15.asked_ref = s32[16,1,128]{2,1,0:T(1,128)S(1)} all-to-all(s32[16,1,128]{2,1,0:T(1,128)S(1)} %make_requests.1.after_ref), channel_id=1, replica_groups=mesh['gx'=16,'gy'=8] {'gx'}, dimensions={0} | all-to-all | bytes 16384 | tf_op jit(solution)/shard_map/all_to_all | solution.py:494
  24.6 0.0 collective-permute-done.south_ref
  24.6 0.0 collective-permute-done.1.north_ref
  24.6 1.4 %cut_patches.1 = (f32[16,8,128]{2,1,0:T(8,128)S(1)}, f32[80,128]{1,0:T(8,128)S(1)}, f32[80,128]{1,0:T(8,128)S(1)}) custom-call(s32[16,1,128]{2,1,0:T(1,128)S(1)} %all_to_all.15.asked_ref, f32[128,128]{1,0:T(8,128)S(1)} %get-tuple-element.14.block_ref, f32[64,128]{1,0:T(8,128)S(1)} %collective-permute-done.south_ref, ...), custom_call_target="tpu_custom_call" | custom-call | tf_op jit(solution)/shard_map/cut_patches/pallas_call | solution.py:204
  26.0 10.6 %all_to_all.16.winds_ref = f32[16,8,128]{2,1,0:T(8,128)S(1)} all-to-all(f32[16,8,128]{2,1,0:T(8,128)S(1)} %get-tuple-element.19), channel_id=1, replica_groups=mesh['gx'=16,'gy'=8] {'gx'}, dimensions={0} | all-to-all | bytes 131072 | tf_op jit(solution)/shard_map/all_to_all | solution.py:494
  36.6 0.0 copy-done.1
  36.6 0.0 copy-done.3
  36.6 11.1 %fire.1 = (f32[16,128,128]{2,1,0:T(8,128)}, f32[16,128,128]{2,1,0:T(8,128)}, f32[32,8,128]{2,1,0:T(8,128)}) custom-call(s32[16]{0:T(128)S(1)} %bitcast.8, s32[16]{0:T(128)S(1)} %bitcast.10, f32[16,8,128]{2,1,0:T(8,128)S(1)} %all_to_all.16.winds_ref, f32[16,128,128]{2,1,0:T(8,128)} %bitcast.11, f32[16,128,128]{2,1,0:T(8,128)} %bitcast.12, ...), custom_call_target="tpu_custom_call" | custom-call | flops 50000000 | bytes 6500000 | tf_op jit(solution)/shard_map/fire/pallas_call | solution.py:410
  47.8 5.4 %all-to-all-start.2 = ((f32[32,8,128]{2,1,0:T(8,128)}), f32[32,8,128]{2,1,0:T(8,128)S(1)}, u32[]{:S(2)}, u32[]{:S(2)}) async-start(f32[32,8,128]{2,1,0:T(8,128)} %get-tuple-element.20), calls=%async_computation.2 | async-start | bytes 262144 | tf_op jit(solution)/shard_map/all_to_all | solution.py:494
  53.2 3.4 %collective-permute-start.2 = (f32[80,128]{1,0:T(8,128)S(1)}, f32[80,128]{1,0:T(8,128)S(1)}, u32[]{:S(2)}, u32[]{:S(2)}) collective-permute-start(f32[80,128]{1,0:T(8,128)S(1)} %get-tuple-element.21), channel_id=1, source_target_pairs={{0,8},{8,16},{16,24},{24,32},{32,40},{40,48},{48,56},{56,64},{64,7... | collective-permute-start | bytes 122888 | tf_op jit(solution)/shard_map/ppermute | solution.py:490
  56.5 2.5 %collective-permute-start.3 = (f32[80,128]{1,0:T(8,128)S(1)}, f32[80,128]{1,0:T(8,128)S(1)}, u32[]{:S(2)}, u32[]{:S(2)}) collective-permute-start(f32[80,128]{1,0:T(8,128)S(1)} %get-tuple-element.22), channel_id=1, source_target_pairs={{8,0},{16,8},{24,16},{32,24},{40,32},{48,40},{56,48},{64,56},{72,6... | collective-permute-start | bytes 122888 | tf_op jit(solution)/shard_map/ppermute | solution.py:490
  59.0 0.0 collective-permute-done.2.west_ref
  59.0 5.5 %collective-permute-done.3.east_ref = f32[80,128]{1,0:T(8,128)S(1)} collective-permute-done((f32[80,128]{1,0:T(8,128)S(1)}, f32[80,128]{1,0:T(8,128)S(1)}, u32[]{:S(2)}, u32[]{:S(2)}) %collective-permute-start.3) | collective-permute-done | bytes 40992 | tf_op jit(solution)/shard_map/ppermute | solution.py:490
  64.5 4.9 %advect.1.part_ref = f32[80,64,128]{2,1,0:T(8,128)S(1)} custom-call(f32[80,64,128]{2,1,0:T(8,128)} %theta_ref.3, f32[80,64,128]{2,1,0:T(8,128)} %u_ref.3, f32[80,64,128]{2,1,0:T(8,128)} %v_ref.3, f32[80,128]{1,0:T(8,128)S(1)} %collective-permute-done.2.west_ref, f32[80,128]{1,0:T(8,128)S(1)} %collective-permute-done.3.east_ref, ...), custom_call_target="tpu_custom_call" | custom-call | flops 14000000 | bytes 8000000 | tf_op jit(solution)/shard_map/advect/pallas_call | solution.py:268
  69.5 0.0 all-to-all-done.2.inbox_ref
  69.5 1.9 %finish.1 = f32[80,64,128]{2,1,0:T(8,128)} custom-call(f32[32,8,128]{2,1,0:T(8,128)S(1)} %all-to-all-done.2.inbox_ref, f32[80,64,128]{2,1,0:T(8,128)S(1)} %advect.1.part_ref), custom_call_target="tpu_custom_call" | custom-call | flops 3000000 | bytes 2700000 | tf_op jit(solution)/shard_map/finish/pallas_call | solution.py:471
Async XLA Ops:
  0.6 0.7 copy-start
  1.3 0.7 copy-start.2
  2.6 34.0 %copy-start.1 = (s32[1,1,16]{2,1,0:T(1,128)S(1)}, s32[1,1,16]{2,1,0:T(1,128)}, u32[]{:S(2)}) copy-start(s32[1,1,16]{2,1,0:T(1,128)} %param.14) | copy-start | bytes 196
  2.6 34.0 %copy-start.3 = (s32[1,1,16]{2,1,0:T(1,128)S(1)}, s32[1,1,16]{2,1,0:T(1,128)}, u32[]{:S(2)}) copy-start(s32[1,1,16]{2,1,0:T(1,128)} %param.15) | copy-start | bytes 196
  5.3 19.2 %collective-permute-start = (f32[64,128]{1,0:T(8,128)S(1)}, f32[64,128]{1,0:T(8,128)S(1)}, u32[]{:S(2)}, u32[]{:S(2)}) collective-permute-start(f32[64,128]{1,0:T(8,128)S(1)} %get-tuple-element.15), channel_id=1, source_target_pairs={{0,1},{1,2},{2,3},{3,4},{4,5},{5,6},{6,7},{8,9},{9,10},{10,11},{11... | collective-permute-start | bytes 98312 | tf_op jit(solution)/shard_map/ppermute | solution.py:490
  7.3 17.3 %collective-permute-start.1 = (f32[64,128]{1,0:T(8,128)S(1)}, f32[64,128]{1,0:T(8,128)S(1)}, u32[]{:S(2)}, u32[]{:S(2)}) collective-permute-start(f32[64,128]{1,0:T(8,128)S(1)} %get-tuple-element.16), channel_id=1, source_target_pairs={{1,0},{2,1},{3,2},{4,3},{5,4},{6,5},{7,6},{9,8},{10,9},{11,10},{12... | collective-permute-start | bytes 98312 | tf_op jit(solution)/shard_map/ppermute | solution.py:490
  47.8 21.7 %all-to-all-start.2 = ((f32[32,8,128]{2,1,0:T(8,128)}), f32[32,8,128]{2,1,0:T(8,128)S(1)}, u32[]{:S(2)}, u32[]{:S(2)}) async-start(f32[32,8,128]{2,1,0:T(8,128)} %get-tuple-element.20), calls=%async_computation.2 | async-start | bytes 262144 | tf_op jit(solution)/shard_map/all_to_all | solution.py:494
  53.2 5.9 %collective-permute-start.2 = (f32[80,128]{1,0:T(8,128)S(1)}, f32[80,128]{1,0:T(8,128)S(1)}, u32[]{:S(2)}, u32[]{:S(2)}) collective-permute-start(f32[80,128]{1,0:T(8,128)S(1)} %get-tuple-element.21), channel_id=1, source_target_pairs={{0,8},{8,16},{16,24},{24,32},{32,40},{40,48},{48,56},{56,64},{64,7... | collective-permute-start | bytes 122888 | tf_op jit(solution)/shard_map/ppermute | solution.py:490
  56.5 8.0 %collective-permute-start.3 = (f32[80,128]{1,0:T(8,128)S(1)}, f32[80,128]{1,0:T(8,128)S(1)}, u32[]{:S(2)}, u32[]{:S(2)}) collective-permute-start(f32[80,128]{1,0:T(8,128)S(1)} %get-tuple-element.22), channel_id=1, source_target_pairs={{8,0},{16,8},{24,16},{32,24},{40,32},{48,40},{56,48},{64,56},{72,6... | collective-permute-start | bytes 122888 | tf_op jit(solution)/shard_map/ppermute | solution.py:490

commit v5 on v4

--- a/solution.py
+++ b/solution.py
@@ -55,6 +55,14 @@
     return pltpu.CompilerParams(vmem_limit_bytes=mib * 1024 * 1024)
 
 
+def to_scalars(refs, scalars, sems):
+    copies = [pltpu.make_async_copy(ref, own, sems.at[c]) for c, (ref, own) in enumerate(zip(refs, scalars))]
+    for copy in copies:
+        copy.start()
+    for copy in copies:
+        copy.wait()
+
+
 def ranks_of(owner_ref, count, peers):
     for d in range(peers):
         count[d] = 0
@@ -66,7 +74,8 @@
     return ranks
 
 
-def request_kernel(owner_ref, place_ref, out_ref, table, count):
+def request_kernel(owner_far, place_far, out_ref, owner_ref, place_ref, table, count, sems):
+    to_scalars((owner_far, place_far), (owner_ref, place_ref), sems)
     peers = out_ref.shape[0]
     for i in range((peers + 2) * CAP):
         table[i] = -1
@@ -79,25 +88,40 @@
         for g, side in enumerate(SIDES):
             for r in range(CAP):
                 line = jnp.where(lane == g * CAP + r, table[(peer + 1 + side) * CAP + r], line)
-        out_ref[peer] = line
+        out_ref[peer] = jnp.broadcast_to(line, (8, 128))
 
 
 def make_requests(owners, places, peers):
     return pl.pallas_call(
         request_kernel,
-        in_specs=[SCALARS, SCALARS],
+        in_specs=[FAR, FAR],
         out_specs=LOCAL,
-        out_shape=pltpu.VMEM((peers, 1, 128), jnp.int32),
-        scratch_shapes=[pltpu.SMEM(((peers + 2) * CAP,), jnp.int32), pltpu.SMEM((peers,), jnp.int32)],
+        out_shape=pltpu.VMEM((peers, 8, 128), jnp.int32),
+        scratch_shapes=[
+            pltpu.SMEM((TPD,), jnp.int32),
+            pltpu.SMEM((TPD,), jnp.int32),
+            pltpu.SMEM(((peers + 2) * CAP,), jnp.int32),
+            pltpu.SMEM((peers,), jnp.int32),
+            pltpu.SemaphoreType.DMA((2,)),
+        ],
         name="make_requests",
         compiler_params=params(4),
-    )(owners, places)
+    )(far(owners), far(places))
+
+
+def place_on(axis):
+    index = lax.axis_index(axis)
+    even = lax.rem(index, 2) == 0
+    return even, jnp.logical_or(index == 0, index == lax.axis_size(axis) - 1)
 
 
 def edge_kernel(
     after_ref, theta_ref, u_ref, v_ref,
-    block_ref, first_x_ref, last_x_ref, first_y_ref, last_y_ref, theta, sems, wind_sems,
+    block_ref, one_x_ref, two_x_ref, one_y_ref, two_y_ref, theta, sems, wind_sems,
 ):
+    even_x, wraps_x = place_on("gx")
+    even_y, wraps_y = place_on("gy")
+
     def copy(g):
         part = pl.ds(g * GROUP, GROUP)
         return pltpu.make_async_copy(theta_ref.at[part], theta.at[part], sems.at[g])
@@ -121,8 +145,9 @@
         for k in range(GROUP):
             z = g * GROUP + k
             cells = theta[z]
-            first_x_ref[pl.ds(z, 1)] = cells[0:1]
-            last_x_ref[pl.ds(z, 1)] = cells[CX - 1 : CX]
+            low, high = cells[0:1], cells[CX - 1 : CX]
+            one_x_ref[pl.ds(z, 1)] = jnp.where(even_x, high, low)
+            two_x_ref[pl.ds(z, 1)] = jnp.where(wraps_x, 0.0, jnp.where(even_x, low, high))
             turned = pltpu.roll(cells, k + 1, 1)
             first = jnp.where(lane == k + 1, turned, first)
             last = jnp.where(lane == k, turned, last)
@@ -136,8 +161,8 @@
         cells = block_ref[c * CX : (c + 1) * CX]
         first = jnp.where(lane == WIND + c, pltpu.roll(cells, WIND + c, 1), first)
         last = jnp.where(lane == WIND + c, pltpu.roll(cells, WIND + c + 1, 1), last)
-    first_y_ref[...] = first
-    last_y_ref[...] = last
+    one_y_ref[...] = jnp.where(even_y, last, first)
+    two_y_ref[...] = jnp.where(wraps_y, 0.0, jnp.where(even_y, first, last))
 
 
 def make_edges(after, theta, wind_u, wind_v):
@@ -160,23 +185,29 @@
 
 
 def cut_kernel(
-    asked_ref, block_ref, south_ref, north_ref, first_x_ref, last_x_ref,
-    out_ref, first_x_out, last_x_out, surface, edges,
+    asked_far, block_ref, one_y_ref, two_y_ref, one_x_ref, two_x_ref,
+    out_ref, one_x_out, two_x_out, surface, edges, asked_ref, sem,
 ):
-    first_x_out[...] = first_x_ref[...]
-    last_x_out[...] = last_x_ref[...]
+    copy = pltpu.make_async_copy(asked_far.at[:, 0:1], asked_ref, sem)
+    copy.start()
+    one_x_out[...] = one_x_ref[...]
+    two_x_out[...] = two_x_ref[...]
+    even, _ = place_on("gy")
+    south = jnp.where(even, two_y_ref[...], one_y_ref[...])
+    north = jnp.where(even, one_y_ref[...], two_y_ref[...])
     wide = iota(1, (CX, 128))
     lane = iota(1)
     blank = jnp.zeros((RIM, 128), F32)
     for c in range(2):
-        low = jnp.broadcast_to(south_ref[:, WIND + c : WIND + c + 1], (CX, 128))
-        high = jnp.broadcast_to(north_ref[:, WIND + c : WIND + c + 1], (CX, 128))
+        low = jnp.broadcast_to(south[:, WIND + c : WIND + c + 1], (CX, 128))
+        high = jnp.broadcast_to(north[:, WIND + c : WIND + c + 1], (CX, 128))
         surface[c, 0:RIM] = blank
         surface[c, RIM : RIM + CX] = block_ref[c * CX : (c + 1) * CX]
         surface[c, RIM + CX :] = blank
         edges[c, 0:RIM] = blank
         edges[c, RIM : RIM + CX] = jnp.where(wide % 8 == 0, low, high)
         edges[c, RIM + CX :] = blank
+    copy.wait()
     tiles_y = CY // TA
     for source in range(out_ref.shape[0]):
         message = jnp.zeros((8, 128), F32)
@@ -197,23 +228,29 @@
         out_ref[source] = message
 
 
-def cut_patches(asked, block, south, north, first_x, last_x):
+def cut_patches(asked, block, one_y, two_y, one_x, two_x):
     peers = asked.shape[0]
     row = pltpu.VMEM((LZ, 128), F32)
     rows = CX + 2 * RIM
     return pl.pallas_call(
         cut_kernel,
-        in_specs=[SCALARS] + [LOCAL] * 5,
+        in_specs=[LOCAL] * 6,
         out_specs=[LOCAL] * 3,
         out_shape=[pltpu.VMEM((peers, 8, 128), F32), row, row],
-        scratch_shapes=[pltpu.VMEM((2, rows, 128), F32), pltpu.VMEM((2, rows, 128), F32)],
+        scratch_shapes=[
+            pltpu.VMEM((2, rows, 128), F32),
+            pltpu.VMEM((2, rows, 128), F32),
+            pltpu.SMEM((peers, 1, 128), jnp.int32),
+            pltpu.SemaphoreType.DMA(()),
+        ],
         name="cut_patches",
         compiler_params=params(4),
-    )(asked, *(near(a) for a in (block, south, north, first_x, last_x)))
+    )(*(near(a) for a in (asked, block, one_y, two_y, one_x, two_x)))
 
 
 def advect_kernel(
-    theta_ref, u_ref, v_ref, west_ref, east_ref, south_ref, north_ref, out_ref, theta, wind_u, wind_v, sems
+    theta_ref, u_ref, v_ref, one_x_ref, two_x_ref, one_y_ref, two_y_ref,
+    out_ref, theta, wind_u, wind_v, west_ref, east_ref, sems,
 ):
     def copies(g):
         part = pl.ds(g * GROUP, GROUP)
@@ -226,6 +263,12 @@
     for g in range(GROUPS):
         for copy in copies(g):
             copy.start()
+    even, _ = place_on("gx")
+    west_ref[...] = jnp.where(even, two_x_ref[...], one_x_ref[...])
+    east_ref[...] = jnp.where(even, one_x_ref[...], two_x_ref[...])
+    even, _ = place_on("gy")
+    south = jnp.where(even, two_y_ref[...], one_y_ref[...])
+    north = jnp.where(even, one_y_ref[...], two_y_ref[...])
     lane = iota(1, (CX, 128))
     row = iota(0, (CX, 128))
 
@@ -260,7 +303,7 @@
             end(k, begun[k])
         return pltpu.roll(south_all, 128 - GROUP, 1), pltpu.roll(north_all, 128 - GROUP, 1)
 
-    lax.fori_loop(0, GROUPS, one, (south_ref[...], north_ref[...]))
+    lax.fori_loop(0, GROUPS, one, (south, north))
 
 
 def advect(theta, wind_u, wind_v, *rims):
@@ -270,7 +313,14 @@
         in_specs=[FAR] * 3 + [LOCAL] * 4,
         out_specs=LOCAL,
         out_shape=whole,
-        scratch_shapes=[whole, whole, whole, pltpu.SemaphoreType.DMA((3, GROUPS))],
+        scratch_shapes=[
+            whole,
+            whole,
+            whole,
+            pltpu.VMEM((LZ, 128), F32),
+            pltpu.VMEM((LZ, 128), F32),
+            pltpu.SemaphoreType.DMA((3, GROUPS)),
+        ],
         name="advect",
         compiler_params=params(12),
         cost_estimate=pl.CostEstimate(flops=14_000_000, bytes_accessed=8_000_000, transcendentals=0),
@@ -278,11 +328,11 @@
 
 
 def fire_kernel(
-    peers, waits, owner_ref, place_ref, winds_ref, level_ref, fuel_ref, base_ref, *rest
+    peers, waits, owner_far, place_far, winds_ref, level_ref, fuel_ref, base_ref, *rest
 ):
     (
         level_out, fuel_out, outbox, begins, slopes, heats,
-        level_own, fuel_own, base_own, count, in_sems, out_sems,
+        level_own, fuel_own, base_own, owner_ref, place_ref, count, scalar_sems, in_sems, out_sems,
     ) = rest[waits:]
     lane = iota(1)
     row = iota(0)
@@ -301,6 +351,7 @@
             for c, (source, target) in enumerate(pairs)
         ]
 
+    to_scalars((owner_far, place_far), (owner_ref, place_ref), scalar_sems)
     for t in range(TPD):
         for copy in inputs(t):
             copy.start()
@@ -409,7 +460,7 @@
     tiles = (TPD, S, S)
     return pl.pallas_call(
         functools.partial(fire_kernel, peers, len(waits)),
-        in_specs=[SCALARS, SCALARS, LOCAL] + [FAR] * 3 + [ANYWHERE] * len(waits),
+        in_specs=[FAR, FAR, LOCAL] + [FAR] * 3 + [ANYWHERE] * len(waits),
         out_specs=[ANYWHERE, ANYWHERE, LOCAL],
         out_shape=[
             jax.ShapeDtypeStruct(tiles, F32),
@@ -423,7 +474,10 @@
             pltpu.VMEM(tiles, F32),
             pltpu.VMEM(tiles, F32),
             pltpu.VMEM(tiles, F32),
+            pltpu.SMEM((TPD,), jnp.int32),
+            pltpu.SMEM((TPD,), jnp.int32),
             pltpu.SMEM((peers,), jnp.int32),
+            pltpu.SemaphoreType.DMA((2,)),
             pltpu.SemaphoreType.DMA((3, TPD)),
             pltpu.SemaphoreType.DMA((2, TPD)),
         ],
@@ -432,7 +486,7 @@
         cost_estimate=pl.CostEstimate(
             flops=50_000_000, bytes_accessed=6_500_000, transcendentals=3_200_000
         ),
-    )(owners, places, near(winds), *(far(a) for a in (level_set, fuel_load, spread_base)), *waits)
+    )(far(owners), far(places), near(winds), *(far(a) for a in (level_set, fuel_load, spread_base)), *waits)
 
 
 def final_kernel(inbox_ref, part_ref, out_ref, field, result, sems):
@@ -484,10 +538,11 @@
     )(near(inbox), near(part))
 
 
-def shifted(cells, axis, up):
-    ends = lax.axis_size(axis) - 1
-    pairs = [(i, i + 1) if up else (i + 1, i) for i in range(ends)]
-    return lax.ppermute(cells, axis, pairs)
+def swapped(one, two, axis):
+    count = lax.axis_size(axis)
+    pairs = [(i, i ^ 1) for i in range(count)]
+    others = [((i + 1) % count, ((i ^ 1) + 1) % count) for i in range(count)]
+    return lax.ppermute(one, axis, pairs), lax.ppermute(two, axis, others)
 
 
 def exchange(cells):
@@ -500,19 +555,17 @@
     requests = make_requests(owners, places, peers)
     asked = exchange(requests)
 
-    block, first_x, last_x, first_y, last_y = make_edges(requests, theta, wind_u, wind_v)
-    south = shifted(last_y, "gy", True)
-    north = shifted(first_y, "gy", False)
-
-    patches, first_x, last_x = cut_patches(asked, block, south, north, first_x, last_x)
+    block, one_x, two_x, one_y, two_y = make_edges(requests, theta, wind_u, wind_v)
+    rims_y = swapped(one_y, two_y, "gy")
+
+    patches, one_x, two_x = cut_patches(asked, block, *rims_y, one_x, two_x)
     winds = exchange(patches)
-    west = shifted(last_x, "gx", True)
-    east = shifted(first_x, "gx", False)
+    rims_x = swapped(one_x, two_x, "gx")
 
     level_out, fuel_out, outbox = fire(
-        owners, places, winds, level_set[0, 0], fuel_load[0, 0], spread_base[0, 0], peers, ()
+        owners, places, winds, level_set[0, 0], fuel_load[0, 0], spread_base[0, 0], peers, rims_x
     )
-    part = advect(theta, wind_u, wind_v, west, east, south, north)
+    part = advect(theta, wind_u, wind_v, *rims_x, *rims_y)
     inbox = exchange(outbox)
     theta_next = finish(inbox, part)
     return (theta_next, level_out[None, None], fuel_out[None, None])

time: 71.8 us -> 63.3 us (0.88)
  the two profiles are of different devices: /device:TPU:22 before, /device:TPU:0 now
where the time goes in v5:
time: 63.3 us; the launch traced here: 62.9 us
  starting transfers between devices  29.9 us (47%)
  Pallas kernels  24.3 us (38%)
  waiting for transfers between devices  7.92 us (13%)
  between operations  0.71 us (1%)
    all_to_all x3, starting transfers between devices, exchange(): return lax.all_to_all(cells, 'gx', split_axis=0, concat_axis=0, tiled=True)  20.6 us
    pallas_call x1, Pallas kernels, fire(): pl.pallas_call(functools.partial(fire_kernel, peers, len(waits)), in_spec...  11.3 us
    ppermute x4, starting transfers between devices, swapped(): return (lax.ppermute(one, axis, pairs), lax.ppermute(two, axis, others))  9.31 us
    pallas_call x1, Pallas kernels, advect(): pl.pallas_call(advect_kernel, in_specs=[FAR] * 3 + [LOCAL] * 4, out_specs...  4.94 us
    ppermute x4, waiting for transfers between devices, swapped(): return (lax.ppermute(one, axis, pairs), lax.ppermute(two, axis, others))  4.73 us
    all_to_all x3, waiting for transfers between devices, exchange(): return lax.all_to_all(cells, 'gx', split_axis=0, concat_axis=0, tiled=True)  3.19 us
    pallas_call x1, Pallas kernels, make_edges(): pl.pallas_call(edge_kernel, in_specs=[ANYWHERE, FAR, FAR, FAR], out_specs...  2.71 us
    pallas_call x1, Pallas kernels, cut_patches(): pl.pallas_call(cut_kernel, in_specs=[LOCAL] * 6, out_specs=[LOCAL] * 3, o...  2.06 us
  transfers between devices with their start and end apart: 7, of which 4 were waited for; matrix products, arithmetic and copies ran while one was open for 0% of the time, Pallas kernels for 12%

profile of v5, /device:TPU:0, one launch (start us, length us, event | category | flops | bytes accessed | tf_op | source)
XLA Modules:
  0.0 62.9 jit_solution(3163771427715678517)
XLA Ops:
  0.6 1.4 %make_requests.1.after_ref = s32[16,8,128]{2,1,0:T(8,128)} custom-call(s32[16]{0:T(128)} %bitcast.7, s32[16]{0:T(128)} %bitcast.9), custom_call_target="tpu_custom_call" | custom-call | tf_op jit(solution)/shard_map/make_requests/pallas_call | solution.py:95
  2.1 8.0 %all-to-all-start = ((s32[16,8,128]{2,1,0:T(8,128)}), s32[16,8,128]{2,1,0:T(8,128)S(1)}, u32[]{:S(2)}, u32[]{:S(2)}) async-start(s32[16,8,128]{2,1,0:T(8,128)} %make_requests.1.after_ref), calls=%async_computation | async-start | bytes 131072 | tf_op jit(solution)/shard_map/all_to_all | solution.py:549
  10.1 2.7 %edges.1 = (f32[128,128]{1,0:T(8,128)S(1)}, f32[80,128]{1,0:T(8,128)S(1)}, f32[80,128]{1,0:T(8,128)S(1)}, f32[64,128]{1,0:T(8,128)S(1)}, f32[64,128]{1,0:T(8,128)S(1)}) custom-call(s32[16,8,128]{2,1,0:T(8,128)} %make_requests.1.after_ref, f32[80,64,128]{2,1,0:T(8,128)} %theta_ref.3, f32[80,64,128]{2,1,0:T(8,128)} %u_ref.3, f32[80,64,128]{2,1,0:T(8,128)} %v_ref.3), custom_call_target="tpu_custom_call" | custom-call | flops 4000000 | bytes 2700000 | tf_op jit(solution)/shard_map/edges/pallas_call | solution.py:171
  12.8 0.1 collective-permute-start
  12.9 3.1 %collective-permute-start.1 = (f32[64,128]{1,0:T(8,128)S(1)}, f32[64,128]{1,0:T(8,128)S(1)}, u32[]{:S(2)}, u32[]{:S(2)}) collective-permute-start(f32[64,128]{1,0:T(8,128)S(1)} %get-tuple-element.16), channel_id=1, source_target_pairs={{1,2},{2,1},{3,4},{4,3},{5,6},{6,5},{7,0},{0,7},{9,10},{10,9},{11,... | collective-permute-start | bytes 98312 | tf_op jit(solution)/shard_map/ppermute | solution.py:545
  16.0 0.0 collective-permute-done.one_y_ref
  16.0 1.6 %collective-permute-done.1.two_y_ref = f32[64,128]{1,0:T(8,128)S(1)} collective-permute-done((f32[64,128]{1,0:T(8,128)S(1)}, f32[64,128]{1,0:T(8,128)S(1)}, u32[]{:S(2)}, u32[]{:S(2)}) %collective-permute-start.1) | collective-permute-done | bytes 32800 | tf_op jit(solution)/shard_map/ppermute | solution.py:545
  17.6 0.1 all-to-all-done.asked_far
  17.7 2.1 %cut_patches.1 = (f32[16,8,128]{2,1,0:T(8,128)}, f32[80,128]{1,0:T(8,128)S(1)}, f32[80,128]{1,0:T(8,128)S(1)}) custom-call(s32[16,8,128]{2,1,0:T(8,128)S(1)} %all-to-all-done.asked_far, f32[128,128]{1,0:T(8,128)S(1)} %get-tuple-element.14.block_ref, f32[64,128]{1,0:T(8,128)S(1)} %collective-permute-done.one_y_ref, ...), custom_call_target="tpu_custom_call" | custom-call | tf_op jit(solution)/shard_map/cut_patches/pallas_call | solution.py:235
  19.8 7.1 %all-to-all-start.1 = ((f32[16,8,128]{2,1,0:T(8,128)}), f32[16,8,128]{2,1,0:T(8,128)S(1)}, u32[]{:S(2)}, u32[]{:S(2)}) async-start(f32[16,8,128]{2,1,0:T(8,128)} %get-tuple-element.19), calls=%async_computation.1 | async-start | bytes 131072 | tf_op jit(solution)/shard_map/all_to_all | solution.py:549
  26.9 1.9 %collective-permute-start.2 = (f32[80,128]{1,0:T(8,128)S(1)}, f32[80,128]{1,0:T(8,128)S(1)}, u32[]{:S(2)}, u32[]{:S(2)}) collective-permute-start(f32[80,128]{1,0:T(8,128)S(1)} %get-tuple-element.20), channel_id=1, source_target_pairs={{0,8},{8,0},{16,24},{24,16},{32,40},{40,32},{48,56},{56,48},{64,72... | collective-permute-start | bytes 122888 | tf_op jit(solution)/shard_map/ppermute | solution.py:545
  28.8 4.2 %collective-permute-start.3 = (f32[80,128]{1,0:T(8,128)S(1)}, f32[80,128]{1,0:T(8,128)S(1)}, u32[]{:S(2)}, u32[]{:S(2)}) collective-permute-start(f32[80,128]{1,0:T(8,128)S(1)} %get-tuple-element.21), channel_id=1, source_target_pairs={{8,16},{16,8},{24,32},{32,24},{40,48},{48,40},{56,64},{64,56},{72,... | collective-permute-start | bytes 122888 | tf_op jit(solution)/shard_map/ppermute | solution.py:545
  33.0 0.0 collective-permute-done.2.rest_0_.one_x_ref
  33.0 3.1 %collective-permute-done.3.rest_1_.two_x_ref = f32[80,128]{1,0:T(8,128)S(1)} collective-permute-done((f32[80,128]{1,0:T(8,128)S(1)}, f32[80,128]{1,0:T(8,128)S(1)}, u32[]{:S(2)}, u32[]{:S(2)}) %collective-permute-start.3) | collective-permute-done | bytes 40992 | tf_op jit(solution)/shard_map/ppermute | solution.py:545
  36.1 0.0 all-to-all-done.1.winds_ref
  36.1 11.3 %fire.1 = (f32[16,128,128]{2,1,0:T(8,128)}, f32[16,128,128]{2,1,0:T(8,128)}, f32[32,8,128]{2,1,0:T(8,128)}) custom-call(s32[16]{0:T(128)} %bitcast.8, s32[16]{0:T(128)} %bitcast.10, f32[16,8,128]{2,1,0:T(8,128)S(1)} %all-to-all-done.1.winds_ref, f32[16,128,128]{2,1,0:T(8,128)} %bitcast.11, f32[16,128,128]{2,1,0:T(8,128)} %bitcast.12, ...), custom_call_target="tpu_custom_call" | custom-call | flops 50000000 | bytes 6500000 | tf_op jit(solution)/shard_map/fire/pallas_call | solution.py:461
  47.4 5.6 %all-to-all-start.2 = ((f32[32,8,128]{2,1,0:T(8,128)}), f32[32,8,128]{2,1,0:T(8,128)S(1)}, u32[]{:S(2)}, u32[]{:S(2)}) async-start(f32[32,8,128]{2,1,0:T(8,128)} %get-tuple-element.22), calls=%async_computation.2 | async-start | bytes 262144 | tf_op jit(solution)/shard_map/all_to_all | solution.py:549
  53.0 4.9 %advect.1.part_ref = f32[80,64,128]{2,1,0:T(8,128)S(1)} custom-call(f32[80,64,128]{2,1,0:T(8,128)} %theta_ref.3, f32[80,64,128]{2,1,0:T(8,128)} %u_ref.3, f32[80,64,128]{2,1,0:T(8,128)} %v_ref.3, f32[80,128]{1,0:T(8,128)S(1)} %collective-permute-done.2.rest_0_.one_x_ref, f32[80,128]{1,0:T(8,128)S(1)} %collective-permute-done.3.rest_1_.two_x_ref, ...), custom_call_target="tpu_custom_call" | custom-call | flops 14000000 | bytes 8000000 | tf_op jit(solution)/shard_map/advect/pallas_call | solution.py:311
  57.9 3.0 %all-to-all-done.2.inbox_ref = f32[32,8,128]{2,1,0:T(8,128)S(1)} async-done(((f32[32,8,128]{2,1,0:T(8,128)}), f32[32,8,128]{2,1,0:T(8,128)S(1)}, u32[]{:S(2)}, u32[]{:S(2)}) %all-to-all-start.2) | async-done | bytes 131104 | tf_op jit(solution)/shard_map/all_to_all | solution.py:549
  61.0 1.9 %finish.1 = f32[80,64,128]{2,1,0:T(8,128)} custom-call(f32[32,8,128]{2,1,0:T(8,128)S(1)} %all-to-all-done.2.inbox_ref, f32[80,64,128]{2,1,0:T(8,128)S(1)} %advect.1.part_ref), custom_call_target="tpu_custom_call" | custom-call | flops 3000000 | bytes 2700000 | tf_op jit(solution)/shard_map/finish/pallas_call | solution.py:525
Async XLA Ops:
  2.1 15.6 %all-to-all-start = ((s32[16,8,128]{2,1,0:T(8,128)}), s32[16,8,128]{2,1,0:T(8,128)S(1)}, u32[]{:S(2)}, u32[]{:S(2)}) async-start(s32[16,8,128]{2,1,0:T(8,128)} %make_requests.1.after_ref), calls=%async_computation | async-start | bytes 131072 | tf_op jit(solution)/shard_map/all_to_all | solution.py:549
  12.8 3.2 %collective-permute-start = (f32[64,128]{1,0:T(8,128)S(1)}, f32[64,128]{1,0:T(8,128)S(1)}, u32[]{:S(2)}, u32[]{:S(2)}) collective-permute-start(f32[64,128]{1,0:T(8,128)S(1)} %get-tuple-element.15), channel_id=1, source_target_pairs={{0,1},{1,0},{2,3},{3,2},{4,5},{5,4},{6,7},{7,6},{8,9},{9,8},{10,11... | collective-permute-start | bytes 98312 | tf_op jit(solution)/shard_map/ppermute | solution.py:545
  12.9 4.7 %collective-permute-start.1 = (f32[64,128]{1,0:T(8,128)S(1)}, f32[64,128]{1,0:T(8,128)S(1)}, u32[]{:S(2)}, u32[]{:S(2)}) collective-permute-start(f32[64,128]{1,0:T(8,128)S(1)} %get-tuple-element.16), channel_id=1, source_target_pairs={{1,2},{2,1},{3,4},{4,3},{5,6},{6,5},{7,0},{0,7},{9,10},{10,9},{11,... | collective-permute-start | bytes 98312 | tf_op jit(solution)/shard_map/ppermute | solution.py:545
  19.8 16.3 %all-to-all-start.1 = ((f32[16,8,128]{2,1,0:T(8,128)}), f32[16,8,128]{2,1,0:T(8,128)S(1)}, u32[]{:S(2)}, u32[]{:S(2)}) async-start(f32[16,8,128]{2,1,0:T(8,128)} %get-tuple-element.19), calls=%async_computation.1 | async-start | bytes 131072 | tf_op jit(solution)/shard_map/all_to_all | solution.py:549
  26.9 6.1 %collective-permute-start.2 = (f32[80,128]{1,0:T(8,128)S(1)}, f32[80,128]{1,0:T(8,128)S(1)}, u32[]{:S(2)}, u32[]{:S(2)}) collective-permute-start(f32[80,128]{1,0:T(8,128)S(1)} %get-tuple-element.20), channel_id=1, source_target_pairs={{0,8},{8,0},{16,24},{24,16},{32,40},{40,32},{48,56},{56,48},{64,72... | collective-permute-start | bytes 122888 | tf_op jit(solution)/shard_map/ppermute | solution.py:545
  28.8 7.3 %collective-permute-start.3 = (f32[80,128]{1,0:T(8,128)S(1)}, f32[80,128]{1,0:T(8,128)S(1)}, u32[]{:S(2)}, u32[]{:S(2)}) collective-permute-start(f32[80,128]{1,0:T(8,128)S(1)} %get-tuple-element.21), channel_id=1, source_target_pairs={{8,16},{16,8},{24,32},{32,24},{40,48},{48,40},{56,64},{64,56},{72,... | collective-permute-start | bytes 122888 | tf_op jit(solution)/shard_map/ppermute | solution.py:545
  47.4 13.6 %all-to-all-start.2 = ((f32[32,8,128]{2,1,0:T(8,128)}), f32[32,8,128]{2,1,0:T(8,128)S(1)}, u32[]{:S(2)}, u32[]{:S(2)}) async-start(f32[32,8,128]{2,1,0:T(8,128)} %get-tuple-element.22), calls=%async_computation.2 | async-start | bytes 262144 | tf_op jit(solution)/shard_map/all_to_all | solution.py:549

commit v6 on v5

--- a/solution.py
+++ b/solution.py
@@ -22,7 +22,7 @@
 WIND = 100
 GROUP = 8
 GROUPS = LZ // GROUP
-SIDE = 2
+SIDE = 4
 AHEAD = 2
 
 time_step = 0.03
@@ -337,24 +337,21 @@
     lane = iota(1)
     row = iota(0)
 
-    def inputs(t):
-        pairs = ((level_ref, level_own), (fuel_ref, fuel_own), (base_ref, base_own))
+    def bases(i):
+        some = pl.ds(i * SIDE, SIDE)
+        return pltpu.make_async_copy(base_ref.at[some], base_own.at[some], in_sems.at[i])
+
+    def results(i):
+        some = pl.ds(i * SIDE, SIDE)
+        pairs = ((level_own, level_out), (fuel_own, fuel_out))
         return [
-            pltpu.make_async_copy(source.at[t], target.at[t], in_sems.at[c, t])
+            pltpu.make_async_copy(source.at[some], target.at[some], out_sems.at[c, i])
             for c, (source, target) in enumerate(pairs)
         ]
 
-    def results(t):
-        pairs = ((level_own, level_out), (fuel_own, fuel_out))
-        return [
-            pltpu.make_async_copy(source.at[t], target.at[t], out_sems.at[c, t])
-            for c, (source, target) in enumerate(pairs)
-        ]
-
+    for i in range(TPD // SIDE):
+        bases(i).start()
     to_scalars((owner_far, place_far), (owner_ref, place_ref), scalar_sems)
-    for t in range(TPD):
-        for copy in inputs(t):
-            copy.start()
 
     tiles_y = CY // TA
     low_row = (row + 1) // 2
@@ -387,8 +384,8 @@
     def burn(t):
         begin = [begins[2 * t + c] for c in range(2)]
         slope = [slopes[2 * t + c] for c in range(2)]
-        level = [level_own[t, pl.ds(k, 8, stride=ROWS), :] for k in range(ROWS)]
-        fuel = [fuel_own[t, pl.ds(k, 8, stride=ROWS), :] for k in range(ROWS)]
+        level = [level_ref[t, pl.ds(k, 8, stride=ROWS), :] for k in range(ROWS)]
+        fuel = [fuel_ref[t, pl.ds(k, 8, stride=ROWS), :] for k in range(ROWS)]
         heat = sum(fuel[1:], fuel[0])
         rate = [base_own[t, pl.ds(k, 8, stride=ROWS), :] * (0.5 * time_step) for k in range(ROWS)]
         wind = [[begin[c] + slope[c] * float(k) for k in range(ROWS)] for c in range(2)]
@@ -411,9 +408,10 @@
                 move = jnp.maximum(length + (wind[0][k] * dx + wind[1][k] * dy), 0.0)
                 around = (east + west) + (north[k] + south[k])
                 cell = cell * (1.0 - 4.0 * diffusion) + around * diffusion - rate[k] * move
-                fuel[k] = fuel[k] * ((1.0 - 0.5 * burn_rate) + (0.5 * burn_rate) * jnp.tanh(cell))
+                fuel[k] = fuel[k] * (jnp.tanh(cell) + (2.0 / burn_rate - 1.0))
                 new.append(cell)
             level = new
+        fuel = [cell * (0.5 * burn_rate) ** KSUB for cell in fuel]
         yield
         for k in range(ROWS):
             level_own[t, pl.ds(k, 8, stride=ROWS), :] = level[k]
@@ -422,15 +420,12 @@
 
     def some(i, carry):
         tiles = [i * SIDE + j for j in range(SIDE)]
-        for t in tiles:
-            for copy in inputs(t):
-                copy.wait()
+        bases(i).wait()
         works = [burn(t) for t in tiles]
         while works:
             works = [w for w in works if next(w, works) is None]
-        for t in tiles:
-            for copy in results(t):
-                copy.start()
+        for copy in results(i):
+            copy.start()
         return carry
 
     lax.fori_loop(0, TPD // SIDE, some, 0)
@@ -451,8 +446,8 @@
         for b in range(TA):
             message = jnp.where(jnp.logical_and(row < TA, lane == y_own + b), sums[t][b], message)
         outbox[owner_ref[t] * CAP + ranks[t]] = message
-    for t in range(TPD):
-        for copy in results(t):
+    for i in range(TPD // SIDE):
+        for copy in results(i):
             copy.wait()
 
 
@@ -460,7 +455,7 @@
     tiles = (TPD, S, S)
     return pl.pallas_call(
         functools.partial(fire_kernel, peers, len(waits)),
-        in_specs=[FAR, FAR, LOCAL] + [FAR] * 3 + [ANYWHERE] * len(waits),
+        in_specs=[FAR, FAR] + [LOCAL] * 3 + [FAR] + [ANYWHERE] * len(waits),
         out_specs=[ANYWHERE, ANYWHERE, LOCAL],
         out_shape=[
             jax.ShapeDtypeStruct(tiles, F32),
@@ -478,15 +473,15 @@
             pltpu.SMEM((TPD,), jnp.int32),
             pltpu.SMEM((peers,), jnp.int32),
             pltpu.SemaphoreType.DMA((2,)),
-            pltpu.SemaphoreType.DMA((3, TPD)),
-            pltpu.SemaphoreType.DMA((2, TPD)),
+            pltpu.SemaphoreType.DMA((TPD // SIDE,)),
+            pltpu.SemaphoreType.DMA((2, TPD // SIDE)),
         ],
         name="fire",
         compiler_params=params(12),
         cost_estimate=pl.CostEstimate(
             flops=50_000_000, bytes_accessed=6_500_000, transcendentals=3_200_000
         ),
-    )(far(owners), far(places), near(winds), *(far(a) for a in (level_set, fuel_load, spread_base)), *waits)
+    )(far(owners), far(places), *(near(a) for a in (winds, level_set, fuel_load)), far(spread_base), *waits)
 
 
 def final_kernel(inbox_ref, part_ref, out_ref, field, result, sems):
@@ -541,7 +536,7 @@
 def swapped(one, two, axis):
     count = lax.axis_size(axis)
     pairs = [(i, i ^ 1) for i in range(count)]
-    others = [((i + 1) % count, ((i ^ 1) + 1) % count) for i in range(count)]
+    others = [(i + 1, (i ^ 1) + 1) for i in range(count - 2)] + [(0, 0), (count - 1, count - 1)]
     return lax.ppermute(one, axis, pairs), lax.ppermute(two, axis, others)
 
 

time: 63.3 us -> 63 us (level)
  the two profiles are of different devices: /device:TPU:0 before, /device:TPU:16 now
where the time goes in v6:
time: 63 us; the launch traced here: 62.7 us
  starting transfers between devices  28.1 us (45%)
  Pallas kernels  22.7 us (36%)
  waiting for transfers between devices  11.2 us (18%)
  between operations  0.74 us (1%)
    all_to_all x3, starting transfers between devices, exchange(): return lax.all_to_all(cells, 'gx', split_axis=0, concat_axis=0, tiled=True)  22.9 us
    pallas_call x1, Pallas kernels, fire(): pl.pallas_call(functools.partial(fire_kernel, peers, len(waits)), in_spec...  9.46 us
    all_to_all x3, waiting for transfers between devices, exchange(): return lax.all_to_all(cells, 'gx', split_axis=0, concat_axis=0, tiled=True)  6.54 us
    ppermute x4, starting transfers between devices, swapped(): return (lax.ppermute(one, axis, pairs), lax.ppermute(two, axis, others))  5.14 us
    pallas_call x1, Pallas kernels, advect(): pl.pallas_call(advect_kernel, in_specs=[FAR] * 3 + [LOCAL] * 4, out_specs...  4.94 us
    ppermute x4, waiting for transfers between devices, swapped(): return (lax.ppermute(one, axis, pairs), lax.ppermute(two, axis, others))  4.64 us
    pallas_call x1, Pallas kernels, make_edges(): pl.pallas_call(edge_kernel, in_specs=[ANYWHERE, FAR, FAR, FAR], out_specs...  2.85 us
    pallas_call x1, Pallas kernels, cut_patches(): pl.pallas_call(cut_kernel, in_specs=[LOCAL] * 6, out_specs=[LOCAL] * 3, o...  2.06 us
  transfers between devices with their start and end apart: 7, of which 4 were waited for; matrix products, arithmetic and copies ran while one was open for 0% of the time, Pallas kernels for 12%

profile of v6, /device:TPU:16, one launch (start us, length us, event | category | flops | bytes accessed | tf_op | source)
XLA Modules:
  0.0 62.7 jit_solution(17072164497926025959)
XLA Ops:
  0.6 1.4 %make_requests.1.after_ref = s32[16,8,128]{2,1,0:T(8,128)} custom-call(s32[16]{0:T(128)} %bitcast.9, s32[16]{0:T(128)} %bitcast.11), custom_call_target="tpu_custom_call" | custom-call | tf_op jit(solution)/shard_map/make_requests/pallas_call | solution.py:95
  2.1 7.9 %all-to-all-start = ((s32[16,8,128]{2,1,0:T(8,128)}), s32[16,8,128]{2,1,0:T(8,128)S(1)}, u32[]{:S(2)}, u32[]{:S(2)}) async-start(s32[16,8,128]{2,1,0:T(8,128)} %make_requests.1.after_ref), calls=%async_computation | async-start | bytes 131072 | tf_op jit(solution)/shard_map/all_to_all | solution.py:544
  10.0 0.0 copy-start
  10.0 0.0 copy-start.1
  10.0 2.9 %edges.1 = (f32[128,128]{1,0:T(8,128)S(1)}, f32[80,128]{1,0:T(8,128)S(1)}, f32[80,128]{1,0:T(8,128)S(1)}, f32[64,128]{1,0:T(8,128)S(1)}, f32[64,128]{1,0:T(8,128)S(1)}) custom-call(s32[16,8,128]{2,1,0:T(8,128)} %make_requests.1.after_ref, f32[80,64,128]{2,1,0:T(8,128)} %theta_ref.3, f32[80,64,128]{2,1,0:T(8,128)} %u_ref.3, f32[80,64,128]{2,1,0:T(8,128)} %v_ref.3), custom_call_target="tpu_custom_call" | custom-call | flops 4000000 | bytes 2700000 | tf_op jit(solution)/shard_map/edges/pallas_call | solution.py:171
  12.9 0.1 collective-permute-start
  12.9 2.4 %collective-permute-start.1 = (f32[64,128]{1,0:T(8,128)S(1)}, f32[64,128]{1,0:T(8,128)S(1)}, u32[]{:S(2)}, u32[]{:S(2)}) collective-permute-start(f32[64,128]{1,0:T(8,128)S(1)} %get-tuple-element.16), channel_id=1, source_target_pairs={{1,2},{2,1},{3,4},{4,3},{5,6},{6,5},{0,0},{7,7},{9,10},{10,9},{11,... | collective-permute-start | bytes 98312 | tf_op jit(solution)/shard_map/ppermute | solution.py:540
  15.4 0.0 collective-permute-done.one_y_ref
  15.4 2.8 %collective-permute-done.1.two_y_ref = f32[64,128]{1,0:T(8,128)S(1)} collective-permute-done((f32[64,128]{1,0:T(8,128)S(1)}, f32[64,128]{1,0:T(8,128)S(1)}, u32[]{:S(2)}, u32[]{:S(2)}) %collective-permute-start.1) | collective-permute-done | bytes 32800 | tf_op jit(solution)/shard_map/ppermute | solution.py:540
  18.2 0.0 all-to-all-done.asked_far
  18.2 2.1 %cut_patches.1 = (f32[16,8,128]{2,1,0:T(8,128)}, f32[80,128]{1,0:T(8,128)S(1)}, f32[80,128]{1,0:T(8,128)S(1)}) custom-call(s32[16,8,128]{2,1,0:T(8,128)S(1)} %all-to-all-done.asked_far, f32[128,128]{1,0:T(8,128)S(1)} %get-tuple-element.14.block_ref, f32[64,128]{1,0:T(8,128)S(1)} %collective-permute-done.one_y_ref, ...), custom_call_target="tpu_custom_call" | custom-call | tf_op jit(solution)/shard_map/cut_patches/pallas_call | solution.py:235
  20.3 7.2 %all-to-all-start.1 = ((f32[16,8,128]{2,1,0:T(8,128)}), f32[16,8,128]{2,1,0:T(8,128)S(1)}, u32[]{:S(2)}, u32[]{:S(2)}) async-start(f32[16,8,128]{2,1,0:T(8,128)} %get-tuple-element.19), calls=%async_computation.1 | async-start | bytes 131072 | tf_op jit(solution)/shard_map/all_to_all | solution.py:544
  27.5 2.0 %collective-permute-start.2 = (f32[80,128]{1,0:T(8,128)S(1)}, f32[80,128]{1,0:T(8,128)S(1)}, u32[]{:S(2)}, u32[]{:S(2)}) collective-permute-start(f32[80,128]{1,0:T(8,128)S(1)} %get-tuple-element.20), channel_id=1, source_target_pairs={{0,8},{8,0},{16,24},{24,16},{32,40},{40,32},{48,56},{56,48},{64,72... | collective-permute-start | bytes 122888 | tf_op jit(solution)/shard_map/ppermute | solution.py:540
  29.4 0.7 %collective-permute-start.3 = (f32[80,128]{1,0:T(8,128)S(1)}, f32[80,128]{1,0:T(8,128)S(1)}, u32[]{:S(2)}, u32[]{:S(2)}) collective-permute-start(f32[80,128]{1,0:T(8,128)S(1)} %get-tuple-element.21), channel_id=1, source_target_pairs={{8,16},{16,8},{24,32},{32,24},{40,48},{48,40},{56,64},{64,56},{72,... | collective-permute-start | bytes 122888 | tf_op jit(solution)/shard_map/ppermute | solution.py:540
  30.1 1.9 %collective-permute-done.2.rest_0_.one_x_ref = f32[80,128]{1,0:T(8,128)S(1)} collective-permute-done((f32[80,128]{1,0:T(8,128)S(1)}, f32[80,128]{1,0:T(8,128)S(1)}, u32[]{:S(2)}, u32[]{:S(2)}) %collective-permute-start.2) | collective-permute-done | bytes 40992 | tf_op jit(solution)/shard_map/ppermute | solution.py:540
  32.0 0.0 collective-permute-done.3.rest_1_.two_x_ref
  32.0 3.5 %all-to-all-done.1.winds_ref = f32[16,8,128]{2,1,0:T(8,128)S(1)} async-done(((f32[16,8,128]{2,1,0:T(8,128)}), f32[16,8,128]{2,1,0:T(8,128)S(1)}, u32[]{:S(2)}, u32[]{:S(2)}) %all-to-all-start.1) | async-done | bytes 65568 | tf_op jit(solution)/shard_map/all_to_all | solution.py:544
  35.5 0.0 copy-done
  35.5 0.0 copy-done.1
  35.5 9.5 %fire.1 = (f32[16,128,128]{2,1,0:T(8,128)}, f32[16,128,128]{2,1,0:T(8,128)}, f32[32,8,128]{2,1,0:T(8,128)}) custom-call(s32[16]{0:T(128)} %bitcast.10, s32[16]{0:T(128)} %bitcast.12, f32[16,8,128]{2,1,0:T(8,128)S(1)} %all-to-all-done.1.winds_ref, f32[16,128,128]{2,1,0:T(8,128)S(1)} %bitcast.7, f32[16,128,128]{2,1,0:T(8,128)S(1)} %bitcast.8, ...), custom_call_target="tpu_custom_call" | custom-call | flops 50000000 | bytes 6500000 | tf_op jit(solution)/shard_map/fire/pallas_call | solution.py:456
  44.9 7.8 %all-to-all-start.2 = ((f32[32,8,128]{2,1,0:T(8,128)}), f32[32,8,128]{2,1,0:T(8,128)S(1)}, u32[]{:S(2)}, u32[]{:S(2)}) async-start(f32[32,8,128]{2,1,0:T(8,128)} %get-tuple-element.22), calls=%async_computation.2 | async-start | bytes 262144 | tf_op jit(solution)/shard_map/all_to_all | solution.py:544
  52.8 4.9 %advect.1.part_ref = f32[80,64,128]{2,1,0:T(8,128)S(1)} custom-call(f32[80,64,128]{2,1,0:T(8,128)} %theta_ref.3, f32[80,64,128]{2,1,0:T(8,128)} %u_ref.3, f32[80,64,128]{2,1,0:T(8,128)} %v_ref.3, f32[80,128]{1,0:T(8,128)S(1)} %collective-permute-done.2.rest_0_.one_x_ref, f32[80,128]{1,0:T(8,128)S(1)} %collective-permute-done.3.rest_1_.two_x_ref, ...), custom_call_target="tpu_custom_call" | custom-call | flops 14000000 | bytes 8000000 | tf_op jit(solution)/shard_map/advect/pallas_call | solution.py:311
  57.7 3.0 %all-to-all-done.2.inbox_ref = f32[32,8,128]{2,1,0:T(8,128)S(1)} async-done(((f32[32,8,128]{2,1,0:T(8,128)}), f32[32,8,128]{2,1,0:T(8,128)S(1)}, u32[]{:S(2)}, u32[]{:S(2)}) %all-to-all-start.2) | async-done | bytes 131104 | tf_op jit(solution)/shard_map/all_to_all | solution.py:544
  60.8 1.9 %finish.1 = f32[80,64,128]{2,1,0:T(8,128)} custom-call(f32[32,8,128]{2,1,0:T(8,128)S(1)} %all-to-all-done.2.inbox_ref, f32[80,64,128]{2,1,0:T(8,128)S(1)} %advect.1.part_ref), custom_call_target="tpu_custom_call" | custom-call | flops 3000000 | bytes 2700000 | tf_op jit(solution)/shard_map/finish/pallas_call | solution.py:520
Async XLA Ops:
  2.1 16.1 %all-to-all-start = ((s32[16,8,128]{2,1,0:T(8,128)}), s32[16,8,128]{2,1,0:T(8,128)S(1)}, u32[]{:S(2)}, u32[]{:S(2)}) async-start(s32[16,8,128]{2,1,0:T(8,128)} %make_requests.1.after_ref), calls=%async_computation | async-start | bytes 131072 | tf_op jit(solution)/shard_map/all_to_all | solution.py:544
  10.0 25.5 %copy-start = (f32[1,1,16,128,128]{4,3,2,1,0:T(8,128)S(1)}, f32[1,1,16,128,128]{4,3,2,1,0:T(8,128)}, u32[]{:S(2)}) copy-start(f32[1,1,16,128,128]{4,3,2,1,0:T(8,128)} %param.11) | copy-start | bytes 3145732
  10.0 25.5 %copy-start.1 = (f32[1,1,16,128,128]{4,3,2,1,0:T(8,128)S(1)}, f32[1,1,16,128,128]{4,3,2,1,0:T(8,128)}, u32[]{:S(2)}) copy-start(f32[1,1,16,128,128]{4,3,2,1,0:T(8,128)} %param.12) | copy-start | bytes 3145732
  12.9 2.6 %collective-permute-start = (f32[64,128]{1,0:T(8,128)S(1)}, f32[64,128]{1,0:T(8,128)S(1)}, u32[]{:S(2)}, u32[]{:S(2)}) collective-permute-start(f32[64,128]{1,0:T(8,128)S(1)} %get-tuple-element.15), channel_id=1, source_target_pairs={{0,1},{1,0},{2,3},{3,2},{4,5},{5,4},{6,7},{7,6},{8,9},{9,8},{10,11... | collective-permute-start | bytes 98312 | tf_op jit(solution)/shard_map/ppermute | solution.py:540
  12.9 5.2 %collective-permute-start.1 = (f32[64,128]{1,0:T(8,128)S(1)}, f32[64,128]{1,0:T(8,128)S(1)}, u32[]{:S(2)}, u32[]{:S(2)}) collective-permute-start(f32[64,128]{1,0:T(8,128)S(1)} %get-tuple-element.16), channel_id=1, source_target_pairs={{1,2},{2,1},{3,4},{4,3},{5,6},{6,5},{0,0},{7,7},{9,10},{10,9},{11,... | collective-permute-start | bytes 98312 | tf_op jit(solution)/shard_map/ppermute | solution.py:540
  20.3 15.2 %all-to-all-start.1 = ((f32[16,8,128]{2,1,0:T(8,128)}), f32[16,8,128]{2,1,0:T(8,128)S(1)}, u32[]{:S(2)}, u32[]{:S(2)}) async-start(f32[16,8,128]{2,1,0:T(8,128)} %get-tuple-element.19), calls=%async_computation.1 | async-start | bytes 131072 | tf_op jit(solution)/shard_map/all_to_all | solution.py:544
  27.5 4.5 %collective-permute-start.2 = (f32[80,128]{1,0:T(8,128)S(1)}, f32[80,128]{1,0:T(8,128)S(1)}, u32[]{:S(2)}, u32[]{:S(2)}) collective-permute-start(f32[80,128]{1,0:T(8,128)S(1)} %get-tuple-element.20), channel_id=1, source_target_pairs={{0,8},{8,0},{16,24},{24,16},{32,40},{40,32},{48,56},{56,48},{64,72... | collective-permute-start | bytes 122888 | tf_op jit(solution)/shard_map/ppermute | solution.py:540
  29.4 2.5 %collective-permute-start.3 = (f32[80,128]{1,0:T(8,128)S(1)}, f32[80,128]{1,0:T(8,128)S(1)}, u32[]{:S(2)}, u32[]{:S(2)}) collective-permute-start(f32[80,128]{1,0:T(8,128)S(1)} %get-tuple-element.21), channel_id=1, source_target_pairs={{8,16},{16,8},{24,32},{32,24},{40,48},{48,40},{56,64},{64,56},{72,... | collective-permute-start | bytes 122888 | tf_op jit(solution)/shard_map/ppermute | solution.py:540
  44.9 15.8 %all-to-all-start.2 = ((f32[32,8,128]{2,1,0:T(8,128)}), f32[32,8,128]{2,1,0:T(8,128)S(1)}, u32[]{:S(2)}, u32[]{:S(2)}) async-start(f32[32,8,128]{2,1,0:T(8,128)} %get-tuple-element.22), calls=%async_computation.2 | async-start | bytes 262144 | tf_op jit(solution)/shard_map/all_to_all | solution.py:544

commit v7 on v6

--- a/solution.py
+++ b/solution.py
@@ -249,8 +249,8 @@
 
 
 def advect_kernel(
-    theta_ref, u_ref, v_ref, one_x_ref, two_x_ref, one_y_ref, two_y_ref,
-    out_ref, theta, wind_u, wind_v, west_ref, east_ref, sems,
+    theta_ref, u_ref, v_ref, west_ref, east_ref, one_y_ref, two_y_ref,
+    out_ref, theta, wind_u, wind_v, sems,
 ):
     def copies(g):
         part = pl.ds(g * GROUP, GROUP)
@@ -263,9 +263,6 @@
     for g in range(GROUPS):
         for copy in copies(g):
             copy.start()
-    even, _ = place_on("gx")
-    west_ref[...] = jnp.where(even, two_x_ref[...], one_x_ref[...])
-    east_ref[...] = jnp.where(even, one_x_ref[...], two_x_ref[...])
     even, _ = place_on("gy")
     south = jnp.where(even, two_y_ref[...], one_y_ref[...])
     north = jnp.where(even, one_y_ref[...], two_y_ref[...])
@@ -317,8 +314,6 @@
             whole,
             whole,
             whole,
-            pltpu.VMEM((LZ, 128), F32),
-            pltpu.VMEM((LZ, 128), F32),
             pltpu.SemaphoreType.DMA((3, GROUPS)),
         ],
         name="advect",
@@ -430,8 +425,8 @@
 
     lax.fori_loop(0, TPD // SIDE, some, 0)
 
-    for d in range(peers * CAP):
-        outbox[d] = jnp.where(row < TA, 0.0, -1.0)
+    for d in range(peers):
+        outbox[d] = jnp.where(lane < TA, 0.0, -1.0)
     pairs = [heats[t] for t in range(TPD)]
     pairs = [h + pltpu.roll(h, 7, 0) for h in pairs]
     pairs = [jnp.take_along_axis(h, jnp.minimum(2 * row, 7), axis=0) for h in pairs]
@@ -442,10 +437,10 @@
         place = place_ref[t]
         x_own = place // tiles_y * TA
         y_own = lax.rem(place, tiles_y) * TA
-        message = jnp.where(row < TA, 0.0, (x_own + row - TA).astype(F32))
+        message = jnp.where(lane == TA, (x_own + row).astype(F32), y_own.astype(F32))
         for b in range(TA):
-            message = jnp.where(jnp.logical_and(row < TA, lane == y_own + b), sums[t][b], message)
-        outbox[owner_ref[t] * CAP + ranks[t]] = message
+            message = jnp.where(lane == b, sums[t][b], message)
+        outbox[owner_ref[t], pl.ds(ranks[t] * TA, TA), :] = message[0:TA]
     for i in range(TPD // SIDE):
         for copy in results(i):
             copy.wait()
@@ -460,7 +455,7 @@
         out_shape=[
             jax.ShapeDtypeStruct(tiles, F32),
             jax.ShapeDtypeStruct(tiles, F32),
-            pltpu.VMEM((peers * CAP, 8, 128), F32),
+            pltpu.VMEM((peers, 8, 128), F32),
         ],
         scratch_shapes=[
             pltpu.VMEM((2 * TPD, 8, 128), F32),
@@ -484,16 +479,37 @@
     )(far(owners), far(places), *(near(a) for a in (winds, level_set, fuel_load)), far(spread_base), *waits)
 
 
+def row_kernel(outbox_ref, one_x_ref, two_x_ref, outbox_out, west_ref, east_ref):
+    outbox_out[...] = outbox_ref[...]
+    even, _ = place_on("gx")
+    west_ref[...] = jnp.where(even, two_x_ref[...], one_x_ref[...])
+    east_ref[...] = jnp.where(even, one_x_ref[...], two_x_ref[...])
+
+
+def sort_rows(outbox, one_x, two_x):
+    row = pltpu.VMEM((LZ, 128), F32)
+    return pl.pallas_call(
+        row_kernel,
+        in_specs=[LOCAL] * 3,
+        out_specs=[LOCAL] * 3,
+        out_shape=[pltpu.VMEM(outbox.shape, F32), row, row],
+        name="sort_rows",
+        compiler_params=params(4),
+    )(near(outbox), near(one_x), near(two_x))
+
+
 def final_kernel(inbox_ref, part_ref, out_ref, field, result, sems):
     inbox = inbox_ref[...]
-    slots = inbox.shape[0]
-    position = pltpu.roll(inbox, TA, 1).reshape(slots * 8, 128)
-    values = inbox.reshape(slots * 8, 128)
-    lane = iota(1, (slots * 8, 128)).astype(F32)
-    valid = iota(0, (slots * 8, 128)) % 8 < TA
-    hot = jnp.where(jnp.logical_and(valid, lane == position), 1.0, 0.0)
+    rows = inbox.shape[0] * 8
+    values = inbox.reshape(rows, 128)
+    lane = iota(1, (rows, 128)).astype(F32)
+    hot = jnp.where(lane == values[:, TA : TA + 1], 1.0, 0.0)
+    y_own = values[:, TA + 1 : TA + 2]
+    spread = jnp.zeros((rows, 128), F32)
+    for b in range(TA):
+        spread = jnp.where(lane == y_own + float(b), values[:, b : b + 1], spread)
     total = lax.dot_general(
-        hot, values, (((0,), (0,)), ((), ())),
+        hot, spread, (((0,), (0,)), ((), ())),
         precision=lax.Precision.HIGHEST, preferred_element_type=F32,
     )
     field[...] = total[:CX]
@@ -536,7 +552,7 @@
 def swapped(one, two, axis):
     count = lax.axis_size(axis)
     pairs = [(i, i ^ 1) for i in range(count)]
-    others = [(i + 1, (i ^ 1) + 1) for i in range(count - 2)] + [(0, 0), (count - 1, count - 1)]
+    others = [((i + 1) % count, ((i ^ 1) + 1) % count) for i in range(count)]
     return lax.ppermute(one, axis, pairs), lax.ppermute(two, axis, others)
 
 
@@ -558,9 +574,10 @@
     rims_x = swapped(one_x, two_x, "gx")
 
     level_out, fuel_out, outbox = fire(
-        owners, places, winds, level_set[0, 0], fuel_load[0, 0], spread_base[0, 0], peers, rims_x
+        owners, places, winds, level_set[0, 0], fuel_load[0, 0], spread_base[0, 0], peers, ()
     )
-    part = advect(theta, wind_u, wind_v, *rims_x, *rims_y)
+    outbox, west, east = sort_rows(outbox, *rims_x)
+    part = advect(theta, wind_u, wind_v, west, east, *rims_y)
     inbox = exchange(outbox)
     theta_next = finish(inbox, part)
     return (theta_next, level_out[None, None], fuel_out[None, None])

time: 63 us -> 57.8 us (0.917)
  the two profiles are of different devices: /device:TPU:16 before, /device:TPU:0 now
where the time goes in v7:
time: 57.8 us; the launch traced here: 57.4 us
  starting transfers between devices  28 us (48%)
  Pallas kernels  22.8 us (39%)
  waiting for transfers between devices  5.85 us (10%)
  between operations  0.74 us (1%)
    all_to_all x3, starting transfers between devices, exchange(): return lax.all_to_all(cells, 'gx', split_axis=0, concat_axis=0, tiled=True)  18.7 us
    ppermute x4, starting transfers between devices, swapped(): return (lax.ppermute(one, axis, pairs), lax.ppermute(two, axis, others))  9.31 us
    pallas_call x1, Pallas kernels, fire(): pl.pallas_call(functools.partial(fire_kernel, peers, len(waits)), in_spec...  8.8 us
    pallas_call x1, Pallas kernels, advect(): pl.pallas_call(advect_kernel, in_specs=[FAR] * 3 + [LOCAL] * 4, out_specs...  4.93 us
    all_to_all x3, waiting for transfers between devices, exchange(): return lax.all_to_all(cells, 'gx', split_axis=0, concat_axis=0, tiled=True)  4.25 us
    pallas_call x1, Pallas kernels, make_edges(): pl.pallas_call(edge_kernel, in_specs=[ANYWHERE, FAR, FAR, FAR], out_specs...  2.85 us
    pallas_call x1, Pallas kernels, finish(): pl.pallas_call(final_kernel, in_specs=[LOCAL, LOCAL], out_specs=ANYWHERE,...  2.08 us
    pallas_call x1, Pallas kernels, cut_patches(): pl.pallas_call(cut_kernel, in_specs=[LOCAL] * 6, out_specs=[LOCAL] * 3, o...  2.06 us
  transfers between devices with their start and end apart: 7, of which 3 were waited for; matrix products, arithmetic and copies ran while one was open for 0% of the time, Pallas kernels for 29%

profile of v7, /device:TPU:0, one launch (start us, length us, event | category | flops | bytes accessed | tf_op | source)
XLA Modules:
  0.0 57.4 jit_solution(13621789475240034303)
XLA Ops:
  0.6 1.4 %make_requests.1.after_ref = s32[16,8,128]{2,1,0:T(8,128)} custom-call(s32[16]{0:T(128)} %bitcast.9, s32[16]{0:T(128)} %bitcast.11), custom_call_target="tpu_custom_call" | custom-call | tf_op jit(solution)/shard_map/make_requests/pallas_call | solution.py:95
  2.1 8.0 %all-to-all-start = ((s32[16,8,128]{2,1,0:T(8,128)}), s32[16,8,128]{2,1,0:T(8,128)S(1)}, u32[]{:S(2)}, u32[]{:S(2)}) async-start(s32[16,8,128]{2,1,0:T(8,128)} %make_requests.1.after_ref), calls=%async_computation | async-start | bytes 131072 | tf_op jit(solution)/shard_map/all_to_all | solution.py:560
  10.1 0.0 copy-start
  10.1 0.0 copy-start.1
  10.1 2.9 %edges.1 = (f32[128,128]{1,0:T(8,128)S(1)}, f32[80,128]{1,0:T(8,128)S(1)}, f32[80,128]{1,0:T(8,128)S(1)}, f32[64,128]{1,0:T(8,128)S(1)}, f32[64,128]{1,0:T(8,128)S(1)}) custom-call(s32[16,8,128]{2,1,0:T(8,128)} %make_requests.1.after_ref, f32[80,64,128]{2,1,0:T(8,128)} %theta_ref.3, f32[80,64,128]{2,1,0:T(8,128)} %u_ref.3, f32[80,64,128]{2,1,0:T(8,128)} %v_ref.3), custom_call_target="tpu_custom_call" | custom-call | flops 4000000 | bytes 2700000 | tf_op jit(solution)/shard_map/edges/pallas_call | solution.py:171
  12.9 0.1 collective-permute-start
  13.0 3.1 %collective-permute-start.1 = (f32[64,128]{1,0:T(8,128)S(1)}, f32[64,128]{1,0:T(8,128)S(1)}, u32[]{:S(2)}, u32[]{:S(2)}) collective-permute-start(f32[64,128]{1,0:T(8,128)S(1)} %get-tuple-element.19), channel_id=1, source_target_pairs={{1,2},{2,1},{3,4},{4,3},{5,6},{6,5},{7,0},{0,7},{9,10},{10,9},{11,... | collective-permute-start | bytes 98312 | tf_op jit(solution)/shard_map/ppermute | solution.py:556
  16.1 0.0 collective-permute-done.one_y_ref
  16.2 1.6 %collective-permute-done.1.two_y_ref = f32[64,128]{1,0:T(8,128)S(1)} collective-permute-done((f32[64,128]{1,0:T(8,128)S(1)}, f32[64,128]{1,0:T(8,128)S(1)}, u32[]{:S(2)}, u32[]{:S(2)}) %collective-permute-start.1) | collective-permute-done | bytes 32800 | tf_op jit(solution)/shard_map/ppermute | solution.py:556
  17.7 0.0 all-to-all-done.asked_far
  17.8 2.1 %cut_patches.1 = (f32[16,8,128]{2,1,0:T(8,128)}, f32[80,128]{1,0:T(8,128)S(1)}, f32[80,128]{1,0:T(8,128)S(1)}) custom-call(s32[16,8,128]{2,1,0:T(8,128)S(1)} %all-to-all-done.asked_far, f32[128,128]{1,0:T(8,128)S(1)} %get-tuple-element.17.block_ref, f32[64,128]{1,0:T(8,128)S(1)} %collective-permute-done.one_y_ref, ...), custom_call_target="tpu_custom_call" | custom-call | tf_op jit(solution)/shard_map/cut_patches/pallas_call | solution.py:235
  19.8 7.2 %all-to-all-start.1 = ((f32[16,8,128]{2,1,0:T(8,128)}), f32[16,8,128]{2,1,0:T(8,128)S(1)}, u32[]{:S(2)}, u32[]{:S(2)}) async-start(f32[16,8,128]{2,1,0:T(8,128)} %get-tuple-element.22), calls=%async_computation.1 | async-start | bytes 131072 | tf_op jit(solution)/shard_map/all_to_all | solution.py:560
  27.1 1.9 %collective-permute-start.2 = (f32[80,128]{1,0:T(8,128)S(1)}, f32[80,128]{1,0:T(8,128)S(1)}, u32[]{:S(2)}, u32[]{:S(2)}) collective-permute-start(f32[80,128]{1,0:T(8,128)S(1)} %get-tuple-element.24), channel_id=1, source_target_pairs={{0,8},{8,0},{16,24},{24,16},{32,40},{40,32},{48,56},{56,48},{64,72... | collective-permute-start | bytes 122888 | tf_op jit(solution)/shard_map/ppermute | solution.py:556
  29.0 4.2 %collective-permute-start.3 = (f32[80,128]{1,0:T(8,128)S(1)}, f32[80,128]{1,0:T(8,128)S(1)}, u32[]{:S(2)}, u32[]{:S(2)}) collective-permute-start(f32[80,128]{1,0:T(8,128)S(1)} %get-tuple-element.25), channel_id=1, source_target_pairs={{8,16},{16,8},{24,32},{32,24},{40,48},{48,40},{56,64},{64,56},{72,... | collective-permute-start | bytes 122888 | tf_op jit(solution)/shard_map/ppermute | solution.py:556
  33.2 1.6 %all-to-all-done.1.winds_ref = f32[16,8,128]{2,1,0:T(8,128)S(1)} async-done(((f32[16,8,128]{2,1,0:T(8,128)}), f32[16,8,128]{2,1,0:T(8,128)S(1)}, u32[]{:S(2)}, u32[]{:S(2)}) %all-to-all-start.1) | async-done | bytes 65568 | tf_op jit(solution)/shard_map/all_to_all | solution.py:560
  34.7 0.0 copy-done
  34.7 0.0 copy-done.1
  34.7 8.8 %fire.1 = (f32[16,128,128]{2,1,0:T(8,128)}, f32[16,128,128]{2,1,0:T(8,128)}, f32[16,8,128]{2,1,0:T(8,128)S(1)}) custom-call(s32[16]{0:T(128)} %bitcast.10, s32[16]{0:T(128)} %bitcast.12, f32[16,8,128]{2,1,0:T(8,128)S(1)} %all-to-all-done.1.winds_ref, f32[16,128,128]{2,1,0:T(8,128)S(1)} %bitcast.7, f32[16,128,128]{2,1,0:T(8,128)S(1)} %bitcast.8, ...), custom_call_target="tpu_custom_call" | custom-call | flops 50000000 | bytes 6500000 | tf_op jit(solution)/shard_map/fire/pallas_call | solution.py:451
  43.6 0.0 collective-permute-done.2.one_x_ref
  43.6 0.0 collective-permute-done.3.two_x_ref
  43.6 0.6 %sort_rows.1 = (f32[16,8,128]{2,1,0:T(8,128)}, f32[80,128]{1,0:T(8,128)S(1)}, f32[80,128]{1,0:T(8,128)S(1)}) custom-call(f32[16,8,128]{2,1,0:T(8,128)S(1)} %get-tuple-element.23.outbox_ref, f32[80,128]{1,0:T(8,128)S(1)} %collective-permute-done.2.one_x_ref, f32[80,128]{1,0:T(8,128)S(1)} %collective-permute-done.3.two_x_ref), custom_call_target="tpu_custom_call" | custom-call | tf_op jit(solution)/shard_map/sort_rows/pallas_call | solution.py:491
  44.2 3.5 %all-to-all-start.2 = ((f32[16,8,128]{2,1,0:T(8,128)}), f32[16,8,128]{2,1,0:T(8,128)S(1)}, u32[]{:S(2)}, u32[]{:S(2)}) async-start(f32[16,8,128]{2,1,0:T(8,128)} %get-tuple-element.26), calls=%async_computation.2 | async-start | bytes 131072 | tf_op jit(solution)/shard_map/all_to_all | solution.py:560
  47.7 4.9 %advect.1.part_ref = f32[80,64,128]{2,1,0:T(8,128)S(1)} custom-call(f32[80,64,128]{2,1,0:T(8,128)} %theta_ref.3, f32[80,64,128]{2,1,0:T(8,128)} %u_ref.3, f32[80,64,128]{2,1,0:T(8,128)} %v_ref.3, f32[80,128]{1,0:T(8,128)S(1)} %get-tuple-element.27.west_ref, f32[80,128]{1,0:T(8,128)S(1)} %get-tuple-element.28.east_ref, ...), custom_call_target="tpu_custom_call" | custom-call | flops 14000000 | bytes 8000000 | tf_op jit(solution)/shard_map/advect/pallas_call | solution.py:308
  52.7 2.7 %all-to-all-done.2.inbox_ref = f32[16,8,128]{2,1,0:T(8,128)S(1)} async-done(((f32[16,8,128]{2,1,0:T(8,128)}), f32[16,8,128]{2,1,0:T(8,128)S(1)}, u32[]{:S(2)}, u32[]{:S(2)}) %all-to-all-start.2) | async-done | bytes 65568 | tf_op jit(solution)/shard_map/all_to_all | solution.py:560
  55.3 2.1 %finish.1 = f32[80,64,128]{2,1,0:T(8,128)} custom-call(f32[16,8,128]{2,1,0:T(8,128)S(1)} %all-to-all-done.2.inbox_ref, f32[80,64,128]{2,1,0:T(8,128)S(1)} %advect.1.part_ref), custom_call_target="tpu_custom_call" | custom-call | flops 3000000 | bytes 2700000 | tf_op jit(solution)/shard_map/finish/pallas_call | solution.py:536
Async XLA Ops:
  2.1 15.7 %all-to-all-start = ((s32[16,8,128]{2,1,0:T(8,128)}), s32[16,8,128]{2,1,0:T(8,128)S(1)}, u32[]{:S(2)}, u32[]{:S(2)}) async-start(s32[16,8,128]{2,1,0:T(8,128)} %make_requests.1.after_ref), calls=%async_computation | async-start | bytes 131072 | tf_op jit(solution)/shard_map/all_to_all | solution.py:560
  10.1 24.7 %copy-start = (f32[1,1,16,128,128]{4,3,2,1,0:T(8,128)S(1)}, f32[1,1,16,128,128]{4,3,2,1,0:T(8,128)}, u32[]{:S(2)}) copy-start(f32[1,1,16,128,128]{4,3,2,1,0:T(8,128)} %param.11) | copy-start | bytes 3145732
  10.1 24.7 %copy-start.1 = (f32[1,1,16,128,128]{4,3,2,1,0:T(8,128)S(1)}, f32[1,1,16,128,128]{4,3,2,1,0:T(8,128)}, u32[]{:S(2)}) copy-start(f32[1,1,16,128,128]{4,3,2,1,0:T(8,128)} %param.12) | copy-start | bytes 3145732
  12.9 3.2 %collective-permute-start = (f32[64,128]{1,0:T(8,128)S(1)}, f32[64,128]{1,0:T(8,128)S(1)}, u32[]{:S(2)}, u32[]{:S(2)}) collective-permute-start(f32[64,128]{1,0:T(8,128)S(1)} %get-tuple-element.18), channel_id=1, source_target_pairs={{0,1},{1,0},{2,3},{3,2},{4,5},{5,4},{6,7},{7,6},{8,9},{9,8},{10,11... | collective-permute-start | bytes 98312 | tf_op jit(solution)/shard_map/ppermute | solution.py:556
  13.0 4.7 %collective-permute-start.1 = (f32[64,128]{1,0:T(8,128)S(1)}, f32[64,128]{1,0:T(8,128)S(1)}, u32[]{:S(2)}, u32[]{:S(2)}) collective-permute-start(f32[64,128]{1,0:T(8,128)S(1)} %get-tuple-element.19), channel_id=1, source_target_pairs={{1,2},{2,1},{3,4},{4,3},{5,6},{6,5},{7,0},{0,7},{9,10},{10,9},{11,... | collective-permute-start | bytes 98312 | tf_op jit(solution)/shard_map/ppermute | solution.py:556
  19.8 14.9 %all-to-all-start.1 = ((f32[16,8,128]{2,1,0:T(8,128)}), f32[16,8,128]{2,1,0:T(8,128)S(1)}, u32[]{:S(2)}, u32[]{:S(2)}) async-start(f32[16,8,128]{2,1,0:T(8,128)} %get-tuple-element.22), calls=%async_computation.1 | async-start | bytes 131072 | tf_op jit(solution)/shard_map/all_to_all | solution.py:560
  27.1 16.5 %collective-permute-start.2 = (f32[80,128]{1,0:T(8,128)S(1)}, f32[80,128]{1,0:T(8,128)S(1)}, u32[]{:S(2)}, u32[]{:S(2)}) collective-permute-start(f32[80,128]{1,0:T(8,128)S(1)} %get-tuple-element.24), channel_id=1, source_target_pairs={{0,8},{8,0},{16,24},{24,16},{32,40},{40,32},{48,56},{56,48},{64,72... | collective-permute-start | bytes 122888 | tf_op jit(solution)/shard_map/ppermute | solution.py:556
  29.0 14.6 %collective-permute-start.3 = (f32[80,128]{1,0:T(8,128)S(1)}, f32[80,128]{1,0:T(8,128)S(1)}, u32[]{:S(2)}, u32[]{:S(2)}) collective-permute-start(f32[80,128]{1,0:T(8,128)S(1)} %get-tuple-element.25), channel_id=1, source_target_pairs={{8,16},{16,8},{24,32},{32,24},{40,48},{48,40},{56,64},{64,56},{72,... | collective-permute-start | bytes 122888 | tf_op jit(solution)/shard_map/ppermute | solution.py:556
  44.2 11.1 %all-to-all-start.2 = ((f32[16,8,128]{2,1,0:T(8,128)}), f32[16,8,128]{2,1,0:T(8,128)S(1)}, u32[]{:S(2)}, u32[]{:S(2)}) async-start(f32[16,8,128]{2,1,0:T(8,128)} %get-tuple-element.26), calls=%async_computation.2 | async-start | bytes 131072 | tf_op jit(solution)/shard_map/all_to_all | solution.py:560

commit v8 on v7

--- a/solution.py
+++ b/solution.py
@@ -55,9 +55,9 @@
     return pltpu.CompilerParams(vmem_limit_bytes=mib * 1024 * 1024)
 
 
-def to_scalars(refs, scalars, sems):
+def to_scalars(refs, scalars, sems, others=()):
     copies = [pltpu.make_async_copy(ref, own, sems.at[c]) for c, (ref, own) in enumerate(zip(refs, scalars))]
-    for copy in copies:
+    for copy in [*copies, *others]:
         copy.start()
     for copy in copies:
         copy.wait()
@@ -74,8 +74,14 @@
     return ranks
 
 
-def request_kernel(owner_far, place_far, out_ref, owner_ref, place_ref, table, count, sems):
-    to_scalars((owner_far, place_far), (owner_ref, place_ref), sems)
+def request_kernel(
+    owner_far, place_far, theta_ref, u_ref, v_ref, out_ref, theta_out, block_ref,
+    owner_ref, place_ref, table, count, sems, far_sems,
+):
+    pairs = [(ref.at[0], block_ref.at[c * CX : (c + 1) * CX]) for c, ref in enumerate((u_ref, v_ref))]
+    pairs += [(theta_ref.at[pl.ds(g * LZ // 4, LZ // 4)], theta_out.at[pl.ds(g * LZ // 4, LZ // 4)]) for g in range(4)]
+    copies = [pltpu.make_async_copy(source, target, far_sems.at[i]) for i, (source, target) in enumerate(pairs)]
+    to_scalars((owner_far, place_far), (owner_ref, place_ref), sems, copies)
     peers = out_ref.shape[0]
     for i in range((peers + 2) * CAP):
         table[i] = -1
@@ -89,24 +95,31 @@
             for r in range(CAP):
                 line = jnp.where(lane == g * CAP + r, table[(peer + 1 + side) * CAP + r], line)
         out_ref[peer] = jnp.broadcast_to(line, (8, 128))
-
-
-def make_requests(owners, places, peers):
+    for copy in copies:
+        copy.wait()
+
+
+def make_requests(owners, places, theta, wind_u, wind_v, peers):
     return pl.pallas_call(
         request_kernel,
-        in_specs=[FAR, FAR],
-        out_specs=LOCAL,
-        out_shape=pltpu.VMEM((peers, 8, 128), jnp.int32),
+        in_specs=[FAR] * 5,
+        out_specs=[LOCAL] * 3,
+        out_shape=[
+            pltpu.VMEM((peers, 8, 128), jnp.int32),
+            pltpu.VMEM((LZ, CX, CY), F32),
+            pltpu.VMEM((2 * CX, 128), F32),
+        ],
         scratch_shapes=[
             pltpu.SMEM((TPD,), jnp.int32),
             pltpu.SMEM((TPD,), jnp.int32),
             pltpu.SMEM(((peers + 2) * CAP,), jnp.int32),
             pltpu.SMEM((peers,), jnp.int32),
             pltpu.SemaphoreType.DMA((2,)),
+            pltpu.SemaphoreType.DMA((6,)),
         ],
         name="make_requests",
         compiler_params=params(4),
-    )(far(owners), far(places))
+    )(*(far(a) for a in (owners, places, theta, wind_u, wind_v)))
 
 
 def place_on(axis):
@@ -115,31 +128,14 @@
     return even, jnp.logical_or(index == 0, index == lax.axis_size(axis) - 1)
 
 
-def edge_kernel(
-    after_ref, theta_ref, u_ref, v_ref,
-    block_ref, one_x_ref, two_x_ref, one_y_ref, two_y_ref, theta, sems, wind_sems,
-):
+def edge_kernel(theta, block_ref, one_x_ref, two_x_ref, one_y_ref, two_y_ref):
     even_x, wraps_x = place_on("gx")
     even_y, wraps_y = place_on("gy")
-
-    def copy(g):
-        part = pl.ds(g * GROUP, GROUP)
-        return pltpu.make_async_copy(theta_ref.at[part], theta.at[part], sems.at[g])
-
-    winds = [
-        pltpu.make_async_copy(ref.at[0], block_ref.at[c * CX : (c + 1) * CX], wind_sems.at[c])
-        for c, ref in enumerate((u_ref, v_ref))
-    ]
-    for g in reversed(range(GROUPS)):
-        copy(g).start()
-    for wind in winds:
-        wind.start()
     lane = iota(1, (CX, 128))
 
     def one(i, carry):
         first, last = carry
         g = GROUPS - 1 - i
-        copy(g).wait()
         first = pltpu.roll(first, GROUP, 1)
         last = pltpu.roll(last, GROUP, 1)
         for k in range(GROUP):
@@ -155,8 +151,6 @@
 
     zero = jnp.zeros((CX, 128), F32)
     first, last = lax.fori_loop(0, GROUPS, one, (zero, zero))
-    for wind in winds:
-        wind.wait()
     for c in range(2):
         cells = block_ref[c * CX : (c + 1) * CX]
         first = jnp.where(lane == WIND + c, pltpu.roll(cells, WIND + c, 1), first)
@@ -165,23 +159,18 @@
     two_y_ref[...] = jnp.where(wraps_y, 0.0, jnp.where(even_y, first, last))
 
 
-def make_edges(after, theta, wind_u, wind_v):
+def make_edges(theta, block):
     row = pltpu.VMEM((LZ, 128), F32)
     column = pltpu.VMEM((CX, 128), F32)
     return pl.pallas_call(
         edge_kernel,
-        in_specs=[ANYWHERE, FAR, FAR, FAR],
-        out_specs=[LOCAL] * 5,
-        out_shape=[pltpu.VMEM((2 * CX, 128), F32), row, row, column, column],
-        scratch_shapes=[
-            pltpu.VMEM((LZ, CX, CY), F32),
-            pltpu.SemaphoreType.DMA((GROUPS,)),
-            pltpu.SemaphoreType.DMA((2,)),
-        ],
+        in_specs=[LOCAL] * 2,
+        out_specs=[LOCAL] * 4,
+        out_shape=[row, row, column, column],
         name="edges",
-        compiler_params=params(8),
+        compiler_params=params(4),
         cost_estimate=pl.CostEstimate(flops=4_000_000, bytes_accessed=2_700_000, transcendentals=0),
-    )(after, far(theta), far(wind_u), far(wind_v))
+    )(near(theta), near(block))
 
 
 def cut_kernel(
@@ -322,19 +311,58 @@
     )(far(theta), far(wind_u), far(wind_v), *(near(a) for a in rims))
 
 
+def tile_kernel(after_ref, level_ref, fuel_ref, base_ref, out_ref, level, fuel, base, sems):
+    def copies(i):
+        some = pl.ds(i * SIDE, SIDE)
+        pairs = ((level_ref, level), (fuel_ref, fuel), (base_ref, base))
+        return [
+            pltpu.make_async_copy(source.at[some], target.at[some], sems.at[c, i])
+            for c, (source, target) in enumerate(pairs)
+        ]
+
+    for i in range(TPD // SIDE):
+        for copy in copies(i):
+            copy.start()
+
+    def some(i, carry):
+        for copy in copies(i):
+            copy.wait()
+        for j in range(SIDE):
+            t = i * SIDE + j
+            cells = [fuel[t, pl.ds(k, 8, stride=ROWS), :] for k in range(ROWS)]
+            out_ref[t, 3 * ROWS] = sum(cells[1:], cells[0])
+            for k in range(ROWS):
+                out_ref[t, ROWS + k] = cells[k]
+                out_ref[t, k] = level[t, pl.ds(k, 8, stride=ROWS), :]
+                out_ref[t, 2 * ROWS + k] = base[t, pl.ds(k, 8, stride=ROWS), :] * (0.5 * time_step)
+        return carry
+
+    lax.fori_loop(0, TPD // SIDE, some, 0)
+
+
+def prepare_tiles(after, level_set, fuel_load, spread_base):
+    tiles = pltpu.VMEM((TPD, S, S), F32)
+    return pl.pallas_call(
+        tile_kernel,
+        in_specs=[ANYWHERE, FAR, FAR, FAR],
+        out_specs=LOCAL,
+        out_shape=pltpu.VMEM((TPD, 3 * ROWS + 1, 8, 128), F32),
+        scratch_shapes=[tiles, tiles, tiles, pltpu.SemaphoreType.DMA((3, TPD // SIDE))],
+        name="prepare_tiles",
+        compiler_params=params(8),
+        cost_estimate=pl.CostEstimate(flops=300_000, bytes_accessed=3_200_000, transcendentals=0),
+    )(after, *(far(a) for a in (level_set, fuel_load, spread_base)))
+
+
 def fire_kernel(
-    peers, waits, owner_far, place_far, winds_ref, level_ref, fuel_ref, base_ref, *rest
+    peers, waits, owner_far, place_far, winds_ref, tile_ref, *rest
 ):
     (
         level_out, fuel_out, outbox, begins, slopes, heats,
-        level_own, fuel_own, base_own, owner_ref, place_ref, count, scalar_sems, in_sems, out_sems,
+        level_own, fuel_own, owner_ref, place_ref, count, scalar_sems, out_sems,
     ) = rest[waits:]
     lane = iota(1)
     row = iota(0)
-
-    def bases(i):
-        some = pl.ds(i * SIDE, SIDE)
-        return pltpu.make_async_copy(base_ref.at[some], base_own.at[some], in_sems.at[i])
 
     def results(i):
         some = pl.ds(i * SIDE, SIDE)
@@ -344,8 +372,6 @@
             for c, (source, target) in enumerate(pairs)
         ]
 
-    for i in range(TPD // SIDE):
-        bases(i).start()
     to_scalars((owner_far, place_far), (owner_ref, place_ref), scalar_sems)
 
     tiles_y = CY // TA
@@ -379,10 +405,9 @@
     def burn(t):
         begin = [begins[2 * t + c] for c in range(2)]
         slope = [slopes[2 * t + c] for c in range(2)]
-        level = [level_ref[t, pl.ds(k, 8, stride=ROWS), :] for k in range(ROWS)]
-        fuel = [fuel_ref[t, pl.ds(k, 8, stride=ROWS), :] for k in range(ROWS)]
-        heat = sum(fuel[1:], fuel[0])
-        rate = [base_own[t, pl.ds(k, 8, stride=ROWS), :] * (0.5 * time_step) for k in range(ROWS)]
+        level = [tile_ref[t, k] for k in range(ROWS)]
+        fuel = [tile_ref[t, ROWS + k] for k in range(ROWS)]
+        rate = [tile_ref[t, 2 * ROWS + k] for k in range(ROWS)]
         wind = [[begin[c] + slope[c] * float(k) for k in range(ROWS)] for c in range(2)]
         yield
         for _ in range(KSUB):
@@ -411,11 +436,10 @@
         for k in range(ROWS):
             level_own[t, pl.ds(k, 8, stride=ROWS), :] = level[k]
             fuel_own[t, pl.ds(k, 8, stride=ROWS), :] = fuel[k]
-        heats[t] = (heat - sum(fuel[1:], fuel[0])) * (1.0 / (R * R))
+        heats[t] = (tile_ref[t, 3 * ROWS] - sum(fuel[1:], fuel[0])) * (1.0 / (R * R))
 
     def some(i, carry):
         tiles = [i * SIDE + j for j in range(SIDE)]
-        bases(i).wait()
         works = [burn(t) for t in tiles]
         while works:
             works = [w for w in works if next(w, works) is None]
@@ -446,11 +470,11 @@
             copy.wait()
 
 
-def fire(owners, places, winds, level_set, fuel_load, spread_base, peers, waits):
+def fire(owners, places, winds, tiles_near, peers, waits):
     tiles = (TPD, S, S)
     return pl.pallas_call(
         functools.partial(fire_kernel, peers, len(waits)),
-        in_specs=[FAR, FAR] + [LOCAL] * 3 + [FAR] + [ANYWHERE] * len(waits),
+        in_specs=[FAR, FAR, LOCAL, LOCAL] + [ANYWHERE] * len(waits),
         out_specs=[ANYWHERE, ANYWHERE, LOCAL],
         out_shape=[
             jax.ShapeDtypeStruct(tiles, F32),
@@ -463,12 +487,10 @@
             pltpu.VMEM((TPD, 8, 128), F32),
             pltpu.VMEM(tiles, F32),
             pltpu.VMEM(tiles, F32),
-            pltpu.VMEM(tiles, F32),
             pltpu.SMEM((TPD,), jnp.int32),
             pltpu.SMEM((TPD,), jnp.int32),
             pltpu.SMEM((peers,), jnp.int32),
             pltpu.SemaphoreType.DMA((2,)),
-            pltpu.SemaphoreType.DMA((TPD // SIDE,)),
             pltpu.SemaphoreType.DMA((2, TPD // SIDE)),
         ],
         name="fire",
@@ -476,7 +498,7 @@
         cost_estimate=pl.CostEstimate(
             flops=50_000_000, bytes_accessed=6_500_000, transcendentals=3_200_000
         ),
-    )(far(owners), far(places), *(near(a) for a in (winds, level_set, fuel_load)), far(spread_base), *waits)
+    )(far(owners), far(places), near(winds), near(tiles_near), *waits)
 
 
 def row_kernel(outbox_ref, one_x_ref, two_x_ref, outbox_out, west_ref, east_ref):
@@ -549,11 +571,22 @@
     )(near(inbox), near(part))
 
 
-def swapped(one, two, axis):
-    count = lax.axis_size(axis)
+def swapped_y(one, two):
+    count = lax.axis_size("gy")
     pairs = [(i, i ^ 1) for i in range(count)]
     others = [((i + 1) % count, ((i ^ 1) + 1) % count) for i in range(count)]
-    return lax.ppermute(one, axis, pairs), lax.ppermute(two, axis, others)
+    return lax.ppermute(one, "gy", pairs), lax.ppermute(two, "gy", others)
+
+
+def swapped_x(one, two):
+    count, rows = lax.axis_size("gx"), lax.axis_size("gy")
+    pairs = [(i, i ^ 1) for i in range(count)]
+    others = []
+    for i in range(count):
+        for j in range(rows):
+            to = (i, j ^ 1) if i in (0, count - 1) else (((i - 1) ^ 1) + 1, j)
+            others.append((i * rows + j, to[0] * rows + to[1]))
+    return lax.ppermute(one, "gx", pairs), lax.ppermute(two, ("gx", "gy"), others)
 
 
 def exchange(cells):
@@ -563,19 +596,18 @@
 def body(theta, wind_u, wind_v, level_set, fuel_load, spread_base, tile_owner, tile_place):
     peers = lax.axis_size("gx")
     owners, places = tile_owner[0, 0], tile_place[0, 0]
-    requests = make_requests(owners, places, peers)
+    requests, near_theta, block = make_requests(owners, places, theta, wind_u, wind_v, peers)
     asked = exchange(requests)
 
-    block, one_x, two_x, one_y, two_y = make_edges(requests, theta, wind_u, wind_v)
-    rims_y = swapped(one_y, two_y, "gy")
+    one_x, two_x, one_y, two_y = make_edges(near_theta, block)
+    rims_y = swapped_y(one_y, two_y)
 
     patches, one_x, two_x = cut_patches(asked, block, *rims_y, one_x, two_x)
     winds = exchange(patches)
-    rims_x = swapped(one_x, two_x, "gx")
-
-    level_out, fuel_out, outbox = fire(
-        owners, places, winds, level_set[0, 0], fuel_load[0, 0], spread_base[0, 0], peers, ()
-    )
+    rims_x = swapped_x(one_x, two_x)
+
+    tiles_near = prepare_tiles(patches, level_set[0, 0], fuel_load[0, 0], spread_base[0, 0])
+    level_out, fuel_out, outbox = fire(owners, places, winds, tiles_near, peers, ())
     outbox, west, east = sort_rows(outbox, *rims_x)
     part = advect(theta, wind_u, wind_v, west, east, *rims_y)
     inbox = exchange(outbox)

time: 57.8 us -> 57.5 us (level)
  starting transfers between devices: 28 us -> 23.3 us
  waiting for transfers between devices: 5.85 us -> 9.06 us
  Pallas kernels: 22.8 us -> 24.1 us
    ppermute x4, starting transfers between devices: 9.31 us -> 5.13 us  [the longest x2 3.2 us: swapped_y(): return (lax.ppermute(one, 'gy', pairs), lax.ppermute(two, 'gy', others))]
    all_to_all x3, waiting for transfers between devices: 4.25 us -> 7.45 us  [exchange(): return lax.all_to_all(cells, 'gx', split_axis=0, concat_axis=0, tiled=True)]
    pallas_call x2 -> x3, Pallas kernels: 4.29 us -> 6.3 us  [the longest x1 2.42 us: make_requests(): pl.pallas_call(request_kernel, in_specs=[FAR] * 5, out_specs=[LOCAL] * 3,...]
    pallas_call x1, Pallas kernels: 8.8 us -> 8.07 us  [fire(): pl.pallas_call(functools.partial(fire_kernel, peers, len(waits)), in_spec...]
    all_to_all x3, starting transfers between devices: 18.7 us -> 18.1 us  [exchange(): return lax.all_to_all(cells, 'gx', split_axis=0, concat_axis=0, tiled=True)]
  transfers between devices with their start and end apart: 7 -> 7, of which waited for: 3 -> 4; matrix products, arithmetic and copies ran while one was open for 0% -> 0% of each run, Pallas kernels for 29% -> 30%
where the time goes in v8:
time: 57.5 us; the launch traced here: 57.1 us
  Pallas kernels  24.1 us (42%)
  starting transfers between devices  23.3 us (41%)
  waiting for transfers between devices  9.06 us (16%)
  between operations  0.73 us (1%)
    all_to_all x3, starting transfers between devices, exchange(): return lax.all_to_all(cells, 'gx', split_axis=0, concat_axis=0, tiled=True)  18.1 us
    pallas_call x1, Pallas kernels, fire(): pl.pallas_call(functools.partial(fire_kernel, peers, len(waits)), in_spec...  8.07 us
    all_to_all x3, waiting for transfers between devices, exchange(): return lax.all_to_all(cells, 'gx', split_axis=0, concat_axis=0, tiled=True)  7.45 us
    pallas_call x1, Pallas kernels, advect(): pl.pallas_call(advect_kernel, in_specs=[FAR] * 3 + [LOCAL] * 4, out_specs...  4.93 us
    ppermute x2, starting transfers between devices, swapped_y(): return (lax.ppermute(one, 'gy', pairs), lax.ppermute(two, 'gy', others))  3.2 us
    pallas_call x1, Pallas kernels, make_requests(): pl.pallas_call(request_kernel, in_specs=[FAR] * 5, out_specs=[LOCAL] * 3,...  2.42 us
    pallas_call x1, Pallas kernels, prepare_tiles(): pl.pallas_call(tile_kernel, in_specs=[ANYWHERE, FAR, FAR, FAR], out_specs...  2.25 us
    pallas_call x1, Pallas kernels, finish(): pl.pallas_call(final_kernel, in_specs=[LOCAL, LOCAL], out_specs=ANYWHERE,...  2.08 us
  transfers between devices with their start and end apart: 7, of which 4 were waited for; matrix products, arithmetic and copies ran while one was open for 0% of the time, Pallas kernels for 30%

profile of v8, /device:TPU:0, one launch (start us, length us, event | category | flops | bytes accessed | tf_op | source)
XLA Modules:
  0.0 57.1 jit_solution(3756327065777373303)
XLA Ops:
  0.6 2.4 %make_requests.1 = (s32[16,8,128]{2,1,0:T(8,128)}, f32[80,64,128]{2,1,0:T(8,128)S(1)}, f32[128,128]{1,0:T(8,128)S(1)}) custom-call(s32[16]{0:T(128)} %bitcast.10, s32[16]{0:T(128)} %bitcast.12, f32[80,64,128]{2,1,0:T(8,128)} %theta_ref.3, f32[80,64,128]{2,1,0:T(8,128)} %u_ref.3, f32[80,64,128]{2,1,0:T(8,128)} %v_ref.3), custom_call_target="tpu_custom_call" | custom-call | tf_op jit(solution)/shard_map/make_requests/pallas_call | solution.py:103
  3.1 8.0 %all-to-all-start = ((s32[16,8,128]{2,1,0:T(8,128)}), s32[16,8,128]{2,1,0:T(8,128)S(1)}, u32[]{:S(2)}, u32[]{:S(2)}) async-start(s32[16,8,128]{2,1,0:T(8,128)} %get-tuple-element.19), calls=%async_computation | async-start | bytes 131072 | tf_op jit(solution)/shard_map/all_to_all | solution.py:593
  11.0 1.6 %edges.1 = (f32[80,128]{1,0:T(8,128)S(1)}, f32[80,128]{1,0:T(8,128)S(1)}, f32[64,128]{1,0:T(8,128)S(1)}, f32[64,128]{1,0:T(8,128)S(1)}) custom-call(f32[80,64,128]{2,1,0:T(8,128)S(1)} %get-tuple-element.21.theta, f32[128,128]{1,0:T(8,128)S(1)} %get-tuple-element.20.block_ref), custom_call_target="tpu_custom_call" | custom-call | flops 4000000 | bytes 2700000 | tf_op jit(solution)/shard_map/edges/pallas_call | solution.py:165
  12.7 0.1 collective-permute-start
  12.8 3.1 %collective-permute-start.1 = (f32[64,128]{1,0:T(8,128)S(1)}, f32[64,128]{1,0:T(8,128)S(1)}, u32[]{:S(2)}, u32[]{:S(2)}) collective-permute-start(f32[64,128]{1,0:T(8,128)S(1)} %get-tuple-element.23), channel_id=1, source_target_pairs={{1,2},{2,1},{3,4},{4,3},{5,6},{6,5},{7,0},{0,7},{9,10},{10,9},{11,... | collective-permute-start | bytes 98312 | tf_op jit(solution)/shard_map/ppermute | solution.py:578
  15.9 0.0 collective-permute-done.one_y_ref
  15.9 1.6 %collective-permute-done.1.two_y_ref = f32[64,128]{1,0:T(8,128)S(1)} collective-permute-done((f32[64,128]{1,0:T(8,128)S(1)}, f32[64,128]{1,0:T(8,128)S(1)}, u32[]{:S(2)}, u32[]{:S(2)}) %collective-permute-start.1) | collective-permute-done | bytes 32800 | tf_op jit(solution)/shard_map/ppermute | solution.py:578
  17.5 1.2 %all-to-all-done.asked_far = s32[16,8,128]{2,1,0:T(8,128)S(1)} async-done(((s32[16,8,128]{2,1,0:T(8,128)}), s32[16,8,128]{2,1,0:T(8,128)S(1)}, u32[]{:S(2)}, u32[]{:S(2)}) %all-to-all-start) | async-done | bytes 65568 | tf_op jit(solution)/shard_map/all_to_all | solution.py:593
  18.7 2.1 %cut_patches.1 = (f32[16,8,128]{2,1,0:T(8,128)}, f32[80,128]{1,0:T(8,128)S(1)}, f32[80,128]{1,0:T(8,128)S(1)}) custom-call(s32[16,8,128]{2,1,0:T(8,128)S(1)} %all-to-all-done.asked_far, f32[128,128]{1,0:T(8,128)S(1)} %get-tuple-element.20.block_ref, f32[64,128]{1,0:T(8,128)S(1)} %collective-permute-done.one_y_ref, ...), custom_call_target="tpu_custom_call" | custom-call | tf_op jit(solution)/shard_map/cut_patches/pallas_call | solution.py:224
  20.8 6.0 %all-to-all-start.1 = ((f32[16,8,128]{2,1,0:T(8,128)}), f32[16,8,128]{2,1,0:T(8,128)S(1)}, u32[]{:S(2)}, u32[]{:S(2)}) async-start(f32[16,8,128]{2,1,0:T(8,128)} %get-tuple-element.26.after_ref), calls=%async_computation.1 | async-start | bytes 131072 | tf_op jit(solution)/shard_map/all_to_all | solution.py:593
  26.8 1.9 %collective-permute-start.2 = (f32[80,128]{1,0:T(8,128)S(1)}, f32[80,128]{1,0:T(8,128)S(1)}, u32[]{:S(2)}, u32[]{:S(2)}) collective-permute-start(f32[80,128]{1,0:T(8,128)S(1)} %get-tuple-element.28), channel_id=1, source_target_pairs={{0,8},{8,0},{16,24},{24,16},{32,40},{40,32},{48,56},{56,48},{64,72... | collective-permute-start | bytes 122888 | tf_op jit(solution)/shard_map/ppermute | solution.py:589
  28.7 0.0 collective-permute-start.3
  28.7 2.2 %prepare_tiles.1.tile_ref = f32[16,49,8,128]{3,2,1,0:T(8,128)S(1)} custom-call(f32[16,8,128]{2,1,0:T(8,128)} %get-tuple-element.26.after_ref, f32[16,128,128]{2,1,0:T(8,128)} %bitcast.7, f32[16,128,128]{2,1,0:T(8,128)} %bitcast.8, f32[16,128,128]{2,1,0:T(8,128)} %bitcast.9), custom_call_target="tpu_custom_call" | custom-call | flops 300000 | bytes 3200000 | tf_op jit(solution)/shard_map/prepare_tiles/pallas_call | solution.py:345
  31.0 3.5 %all-to-all-done.1.winds_ref = f32[16,8,128]{2,1,0:T(8,128)S(1)} async-done(((f32[16,8,128]{2,1,0:T(8,128)}), f32[16,8,128]{2,1,0:T(8,128)S(1)}, u32[]{:S(2)}, u32[]{:S(2)}) %all-to-all-start.1) | async-done | bytes 65568 | tf_op jit(solution)/shard_map/all_to_all | solution.py:593
  34.5 8.1 %fire.1 = (f32[16,128,128]{2,1,0:T(8,128)}, f32[16,128,128]{2,1,0:T(8,128)}, f32[16,8,128]{2,1,0:T(8,128)S(1)}) custom-call(s32[16]{0:T(128)} %bitcast.11, s32[16]{0:T(128)} %bitcast.13, f32[16,8,128]{2,1,0:T(8,128)S(1)} %all-to-all-done.1.winds_ref, f32[16,49,8,128]{3,2,1,0:T(8,128)S(1)} %prepare_tiles.1.tile_ref), custom_call_target="tpu_custom_call" | custom-call | flops 50000000 | bytes 6500000 | tf_op jit(solution)/shard_map/fire/pallas_call | solution.py:475
  42.6 0.0 collective-permute-done.2.one_x_ref
  42.6 0.0 collective-permute-done.3.two_x_ref
  42.6 0.6 %sort_rows.1 = (f32[16,8,128]{2,1,0:T(8,128)}, f32[80,128]{1,0:T(8,128)S(1)}, f32[80,128]{1,0:T(8,128)S(1)}) custom-call(f32[16,8,128]{2,1,0:T(8,128)S(1)} %get-tuple-element.27.outbox_ref, f32[80,128]{1,0:T(8,128)S(1)} %collective-permute-done.2.one_x_ref, f32[80,128]{1,0:T(8,128)S(1)} %collective-permute-done.3.two_x_ref), custom_call_target="tpu_custom_call" | custom-call | tf_op jit(solution)/shard_map/sort_rows/pallas_call | solution.py:513
  43.2 4.1 %all-to-all-start.2 = ((f32[16,8,128]{2,1,0:T(8,128)}), f32[16,8,128]{2,1,0:T(8,128)S(1)}, u32[]{:S(2)}, u32[]{:S(2)}) async-start(f32[16,8,128]{2,1,0:T(8,128)} %get-tuple-element.30), calls=%async_computation.2 | async-start | bytes 131072 | tf_op jit(solution)/shard_map/all_to_all | solution.py:593
  47.4 4.9 %advect.1.part_ref = f32[80,64,128]{2,1,0:T(8,128)S(1)} custom-call(f32[80,64,128]{2,1,0:T(8,128)} %theta_ref.3, f32[80,64,128]{2,1,0:T(8,128)} %u_ref.3, f32[80,64,128]{2,1,0:T(8,128)} %v_ref.3, f32[80,128]{1,0:T(8,128)S(1)} %get-tuple-element.31.west_ref, f32[80,128]{1,0:T(8,128)S(1)} %get-tuple-element.32.east_ref, ...), custom_call_target="tpu_custom_call" | custom-call | flops 14000000 | bytes 8000000 | tf_op jit(solution)/shard_map/advect/pallas_call | solution.py:297
  52.3 2.7 %all-to-all-done.2.inbox_ref = f32[16,8,128]{2,1,0:T(8,128)S(1)} async-done(((f32[16,8,128]{2,1,0:T(8,128)}), f32[16,8,128]{2,1,0:T(8,128)S(1)}, u32[]{:S(2)}, u32[]{:S(2)}) %all-to-all-start.2) | async-done | bytes 65568 | tf_op jit(solution)/shard_map/all_to_all | solution.py:593
  55.0 2.1 %finish.1 = f32[80,64,128]{2,1,0:T(8,128)} custom-call(f32[16,8,128]{2,1,0:T(8,128)S(1)} %all-to-all-done.2.inbox_ref, f32[80,64,128]{2,1,0:T(8,128)S(1)} %advect.1.part_ref), custom_call_target="tpu_custom_call" | custom-call | flops 3000000 | bytes 2700000 | tf_op jit(solution)/shard_map/finish/pallas_call | solution.py:558
Async XLA Ops:
  3.1 15.6 %all-to-all-start = ((s32[16,8,128]{2,1,0:T(8,128)}), s32[16,8,128]{2,1,0:T(8,128)S(1)}, u32[]{:S(2)}, u32[]{:S(2)}) async-start(s32[16,8,128]{2,1,0:T(8,128)} %get-tuple-element.19), calls=%async_computation | async-start | bytes 131072 | tf_op jit(solution)/shard_map/all_to_all | solution.py:593
  12.7 3.2 %collective-permute-start = (f32[64,128]{1,0:T(8,128)S(1)}, f32[64,128]{1,0:T(8,128)S(1)}, u32[]{:S(2)}, u32[]{:S(2)}) collective-permute-start(f32[64,128]{1,0:T(8,128)S(1)} %get-tuple-element.22), channel_id=1, source_target_pairs={{0,1},{1,0},{2,3},{3,2},{4,5},{5,4},{6,7},{7,6},{8,9},{9,8},{10,11... | collective-permute-start | bytes 98312 | tf_op jit(solution)/shard_map/ppermute | solution.py:578
  12.8 4.7 %collective-permute-start.1 = (f32[64,128]{1,0:T(8,128)S(1)}, f32[64,128]{1,0:T(8,128)S(1)}, u32[]{:S(2)}, u32[]{:S(2)}) collective-permute-start(f32[64,128]{1,0:T(8,128)S(1)} %get-tuple-element.23), channel_id=1, source_target_pairs={{1,2},{2,1},{3,4},{4,3},{5,6},{6,5},{7,0},{0,7},{9,10},{10,9},{11,... | collective-permute-start | bytes 98312 | tf_op jit(solution)/shard_map/ppermute | solution.py:578
  20.8 13.7 %all-to-all-start.1 = ((f32[16,8,128]{2,1,0:T(8,128)}), f32[16,8,128]{2,1,0:T(8,128)S(1)}, u32[]{:S(2)}, u32[]{:S(2)}) async-start(f32[16,8,128]{2,1,0:T(8,128)} %get-tuple-element.26.after_ref), calls=%async_computation.1 | async-start | bytes 131072 | tf_op jit(solution)/shard_map/all_to_all | solution.py:593
  26.8 15.8 %collective-permute-start.2 = (f32[80,128]{1,0:T(8,128)S(1)}, f32[80,128]{1,0:T(8,128)S(1)}, u32[]{:S(2)}, u32[]{:S(2)}) collective-permute-start(f32[80,128]{1,0:T(8,128)S(1)} %get-tuple-element.28), channel_id=1, source_target_pairs={{0,8},{8,0},{16,24},{24,16},{32,40},{40,32},{48,56},{56,48},{64,72... | collective-permute-start | bytes 122888 | tf_op jit(solution)/shard_map/ppermute | solution.py:589
  28.7 13.9 %collective-permute-start.3 = (f32[80,128]{1,0:T(8,128)S(1)}, f32[80,128]{1,0:T(8,128)S(1)}, u32[]{:S(2)}, u32[]{:S(2)}) collective-permute-start(f32[80,128]{1,0:T(8,128)S(1)} %get-tuple-element.29), channel_id=1, source_target_pairs={{0,1},{1,0},{2,3},{3,2},{4,5},{5,4},{6,7},{7,6},{8,16},{9,17},{10,... | collective-permute-start | bytes 122888 | tf_op jit(solution)/shard_map/ppermute | solution.py:589
  43.2 11.8 %all-to-all-start.2 = ((f32[16,8,128]{2,1,0:T(8,128)}), f32[16,8,128]{2,1,0:T(8,128)S(1)}, u32[]{:S(2)}, u32[]{:S(2)}) async-start(f32[16,8,128]{2,1,0:T(8,128)} %get-tuple-element.30), calls=%async_computation.2 | async-start | bytes 131072 | tf_op jit(solution)/shard_map/all_to_all | solution.py:593

commit v9 on v8

--- a/solution.py
+++ b/solution.py
@@ -74,14 +74,8 @@
     return ranks
 
 
-def request_kernel(
-    owner_far, place_far, theta_ref, u_ref, v_ref, out_ref, theta_out, block_ref,
-    owner_ref, place_ref, table, count, sems, far_sems,
-):
-    pairs = [(ref.at[0], block_ref.at[c * CX : (c + 1) * CX]) for c, ref in enumerate((u_ref, v_ref))]
-    pairs += [(theta_ref.at[pl.ds(g * LZ // 4, LZ // 4)], theta_out.at[pl.ds(g * LZ // 4, LZ // 4)]) for g in range(4)]
-    copies = [pltpu.make_async_copy(source, target, far_sems.at[i]) for i, (source, target) in enumerate(pairs)]
-    to_scalars((owner_far, place_far), (owner_ref, place_ref), sems, copies)
+def request_kernel(owner_far, place_far, out_ref, owner_ref, place_ref, table, count, sems):
+    to_scalars((owner_far, place_far), (owner_ref, place_ref), sems)
     peers = out_ref.shape[0]
     for i in range((peers + 2) * CAP):
         table[i] = -1
@@ -93,33 +87,26 @@
         line = jnp.full((1, 128), -1, jnp.int32)
         for g, side in enumerate(SIDES):
             for r in range(CAP):
-                line = jnp.where(lane == g * CAP + r, table[(peer + 1 + side) * CAP + r], line)
+                line = jnp.where(lane % 8 == g * CAP + r, table[(peer + 1 + side) * CAP + r], line)
         out_ref[peer] = jnp.broadcast_to(line, (8, 128))
-    for copy in copies:
-        copy.wait()
-
-
-def make_requests(owners, places, theta, wind_u, wind_v, peers):
+
+
+def make_requests(owners, places, peers):
     return pl.pallas_call(
         request_kernel,
-        in_specs=[FAR] * 5,
-        out_specs=[LOCAL] * 3,
-        out_shape=[
-            pltpu.VMEM((peers, 8, 128), jnp.int32),
-            pltpu.VMEM((LZ, CX, CY), F32),
-            pltpu.VMEM((2 * CX, 128), F32),
-        ],
+        in_specs=[FAR, FAR],
+        out_specs=LOCAL,
+        out_shape=pltpu.VMEM((peers, 8, 128), jnp.int32),
         scratch_shapes=[
             pltpu.SMEM((TPD,), jnp.int32),
             pltpu.SMEM((TPD,), jnp.int32),
             pltpu.SMEM(((peers + 2) * CAP,), jnp.int32),
             pltpu.SMEM((peers,), jnp.int32),
             pltpu.SemaphoreType.DMA((2,)),
-            pltpu.SemaphoreType.DMA((6,)),
         ],
         name="make_requests",
         compiler_params=params(4),
-    )(*(far(a) for a in (owners, places, theta, wind_u, wind_v)))
+    )(far(owners), far(places))
 
 
 def place_on(axis):
@@ -128,29 +115,40 @@
     return even, jnp.logical_or(index == 0, index == lax.axis_size(axis) - 1)
 
 
-def edge_kernel(theta, block_ref, one_x_ref, two_x_ref, one_y_ref, two_y_ref):
+def edge_kernel(
+    after_ref, theta_ref, u_ref, v_ref,
+    block_ref, one_x_ref, two_x_ref, one_y_ref, two_y_ref, theta, sems, wind_sems,
+):
     even_x, wraps_x = place_on("gx")
     even_y, wraps_y = place_on("gy")
+
+    def copy(g):
+        part = pl.ds(g * GROUP, GROUP)
+        return pltpu.make_async_copy(theta_ref.at[part], theta.at[part], sems.at[g])
+
+    winds = [
+        pltpu.make_async_copy(ref.at[0], block_ref.at[c * CX : (c + 1) * CX], wind_sems.at[c])
+        for c, ref in enumerate((u_ref, v_ref))
+    ]
+    for g in range(GROUPS):
+        copy(g).start()
+    for wind in winds:
+        wind.start()
     lane = iota(1, (CX, 128))
 
-    def one(i, carry):
-        first, last = carry
-        g = GROUPS - 1 - i
-        first = pltpu.roll(first, GROUP, 1)
-        last = pltpu.roll(last, GROUP, 1)
-        for k in range(GROUP):
-            z = g * GROUP + k
-            cells = theta[z]
-            low, high = cells[0:1], cells[CX - 1 : CX]
-            one_x_ref[pl.ds(z, 1)] = jnp.where(even_x, high, low)
-            two_x_ref[pl.ds(z, 1)] = jnp.where(wraps_x, 0.0, jnp.where(even_x, low, high))
-            turned = pltpu.roll(cells, k + 1, 1)
-            first = jnp.where(lane == k + 1, turned, first)
-            last = jnp.where(lane == k, turned, last)
-        return first, last
-
-    zero = jnp.zeros((CX, 128), F32)
-    first, last = lax.fori_loop(0, GROUPS, one, (zero, zero))
+    first = last = jnp.zeros((CX, 128), F32)
+    for z in range(LZ):
+        if z % GROUP == 0:
+            copy(z // GROUP).wait()
+        cells = theta[z]
+        low, high = cells[0:1], cells[CX - 1 : CX]
+        one_x_ref[z : z + 1] = jnp.where(even_x, high, low)
+        two_x_ref[z : z + 1] = jnp.where(wraps_x, 0.0, jnp.where(even_x, low, high))
+        turned = pltpu.roll(cells, z + 1, 1)
+        first = jnp.where(lane == z + 1, turned, first)
+        last = jnp.where(lane == z, turned, last)
+    for wind in winds:
+        wind.wait()
     for c in range(2):
         cells = block_ref[c * CX : (c + 1) * CX]
         first = jnp.where(lane == WIND + c, pltpu.roll(cells, WIND + c, 1), first)
@@ -159,25 +157,41 @@
     two_y_ref[...] = jnp.where(wraps_y, 0.0, jnp.where(even_y, first, last))
 
 
-def make_edges(theta, block):
+def make_edges(after, theta, wind_u, wind_v):
     row = pltpu.VMEM((LZ, 128), F32)
     column = pltpu.VMEM((CX, 128), F32)
     return pl.pallas_call(
         edge_kernel,
-        in_specs=[LOCAL] * 2,
-        out_specs=[LOCAL] * 4,
-        out_shape=[row, row, column, column],
+        in_specs=[ANYWHERE, FAR, FAR, FAR],
+        out_specs=[LOCAL] * 5,
+        out_shape=[pltpu.VMEM((2 * CX, 128), F32), row, row, column, column],
+        scratch_shapes=[
+            pltpu.VMEM((LZ, CX, CY), F32),
+            pltpu.SemaphoreType.DMA((GROUPS,)),
+            pltpu.SemaphoreType.DMA((2,)),
+        ],
         name="edges",
-        compiler_params=params(4),
+        compiler_params=params(8),
         cost_estimate=pl.CostEstimate(flops=4_000_000, bytes_accessed=2_700_000, transcendentals=0),
-    )(near(theta), near(block))
+    )(after, far(theta), far(wind_u), far(wind_v))
 
 
 def cut_kernel(
     asked_far, block_ref, one_y_ref, two_y_ref, one_x_ref, two_x_ref,
-    out_ref, one_x_out, two_x_out, surface, edges, asked_ref, sem,
+    out_ref, one_x_out, two_x_out, surface, edges, plan, asked_ref, sem,
 ):
-    copy = pltpu.make_async_copy(asked_far.at[:, 0:1], asked_ref, sem)
+    places = asked_far[...]
+    peers = places.shape[0]
+    at = iota(2, (peers, 8, 128))
+    tiles_y = CY // TA
+    y_own = jnp.bitwise_and(places, tiles_y - 1) * TA
+    kind = at % 8 // CAP
+    first = lax.shift_right_arithmetic(places, 5) * TA - 1
+    first = first + jnp.where(kind == 0, SIDES[0], jnp.where(kind == 1, SIDES[1], SIDES[2])) * CX
+    first = jnp.where(places < 0, CX, jnp.clip(first, -RIM, CX)) + RIM
+    outside = jnp.where(y_own == 0, 0, jnp.where(y_own == CY - TA, TA + 1, 1000))
+    plan[...] = jnp.where(at < 8, first, jnp.where(at < 16, jnp.bitwise_and(1 - y_own, 127), outside))
+    copy = pltpu.make_async_copy(plan.at[:, 0:1], asked_ref, sem)
     copy.start()
     one_x_out[...] = one_x_ref[...]
     two_x_out[...] = two_x_ref[...]
@@ -197,21 +211,18 @@
         edges[c, RIM : RIM + CX] = jnp.where(wide % 8 == 0, low, high)
         edges[c, RIM + CX :] = blank
     copy.wait()
-    tiles_y = CY // TA
-    for source in range(out_ref.shape[0]):
+    for source in range(peers):
         message = jnp.zeros((8, 128), F32)
-        for g, side in enumerate(SIDES):
+        for g in range(len(SIDES)):
             for r in range(CAP):
-                place = asked_ref[source, 0, g * CAP + r]
-                y_own = jnp.bitwise_and(place, tiles_y - 1) * TA
-                first = lax.shift_right_arithmetic(place, 5) * TA - 1 + side * CX
-                first = jnp.where(place < 0, CX, jnp.clip(first, -RIM, CX)) + RIM
-                begin = (g * CAP + r) * 16
-                outside = jnp.where(y_own == 0, 0, jnp.where(y_own == CY - TA, TA + 1, 1000))
+                slot = g * CAP + r
+                first = asked_ref[source, 0, slot]
+                turn = asked_ref[source, 0, 8 + slot]
+                outside = asked_ref[source, 0, 16 + slot]
+                begin = slot * 16
                 for c in range(2):
                     at = begin + 8 * c
-                    turn = jnp.bitwise_and(at + 1 - y_own, 127)
-                    part = pltpu.roll(surface[c, pl.ds(first, 8), :], turn, 1)
+                    part = pltpu.roll(surface[c, pl.ds(first, 8), :], jnp.bitwise_and(turn + at, 127), 1)
                     part = jnp.where(lane == at + outside, edges[c, pl.ds(first, 8), :], part)
                     message = jnp.where(lane // 8 == at // 8, part, message)
         out_ref[source] = message
@@ -229,6 +240,7 @@
         scratch_shapes=[
             pltpu.VMEM((2, rows, 128), F32),
             pltpu.VMEM((2, rows, 128), F32),
+            pltpu.VMEM((peers, 8, 128), jnp.int32),
             pltpu.SMEM((peers, 1, 128), jnp.int32),
             pltpu.SemaphoreType.DMA(()),
         ],
@@ -596,10 +608,10 @@
 def body(theta, wind_u, wind_v, level_set, fuel_load, spread_base, tile_owner, tile_place):
     peers = lax.axis_size("gx")
     owners, places = tile_owner[0, 0], tile_place[0, 0]
-    requests, near_theta, block = make_requests(owners, places, theta, wind_u, wind_v, peers)
+    requests = make_requests(owners, places, peers)
     asked = exchange(requests)
 
-    one_x, two_x, one_y, two_y = make_edges(near_theta, block)
+    block, one_x, two_x, one_y, two_y = make_edges(requests, theta, wind_u, wind_v)
     rims_y = swapped_y(one_y, two_y)
 
     patches, one_x, two_x = cut_patches(asked, block, *rims_y, one_x, two_x)

time: 57.5 us -> 57 us (level)
  waiting for transfers between devices: 9.06 us -> 8.17 us
  starting transfers between devices: 23.3 us -> 24.1 us
    all_to_all x3, starting transfers between devices: 18.1 us -> 19 us  [exchange(): return lax.all_to_all(cells, 'gx', split_axis=0, concat_axis=0, tiled=True)]
    all_to_all x3, waiting for transfers between devices: 7.45 us -> 6.57 us  [exchange(): return lax.all_to_all(cells, 'gx', split_axis=0, concat_axis=0, tiled=True)]
  transfers between devices with their start and end apart: 7 -> 7, of which waited for: 4 -> 4; matrix products, arithmetic and copies ran while one was open for 0% -> 0% of each run, Pallas kernels for 30% -> 31%
where the time goes in v9:
time: 57 us; the launch traced here: 56.7 us
  starting transfers between devices  24.1 us (42%)
  Pallas kernels  23.6 us (41%)
  waiting for transfers between devices  8.17 us (14%)
  between operations  0.73 us (1%)
    all_to_all x3, starting transfers between devices, exchange(): return lax.all_to_all(cells, 'gx', split_axis=0, concat_axis=0, tiled=True)  19 us
    pallas_call x1, Pallas kernels, fire(): pl.pallas_call(functools.partial(fire_kernel, peers, len(waits)), in_spec...  8.07 us
    all_to_all x3, waiting for transfers between devices, exchange(): return lax.all_to_all(cells, 'gx', split_axis=0, concat_axis=0, tiled=True)  6.57 us
    pallas_call x1, Pallas kernels, advect(): pl.pallas_call(advect_kernel, in_specs=[FAR] * 3 + [LOCAL] * 4, out_specs...  4.93 us
    ppermute x2, starting transfers between devices, swapped_y(): return (lax.ppermute(one, 'gy', pairs), lax.ppermute(two, 'gy', others))  3.2 us
    pallas_call x1, Pallas kernels, make_edges(): pl.pallas_call(edge_kernel, in_specs=[ANYWHERE, FAR, FAR, FAR], out_specs...  2.51 us
    pallas_call x1, Pallas kernels, prepare_tiles(): pl.pallas_call(tile_kernel, in_specs=[ANYWHERE, FAR, FAR, FAR], out_specs...  2.25 us
    pallas_call x1, Pallas kernels, finish(): pl.pallas_call(final_kernel, in_specs=[LOCAL, LOCAL], out_specs=ANYWHERE,...  2.08 us
  transfers between devices with their start and end apart: 7, of which 4 were waited for; matrix products, arithmetic and copies ran while one was open for 0% of the time, Pallas kernels for 31%

profile of v9, /device:TPU:0, one launch (start us, length us, event | category | flops | bytes accessed | tf_op | source)
XLA Modules:
  0.0 56.7 jit_solution(17388884327743935681)
XLA Ops:
  0.6 1.4 %make_requests.1.after_ref = s32[16,8,128]{2,1,0:T(8,128)} custom-call(s32[16]{0:T(128)} %bitcast.10, s32[16]{0:T(128)} %bitcast.12), custom_call_target="tpu_custom_call" | custom-call | tf_op jit(solution)/shard_map/make_requests/pallas_call | solution.py:95
  2.1 8.0 %all-to-all-start = ((s32[16,8,128]{2,1,0:T(8,128)}), s32[16,8,128]{2,1,0:T(8,128)S(1)}, u32[]{:S(2)}, u32[]{:S(2)}) async-start(s32[16,8,128]{2,1,0:T(8,128)} %make_requests.1.after_ref), calls=%async_computation | async-start | bytes 131072 | tf_op jit(solution)/shard_map/all_to_all | solution.py:605
  10.1 2.5 %edges.1 = (f32[128,128]{1,0:T(8,128)S(1)}, f32[80,128]{1,0:T(8,128)S(1)}, f32[80,128]{1,0:T(8,128)S(1)}, f32[64,128]{1,0:T(8,128)S(1)}, f32[64,128]{1,0:T(8,128)S(1)}) custom-call(s32[16,8,128]{2,1,0:T(8,128)} %make_requests.1.after_ref, f32[80,64,128]{2,1,0:T(8,128)} %theta_ref.3, f32[80,64,128]{2,1,0:T(8,128)} %u_ref.3, f32[80,64,128]{2,1,0:T(8,128)} %v_ref.3), custom_call_target="tpu_custom_call" | custom-call | flops 4000000 | bytes 2700000 | tf_op jit(solution)/shard_map/edges/pallas_call | solution.py:163
  12.6 0.1 collective-permute-start
  12.7 3.1 %collective-permute-start.1 = (f32[64,128]{1,0:T(8,128)S(1)}, f32[64,128]{1,0:T(8,128)S(1)}, u32[]{:S(2)}, u32[]{:S(2)}) collective-permute-start(f32[64,128]{1,0:T(8,128)S(1)} %get-tuple-element.19), channel_id=1, source_target_pairs={{1,2},{2,1},{3,4},{4,3},{5,6},{6,5},{7,0},{0,7},{9,10},{10,9},{11,... | collective-permute-start | bytes 98312 | tf_op jit(solution)/shard_map/ppermute | solution.py:590
  15.8 0.0 collective-permute-done.one_y_ref
  15.8 1.6 %collective-permute-done.1.two_y_ref = f32[64,128]{1,0:T(8,128)S(1)} collective-permute-done((f32[64,128]{1,0:T(8,128)S(1)}, f32[64,128]{1,0:T(8,128)S(1)}, u32[]{:S(2)}, u32[]{:S(2)}) %collective-permute-start.1) | collective-permute-done | bytes 32800 | tf_op jit(solution)/shard_map/ppermute | solution.py:590
  17.4 0.3 all-to-all-done.asked_far
  17.7 1.7 %cut_patches.1 = (f32[16,8,128]{2,1,0:T(8,128)}, f32[80,128]{1,0:T(8,128)S(1)}, f32[80,128]{1,0:T(8,128)S(1)}) custom-call(s32[16,8,128]{2,1,0:T(8,128)S(1)} %all-to-all-done.asked_far, f32[128,128]{1,0:T(8,128)S(1)} %get-tuple-element.17.block_ref, f32[64,128]{1,0:T(8,128)S(1)} %collective-permute-done.one_y_ref, ...), custom_call_target="tpu_custom_call" | custom-call | tf_op jit(solution)/shard_map/cut_patches/pallas_call | solution.py:235
  19.4 6.9 %all-to-all-start.1 = ((f32[16,8,128]{2,1,0:T(8,128)}), f32[16,8,128]{2,1,0:T(8,128)S(1)}, u32[]{:S(2)}, u32[]{:S(2)}) async-start(f32[16,8,128]{2,1,0:T(8,128)} %get-tuple-element.22.after_ref), calls=%async_computation.1 | async-start | bytes 131072 | tf_op jit(solution)/shard_map/all_to_all | solution.py:605
  26.3 1.9 %collective-permute-start.2 = (f32[80,128]{1,0:T(8,128)S(1)}, f32[80,128]{1,0:T(8,128)S(1)}, u32[]{:S(2)}, u32[]{:S(2)}) collective-permute-start(f32[80,128]{1,0:T(8,128)S(1)} %get-tuple-element.24), channel_id=1, source_target_pairs={{0,8},{8,0},{16,24},{24,16},{32,40},{40,32},{48,56},{56,48},{64,72... | collective-permute-start | bytes 122888 | tf_op jit(solution)/shard_map/ppermute | solution.py:601
  28.3 0.0 collective-permute-start.3
  28.3 2.2 %prepare_tiles.1.tile_ref = f32[16,49,8,128]{3,2,1,0:T(8,128)S(1)} custom-call(f32[16,8,128]{2,1,0:T(8,128)} %get-tuple-element.22.after_ref, f32[16,128,128]{2,1,0:T(8,128)} %bitcast.7, f32[16,128,128]{2,1,0:T(8,128)} %bitcast.8, f32[16,128,128]{2,1,0:T(8,128)} %bitcast.9), custom_call_target="tpu_custom_call" | custom-call | flops 300000 | bytes 3200000 | tf_op jit(solution)/shard_map/prepare_tiles/pallas_call | solution.py:357
  30.5 3.5 %all-to-all-done.1.winds_ref = f32[16,8,128]{2,1,0:T(8,128)S(1)} async-done(((f32[16,8,128]{2,1,0:T(8,128)}), f32[16,8,128]{2,1,0:T(8,128)S(1)}, u32[]{:S(2)}, u32[]{:S(2)}) %all-to-all-start.1) | async-done | bytes 65568 | tf_op jit(solution)/shard_map/all_to_all | solution.py:605
  34.0 8.1 %fire.1 = (f32[16,128,128]{2,1,0:T(8,128)}, f32[16,128,128]{2,1,0:T(8,128)}, f32[16,8,128]{2,1,0:T(8,128)S(1)}) custom-call(s32[16]{0:T(128)} %bitcast.11, s32[16]{0:T(128)} %bitcast.13, f32[16,8,128]{2,1,0:T(8,128)S(1)} %all-to-all-done.1.winds_ref, f32[16,49,8,128]{3,2,1,0:T(8,128)S(1)} %prepare_tiles.1.tile_ref), custom_call_target="tpu_custom_call" | custom-call | flops 50000000 | bytes 6500000 | tf_op jit(solution)/shard_map/fire/pallas_call | solution.py:487
  42.1 0.0 collective-permute-done.2.one_x_ref
  42.1 0.0 collective-permute-done.3.two_x_ref
  42.1 0.6 %sort_rows.1 = (f32[16,8,128]{2,1,0:T(8,128)}, f32[80,128]{1,0:T(8,128)S(1)}, f32[80,128]{1,0:T(8,128)S(1)}) custom-call(f32[16,8,128]{2,1,0:T(8,128)S(1)} %get-tuple-element.23.outbox_ref, f32[80,128]{1,0:T(8,128)S(1)} %collective-permute-done.2.one_x_ref, f32[80,128]{1,0:T(8,128)S(1)} %collective-permute-done.3.two_x_ref), custom_call_target="tpu_custom_call" | custom-call | tf_op jit(solution)/shard_map/sort_rows/pallas_call | solution.py:525
  42.8 4.1 %all-to-all-start.2 = ((f32[16,8,128]{2,1,0:T(8,128)}), f32[16,8,128]{2,1,0:T(8,128)S(1)}, u32[]{:S(2)}, u32[]{:S(2)}) async-start(f32[16,8,128]{2,1,0:T(8,128)} %get-tuple-element.26), calls=%async_computation.2 | async-start | bytes 131072 | tf_op jit(solution)/shard_map/all_to_all | solution.py:605
  46.9 4.9 %advect.1.part_ref = f32[80,64,128]{2,1,0:T(8,128)S(1)} custom-call(f32[80,64,128]{2,1,0:T(8,128)} %theta_ref.3, f32[80,64,128]{2,1,0:T(8,128)} %u_ref.3, f32[80,64,128]{2,1,0:T(8,128)} %v_ref.3, f32[80,128]{1,0:T(8,128)S(1)} %get-tuple-element.27.west_ref, f32[80,128]{1,0:T(8,128)S(1)} %get-tuple-element.28.east_ref, ...), custom_call_target="tpu_custom_call" | custom-call | flops 14000000 | bytes 8000000 | tf_op jit(solution)/shard_map/advect/pallas_call | solution.py:309
  51.8 2.7 %all-to-all-done.2.inbox_ref = f32[16,8,128]{2,1,0:T(8,128)S(1)} async-done(((f32[16,8,128]{2,1,0:T(8,128)}), f32[16,8,128]{2,1,0:T(8,128)S(1)}, u32[]{:S(2)}, u32[]{:S(2)}) %all-to-all-start.2) | async-done | bytes 65568 | tf_op jit(solution)/shard_map/all_to_all | solution.py:605
  54.6 2.1 %finish.1 = f32[80,64,128]{2,1,0:T(8,128)} custom-call(f32[16,8,128]{2,1,0:T(8,128)S(1)} %all-to-all-done.2.inbox_ref, f32[80,64,128]{2,1,0:T(8,128)S(1)} %advect.1.part_ref), custom_call_target="tpu_custom_call" | custom-call | flops 3000000 | bytes 2700000 | tf_op jit(solution)/shard_map/finish/pallas_call | solution.py:570
Async XLA Ops:
  2.1 15.6 %all-to-all-start = ((s32[16,8,128]{2,1,0:T(8,128)}), s32[16,8,128]{2,1,0:T(8,128)S(1)}, u32[]{:S(2)}, u32[]{:S(2)}) async-start(s32[16,8,128]{2,1,0:T(8,128)} %make_requests.1.after_ref), calls=%async_computation | async-start | bytes 131072 | tf_op jit(solution)/shard_map/all_to_all | solution.py:605
  12.6 3.2 %collective-permute-start = (f32[64,128]{1,0:T(8,128)S(1)}, f32[64,128]{1,0:T(8,128)S(1)}, u32[]{:S(2)}, u32[]{:S(2)}) collective-permute-start(f32[64,128]{1,0:T(8,128)S(1)} %get-tuple-element.18), channel_id=1, source_target_pairs={{0,1},{1,0},{2,3},{3,2},{4,5},{5,4},{6,7},{7,6},{8,9},{9,8},{10,11... | collective-permute-start | bytes 98312 | tf_op jit(solution)/shard_map/ppermute | solution.py:590
  12.7 4.7 %collective-permute-start.1 = (f32[64,128]{1,0:T(8,128)S(1)}, f32[64,128]{1,0:T(8,128)S(1)}, u32[]{:S(2)}, u32[]{:S(2)}) collective-permute-start(f32[64,128]{1,0:T(8,128)S(1)} %get-tuple-element.19), channel_id=1, source_target_pairs={{1,2},{2,1},{3,4},{4,3},{5,6},{6,5},{7,0},{0,7},{9,10},{10,9},{11,... | collective-permute-start | bytes 98312 | tf_op jit(solution)/shard_map/ppermute | solution.py:590
  19.4 14.6 %all-to-all-start.1 = ((f32[16,8,128]{2,1,0:T(8,128)}), f32[16,8,128]{2,1,0:T(8,128)S(1)}, u32[]{:S(2)}, u32[]{:S(2)}) async-start(f32[16,8,128]{2,1,0:T(8,128)} %get-tuple-element.22.after_ref), calls=%async_computation.1 | async-start | bytes 131072 | tf_op jit(solution)/shard_map/all_to_all | solution.py:605
  26.3 15.8 %collective-permute-start.2 = (f32[80,128]{1,0:T(8,128)S(1)}, f32[80,128]{1,0:T(8,128)S(1)}, u32[]{:S(2)}, u32[]{:S(2)}) collective-permute-start(f32[80,128]{1,0:T(8,128)S(1)} %get-tuple-element.24), channel_id=1, source_target_pairs={{0,8},{8,0},{16,24},{24,16},{32,40},{40,32},{48,56},{56,48},{64,72... | collective-permute-start | bytes 122888 | tf_op jit(solution)/shard_map/ppermute | solution.py:601
  28.3 13.8 %collective-permute-start.3 = (f32[80,128]{1,0:T(8,128)S(1)}, f32[80,128]{1,0:T(8,128)S(1)}, u32[]{:S(2)}, u32[]{:S(2)}) collective-permute-start(f32[80,128]{1,0:T(8,128)S(1)} %get-tuple-element.25), channel_id=1, source_target_pairs={{0,1},{1,0},{2,3},{3,2},{4,5},{5,4},{6,7},{7,6},{8,16},{9,17},{10,... | collective-permute-start | bytes 122888 | tf_op jit(solution)/shard_map/ppermute | solution.py:601
  42.8 11.8 %all-to-all-start.2 = ((f32[16,8,128]{2,1,0:T(8,128)}), f32[16,8,128]{2,1,0:T(8,128)S(1)}, u32[]{:S(2)}, u32[]{:S(2)}) async-start(f32[16,8,128]{2,1,0:T(8,128)} %get-tuple-element.26), calls=%async_computation.2 | async-start | bytes 131072 | tf_op jit(solution)/shard_map/all_to_all | solution.py:605

commit v10 on v9

--- a/solution.py
+++ b/solution.py
@@ -22,6 +22,7 @@
 WIND = 100
 GROUP = 8
 GROUPS = LZ // GROUP
+HEAD = 24
 SIDE = 4
 AHEAD = 2
 
@@ -74,8 +75,14 @@
     return ranks
 
 
-def request_kernel(owner_far, place_far, out_ref, owner_ref, place_ref, table, count, sems):
-    to_scalars((owner_far, place_far), (owner_ref, place_ref), sems)
+def request_kernel(
+    owner_far, place_far, theta_ref, u_ref, v_ref, out_ref, head_ref, block_ref,
+    owner_ref, place_ref, table, count, sems, far_sems,
+):
+    pairs = [(ref.at[0], block_ref.at[c * CX : (c + 1) * CX]) for c, ref in enumerate((u_ref, v_ref))]
+    pairs.append((theta_ref.at[0:HEAD], head_ref))
+    others = [pltpu.make_async_copy(source, target, far_sems.at[i]) for i, (source, target) in enumerate(pairs)]
+    to_scalars((owner_far, place_far), (owner_ref, place_ref), sems, others)
     peers = out_ref.shape[0]
     for i in range((peers + 2) * CAP):
         table[i] = -1
@@ -89,24 +96,31 @@
             for r in range(CAP):
                 line = jnp.where(lane % 8 == g * CAP + r, table[(peer + 1 + side) * CAP + r], line)
         out_ref[peer] = jnp.broadcast_to(line, (8, 128))
-
-
-def make_requests(owners, places, peers):
+    for copy in others:
+        copy.wait()
+
+
+def make_requests(owners, places, theta, wind_u, wind_v, peers):
     return pl.pallas_call(
         request_kernel,
-        in_specs=[FAR, FAR],
-        out_specs=LOCAL,
-        out_shape=pltpu.VMEM((peers, 8, 128), jnp.int32),
+        in_specs=[FAR] * 5,
+        out_specs=[LOCAL] * 3,
+        out_shape=[
+            pltpu.VMEM((peers, 8, 128), jnp.int32),
+            pltpu.VMEM((HEAD, CX, CY), F32),
+            pltpu.VMEM((2 * CX, 128), F32),
+        ],
         scratch_shapes=[
             pltpu.SMEM((TPD,), jnp.int32),
             pltpu.SMEM((TPD,), jnp.int32),
             pltpu.SMEM(((peers + 2) * CAP,), jnp.int32),
             pltpu.SMEM((peers,), jnp.int32),
             pltpu.SemaphoreType.DMA((2,)),
+            pltpu.SemaphoreType.DMA((3,)),
         ],
         name="make_requests",
         compiler_params=params(4),
-    )(far(owners), far(places))
+    )(*(far(a) for a in (owners, places, theta, wind_u, wind_v)))
 
 
 def place_on(axis):
@@ -115,40 +129,30 @@
     return even, jnp.logical_or(index == 0, index == lax.axis_size(axis) - 1)
 
 
-def edge_kernel(
-    after_ref, theta_ref, u_ref, v_ref,
-    block_ref, one_x_ref, two_x_ref, one_y_ref, two_y_ref, theta, sems, wind_sems,
-):
+def edge_kernel(head_ref, block_ref, theta_ref, one_x_ref, two_x_ref, one_y_ref, two_y_ref, theta, sems):
     even_x, wraps_x = place_on("gx")
     even_y, wraps_y = place_on("gy")
 
-    def copy(g):
-        part = pl.ds(g * GROUP, GROUP)
-        return pltpu.make_async_copy(theta_ref.at[part], theta.at[part], sems.at[g])
-
-    winds = [
-        pltpu.make_async_copy(ref.at[0], block_ref.at[c * CX : (c + 1) * CX], wind_sems.at[c])
-        for c, ref in enumerate((u_ref, v_ref))
-    ]
-    for g in range(GROUPS):
-        copy(g).start()
-    for wind in winds:
-        wind.start()
+    def copy(z):
+        return pltpu.make_async_copy(
+            theta_ref.at[z : z + GROUP], theta.at[z - HEAD : z - HEAD + GROUP], sems.at[(z - HEAD) // GROUP]
+        )
+
+    for z in range(HEAD, LZ, GROUP):
+        copy(z).start()
     lane = iota(1, (CX, 128))
 
     first = last = jnp.zeros((CX, 128), F32)
     for z in range(LZ):
-        if z % GROUP == 0:
-            copy(z // GROUP).wait()
-        cells = theta[z]
+        if z >= HEAD and z % GROUP == 0:
+            copy(z).wait()
+        cells = head_ref[z] if z < HEAD else theta[z - HEAD]
         low, high = cells[0:1], cells[CX - 1 : CX]
         one_x_ref[z : z + 1] = jnp.where(even_x, high, low)
         two_x_ref[z : z + 1] = jnp.where(wraps_x, 0.0, jnp.where(even_x, low, high))
         turned = pltpu.roll(cells, z + 1, 1)
         first = jnp.where(lane == z + 1, turned, first)
         last = jnp.where(lane == z, turned, last)
-    for wind in winds:
-        wind.wait()
     for c in range(2):
         cells = block_ref[c * CX : (c + 1) * CX]
         first = jnp.where(lane == WIND + c, pltpu.roll(cells, WIND + c, 1), first)
@@ -157,23 +161,22 @@
     two_y_ref[...] = jnp.where(wraps_y, 0.0, jnp.where(even_y, first, last))
 
 
-def make_edges(after, theta, wind_u, wind_v):
+def make_edges(head, block, theta):
     row = pltpu.VMEM((LZ, 128), F32)
     column = pltpu.VMEM((CX, 128), F32)
     return pl.pallas_call(
         edge_kernel,
-        in_specs=[ANYWHERE, FAR, FAR, FAR],
-        out_specs=[LOCAL] * 5,
-        out_shape=[pltpu.VMEM((2 * CX, 128), F32), row, row, column, column],
+        in_specs=[LOCAL, LOCAL, FAR],
+        out_specs=[LOCAL] * 4,
+        out_shape=[row, row, column, column],
         scratch_shapes=[
-            pltpu.VMEM((LZ, CX, CY), F32),
-            pltpu.SemaphoreType.DMA((GROUPS,)),
-            pltpu.SemaphoreType.DMA((2,)),
+            pltpu.VMEM((LZ - HEAD, CX, CY), F32),
+            pltpu.SemaphoreType.DMA(((LZ - HEAD) // GROUP,)),
         ],
         name="edges",
         compiler_params=params(8),
         cost_estimate=pl.CostEstimate(flops=4_000_000, bytes_accessed=2_700_000, transcendentals=0),
-    )(after, far(theta), far(wind_u), far(wind_v))
+    )(near(head), near(block), far(theta))
 
 
 def cut_kernel(
@@ -608,10 +611,10 @@
 def body(theta, wind_u, wind_v, level_set, fuel_load, spread_base, tile_owner, tile_place):
     peers = lax.axis_size("gx")
     owners, places = tile_owner[0, 0], tile_place[0, 0]
-    requests = make_requests(owners, places, peers)
+    requests, head, block = make_requests(owners, places, theta, wind_u, wind_v, peers)
     asked = exchange(requests)
 
-    block, one_x, two_x, one_y, two_y = make_edges(requests, theta, wind_u, wind_v)
+    one_x, two_x, one_y, two_y = make_edges(head, block, theta)
     rims_y = swapped_y(one_y, two_y)
 
     patches, one_x, two_x = cut_patches(asked, block, *rims_y, one_x, two_x)

time: 57 us -> 57 us (level)
  no operation moved by 1% of the time
where the time goes in v10:
time: 57 us; the launch traced here: 56.6 us
  starting transfers between devices  23.7 us (42%)
  Pallas kernels  23.6 us (41%)
  waiting for transfers between devices  8.62 us (15%)
  between operations  0.73 us (1%)
    all_to_all x3, starting transfers between devices, exchange(): return lax.all_to_all(cells, 'gx', split_axis=0, concat_axis=0, tiled=True)  18.6 us
    pallas_call x1, Pallas kernels, fire(): pl.pallas_call(functools.partial(fire_kernel, peers, len(waits)), in_spec...  8.07 us
    all_to_all x3, waiting for transfers between devices, exchange(): return lax.all_to_all(cells, 'gx', split_axis=0, concat_axis=0, tiled=True)  7.02 us
    pallas_call x1, Pallas kernels, advect(): pl.pallas_call(advect_kernel, in_specs=[FAR] * 3 + [LOCAL] * 4, out_specs...  4.93 us
    ppermute x2, starting transfers between devices, swapped_y(): return (lax.ppermute(one, 'gy', pairs), lax.ppermute(two, 'gy', others))  3.2 us
    pallas_call x1, Pallas kernels, prepare_tiles(): pl.pallas_call(tile_kernel, in_specs=[ANYWHERE, FAR, FAR, FAR], out_specs...  2.25 us
    pallas_call x1, Pallas kernels, finish(): pl.pallas_call(final_kernel, in_specs=[LOCAL, LOCAL], out_specs=ANYWHERE,...  2.08 us
    pallas_call x1, Pallas kernels, make_edges(): pl.pallas_call(edge_kernel, in_specs=[LOCAL, LOCAL, FAR], out_specs=[LOCA...  2.06 us
  transfers between devices with their start and end apart: 7, of which 4 were waited for; matrix products, arithmetic and copies ran while one was open for 0% of the time, Pallas kernels for 31%

profile of v10, /device:TPU:0, one launch (start us, length us, event | category | flops | bytes accessed | tf_op | source)
XLA Modules:
  0.0 56.6 jit_solution(9281388938511657165)
XLA Ops:
  0.6 1.8 %make_requests.1 = (s32[16,8,128]{2,1,0:T(8,128)}, f32[24,64,128]{2,1,0:T(8,128)S(1)}, f32[128,128]{1,0:T(8,128)S(1)}) custom-call(s32[16]{0:T(128)} %bitcast.10, s32[16]{0:T(128)} %bitcast.12, f32[80,64,128]{2,1,0:T(8,128)} %theta_ref.5, f32[80,64,128]{2,1,0:T(8,128)} %u_ref.3, f32[80,64,128]{2,1,0:T(8,128)} %v_ref.3), custom_call_target="tpu_custom_call" | custom-call | tf_op jit(solution)/shard_map/make_requests/pallas_call | solution.py:104
  2.5 8.0 %all-to-all-start = ((s32[16,8,128]{2,1,0:T(8,128)}), s32[16,8,128]{2,1,0:T(8,128)S(1)}, u32[]{:S(2)}, u32[]{:S(2)}) async-start(s32[16,8,128]{2,1,0:T(8,128)} %get-tuple-element.19), calls=%async_computation | async-start | bytes 131072 | tf_op jit(solution)/shard_map/all_to_all | solution.py:608
  10.5 2.1 %edges.1 = (f32[80,128]{1,0:T(8,128)S(1)}, f32[80,128]{1,0:T(8,128)S(1)}, f32[64,128]{1,0:T(8,128)S(1)}, f32[64,128]{1,0:T(8,128)S(1)}) custom-call(f32[24,64,128]{2,1,0:T(8,128)S(1)} %get-tuple-element.21.head_ref, f32[128,128]{1,0:T(8,128)S(1)} %get-tuple-element.20.block_ref, f32[80,64,128]{2,1,0:T(8,128)} %theta_ref.5), custom_call_target="tpu_custom_call" | custom-call | flops 4000000 | bytes 2700000 | tf_op jit(solution)/shard_map/edges/pallas_call | solution.py:167
  12.5 0.1 collective-permute-start
  12.6 3.1 %collective-permute-start.1 = (f32[64,128]{1,0:T(8,128)S(1)}, f32[64,128]{1,0:T(8,128)S(1)}, u32[]{:S(2)}, u32[]{:S(2)}) collective-permute-start(f32[64,128]{1,0:T(8,128)S(1)} %get-tuple-element.23), channel_id=1, source_target_pairs={{1,2},{2,1},{3,4},{4,3},{5,6},{6,5},{7,0},{0,7},{9,10},{10,9},{11,... | collective-permute-start | bytes 98312 | tf_op jit(solution)/shard_map/ppermute | solution.py:593
  15.7 0.0 collective-permute-done.one_y_ref
  15.7 1.6 %collective-permute-done.1.two_y_ref = f32[64,128]{1,0:T(8,128)S(1)} collective-permute-done((f32[64,128]{1,0:T(8,128)S(1)}, f32[64,128]{1,0:T(8,128)S(1)}, u32[]{:S(2)}, u32[]{:S(2)}) %collective-permute-start.1) | collective-permute-done | bytes 32800 | tf_op jit(solution)/shard_map/ppermute | solution.py:593
  17.3 0.8 %all-to-all-done.asked_far = s32[16,8,128]{2,1,0:T(8,128)S(1)} async-done(((s32[16,8,128]{2,1,0:T(8,128)}), s32[16,8,128]{2,1,0:T(8,128)S(1)}, u32[]{:S(2)}, u32[]{:S(2)}) %all-to-all-start) | async-done | bytes 65568 | tf_op jit(solution)/shard_map/all_to_all | solution.py:608
  18.1 1.7 %cut_patches.1 = (f32[16,8,128]{2,1,0:T(8,128)}, f32[80,128]{1,0:T(8,128)S(1)}, f32[80,128]{1,0:T(8,128)S(1)}) custom-call(s32[16,8,128]{2,1,0:T(8,128)S(1)} %all-to-all-done.asked_far, f32[128,128]{1,0:T(8,128)S(1)} %get-tuple-element.20.block_ref, f32[64,128]{1,0:T(8,128)S(1)} %collective-permute-done.one_y_ref, ...), custom_call_target="tpu_custom_call" | custom-call | tf_op jit(solution)/shard_map/cut_patches/pallas_call | solution.py:238
  19.8 6.4 %all-to-all-start.1 = ((f32[16,8,128]{2,1,0:T(8,128)}), f32[16,8,128]{2,1,0:T(8,128)S(1)}, u32[]{:S(2)}, u32[]{:S(2)}) async-start(f32[16,8,128]{2,1,0:T(8,128)} %get-tuple-element.26.after_ref), calls=%async_computation.1 | async-start | bytes 131072 | tf_op jit(solution)/shard_map/all_to_all | solution.py:608
  26.3 1.9 %collective-permute-start.2 = (f32[80,128]{1,0:T(8,128)S(1)}, f32[80,128]{1,0:T(8,128)S(1)}, u32[]{:S(2)}, u32[]{:S(2)}) collective-permute-start(f32[80,128]{1,0:T(8,128)S(1)} %get-tuple-element.28), channel_id=1, source_target_pairs={{0,8},{8,0},{16,24},{24,16},{32,40},{40,32},{48,56},{56,48},{64,72... | collective-permute-start | bytes 122888 | tf_op jit(solution)/shard_map/ppermute | solution.py:604
  28.2 0.0 collective-permute-start.3
  28.2 2.2 %prepare_tiles.1.tile_ref = f32[16,49,8,128]{3,2,1,0:T(8,128)S(1)} custom-call(f32[16,8,128]{2,1,0:T(8,128)} %get-tuple-element.26.after_ref, f32[16,128,128]{2,1,0:T(8,128)} %bitcast.7, f32[16,128,128]{2,1,0:T(8,128)} %bitcast.8, f32[16,128,128]{2,1,0:T(8,128)} %bitcast.9), custom_call_target="tpu_custom_call" | custom-call | flops 300000 | bytes 3200000 | tf_op jit(solution)/shard_map/prepare_tiles/pallas_call | solution.py:360
  30.5 3.5 %all-to-all-done.1.winds_ref = f32[16,8,128]{2,1,0:T(8,128)S(1)} async-done(((f32[16,8,128]{2,1,0:T(8,128)}), f32[16,8,128]{2,1,0:T(8,128)S(1)}, u32[]{:S(2)}, u32[]{:S(2)}) %all-to-all-start.1) | async-done | bytes 65568 | tf_op jit(solution)/shard_map/all_to_all | solution.py:608
  34.0 8.1 %fire.1 = (f32[16,128,128]{2,1,0:T(8,128)}, f32[16,128,128]{2,1,0:T(8,128)}, f32[16,8,128]{2,1,0:T(8,128)S(1)}) custom-call(s32[16]{0:T(128)} %bitcast.11, s32[16]{0:T(128)} %bitcast.13, f32[16,8,128]{2,1,0:T(8,128)S(1)} %all-to-all-done.1.winds_ref, f32[16,49,8,128]{3,2,1,0:T(8,128)S(1)} %prepare_tiles.1.tile_ref), custom_call_target="tpu_custom_call" | custom-call | flops 50000000 | bytes 6500000 | tf_op jit(solution)/shard_map/fire/pallas_call | solution.py:490
  42.1 0.0 collective-permute-done.2.one_x_ref
  42.1 0.0 collective-permute-done.3.two_x_ref
  42.1 0.6 %sort_rows.1 = (f32[16,8,128]{2,1,0:T(8,128)}, f32[80,128]{1,0:T(8,128)S(1)}, f32[80,128]{1,0:T(8,128)S(1)}) custom-call(f32[16,8,128]{2,1,0:T(8,128)S(1)} %get-tuple-element.27.outbox_ref, f32[80,128]{1,0:T(8,128)S(1)} %collective-permute-done.2.one_x_ref, f32[80,128]{1,0:T(8,128)S(1)} %collective-permute-done.3.two_x_ref), custom_call_target="tpu_custom_call" | custom-call | tf_op jit(solution)/shard_map/sort_rows/pallas_call | solution.py:528
  42.7 4.1 %all-to-all-start.2 = ((f32[16,8,128]{2,1,0:T(8,128)}), f32[16,8,128]{2,1,0:T(8,128)S(1)}, u32[]{:S(2)}, u32[]{:S(2)}) async-start(f32[16,8,128]{2,1,0:T(8,128)} %get-tuple-element.30), calls=%async_computation.2 | async-start | bytes 131072 | tf_op jit(solution)/shard_map/all_to_all | solution.py:608
  46.9 4.9 %advect.1.part_ref = f32[80,64,128]{2,1,0:T(8,128)S(1)} custom-call(f32[80,64,128]{2,1,0:T(8,128)} %theta_ref.5, f32[80,64,128]{2,1,0:T(8,128)} %u_ref.3, f32[80,64,128]{2,1,0:T(8,128)} %v_ref.3, f32[80,128]{1,0:T(8,128)S(1)} %get-tuple-element.31.west_ref, f32[80,128]{1,0:T(8,128)S(1)} %get-tuple-element.32.east_ref, ...), custom_call_target="tpu_custom_call" | custom-call | flops 14000000 | bytes 8000000 | tf_op jit(solution)/shard_map/advect/pallas_call | solution.py:312
  51.8 2.7 %all-to-all-done.2.inbox_ref = f32[16,8,128]{2,1,0:T(8,128)S(1)} async-done(((f32[16,8,128]{2,1,0:T(8,128)}), f32[16,8,128]{2,1,0:T(8,128)S(1)}, u32[]{:S(2)}, u32[]{:S(2)}) %all-to-all-start.2) | async-done | bytes 65568 | tf_op jit(solution)/shard_map/all_to_all | solution.py:608
  54.5 2.1 %finish.1 = f32[80,64,128]{2,1,0:T(8,128)} custom-call(f32[16,8,128]{2,1,0:T(8,128)S(1)} %all-to-all-done.2.inbox_ref, f32[80,64,128]{2,1,0:T(8,128)S(1)} %advect.1.part_ref), custom_call_target="tpu_custom_call" | custom-call | flops 3000000 | bytes 2700000 | tf_op jit(solution)/shard_map/finish/pallas_call | solution.py:573
Async XLA Ops:
  2.5 15.6 %all-to-all-start = ((s32[16,8,128]{2,1,0:T(8,128)}), s32[16,8,128]{2,1,0:T(8,128)S(1)}, u32[]{:S(2)}, u32[]{:S(2)}) async-start(s32[16,8,128]{2,1,0:T(8,128)} %get-tuple-element.19), calls=%async_computation | async-start | bytes 131072 | tf_op jit(solution)/shard_map/all_to_all | solution.py:608
  12.5 3.2 %collective-permute-start = (f32[64,128]{1,0:T(8,128)S(1)}, f32[64,128]{1,0:T(8,128)S(1)}, u32[]{:S(2)}, u32[]{:S(2)}) collective-permute-start(f32[64,128]{1,0:T(8,128)S(1)} %get-tuple-element.22), channel_id=1, source_target_pairs={{0,1},{1,0},{2,3},{3,2},{4,5},{5,4},{6,7},{7,6},{8,9},{9,8},{10,11... | collective-permute-start | bytes 98312 | tf_op jit(solution)/shard_map/ppermute | solution.py:593
  12.6 4.7 %collective-permute-start.1 = (f32[64,128]{1,0:T(8,128)S(1)}, f32[64,128]{1,0:T(8,128)S(1)}, u32[]{:S(2)}, u32[]{:S(2)}) collective-permute-start(f32[64,128]{1,0:T(8,128)S(1)} %get-tuple-element.23), channel_id=1, source_target_pairs={{1,2},{2,1},{3,4},{4,3},{5,6},{6,5},{7,0},{0,7},{9,10},{10,9},{11,... | collective-permute-start | bytes 98312 | tf_op jit(solution)/shard_map/ppermute | solution.py:593
  19.8 14.1 %all-to-all-start.1 = ((f32[16,8,128]{2,1,0:T(8,128)}), f32[16,8,128]{2,1,0:T(8,128)S(1)}, u32[]{:S(2)}, u32[]{:S(2)}) async-start(f32[16,8,128]{2,1,0:T(8,128)} %get-tuple-element.26.after_ref), calls=%async_computation.1 | async-start | bytes 131072 | tf_op jit(solution)/shard_map/all_to_all | solution.py:608
  26.3 15.8 %collective-permute-start.2 = (f32[80,128]{1,0:T(8,128)S(1)}, f32[80,128]{1,0:T(8,128)S(1)}, u32[]{:S(2)}, u32[]{:S(2)}) collective-permute-start(f32[80,128]{1,0:T(8,128)S(1)} %get-tuple-element.28), channel_id=1, source_target_pairs={{0,8},{8,0},{16,24},{24,16},{32,40},{40,32},{48,56},{56,48},{64,72... | collective-permute-start | bytes 122888 | tf_op jit(solution)/shard_map/ppermute | solution.py:604
  28.2 13.8 %collective-permute-start.3 = (f32[80,128]{1,0:T(8,128)S(1)}, f32[80,128]{1,0:T(8,128)S(1)}, u32[]{:S(2)}, u32[]{:S(2)}) collective-permute-start(f32[80,128]{1,0:T(8,128)S(1)} %get-tuple-element.29), channel_id=1, source_target_pairs={{0,1},{1,0},{2,3},{3,2},{4,5},{5,4},{6,7},{7,6},{8,16},{9,17},{10,... | collective-permute-start | bytes 122888 | tf_op jit(solution)/shard_map/ppermute | solution.py:604
  42.7 11.8 %all-to-all-start.2 = ((f32[16,8,128]{2,1,0:T(8,128)}), f32[16,8,128]{2,1,0:T(8,128)S(1)}, u32[]{:S(2)}, u32[]{:S(2)}) async-start(f32[16,8,128]{2,1,0:T(8,128)} %get-tuple-element.30), calls=%async_computation.2 | async-start | bytes 131072 | tf_op jit(solution)/shard_map/all_to_all | solution.py:608

commit v11 on v10

--- a/solution.py
+++ b/solution.py
@@ -64,20 +64,13 @@
         copy.wait()
 
 
-def ranks_of(owner_ref, count, peers):
-    for d in range(peers):
-        count[d] = 0
-    ranks = []
-    for t in range(TPD):
-        owner = owner_ref[t]
-        ranks.append(count[owner])
-        count[owner] = ranks[t] + 1
-    return ranks
+def ranks_of(owners):
+    return [sum((jnp.where(owners[s] == owners[t], 1, 0) for s in range(t)), jnp.int32(0)) for t in range(TPD)]
 
 
 def request_kernel(
     owner_far, place_far, theta_ref, u_ref, v_ref, out_ref, head_ref, block_ref,
-    owner_ref, place_ref, table, count, sems, far_sems,
+    owner_ref, place_ref, table, sems, far_sems,
 ):
     pairs = [(ref.at[0], block_ref.at[c * CX : (c + 1) * CX]) for c, ref in enumerate((u_ref, v_ref))]
     pairs.append((theta_ref.at[0:HEAD], head_ref))
@@ -86,7 +79,7 @@
     peers = out_ref.shape[0]
     for i in range((peers + 2) * CAP):
         table[i] = -1
-    ranks = ranks_of(owner_ref, count, peers)
+    ranks = ranks_of([owner_ref[t] for t in range(TPD)])
     for t in range(TPD):
         table[(owner_ref[t] + 1) * CAP + ranks[t]] = place_ref[t]
     lane = iota(1, (1, 128))
@@ -114,7 +107,6 @@
             pltpu.SMEM((TPD,), jnp.int32),
             pltpu.SMEM((TPD,), jnp.int32),
             pltpu.SMEM(((peers + 2) * CAP,), jnp.int32),
-            pltpu.SMEM((peers,), jnp.int32),
             pltpu.SemaphoreType.DMA((2,)),
             pltpu.SemaphoreType.DMA((3,)),
         ],
@@ -370,11 +362,11 @@
 
 
 def fire_kernel(
-    peers, waits, owner_far, place_far, winds_ref, tile_ref, *rest
+    peers, waits, owner_vec, place_vec, winds_ref, tile_ref, *rest
 ):
     (
         level_out, fuel_out, outbox, begins, slopes, heats,
-        level_own, fuel_own, owner_ref, place_ref, count, scalar_sems, out_sems,
+        level_own, fuel_own, out_sems,
     ) = rest[waits:]
     lane = iota(1)
     row = iota(0)
@@ -387,7 +379,9 @@
             for c, (source, target) in enumerate(pairs)
         ]
 
-    to_scalars((owner_far, place_far), (owner_ref, place_ref), scalar_sems)
+    owner_all, place_all = owner_vec[...], place_vec[...]
+    owners = [owner_all[t] for t in range(TPD)]
+    places = [place_all[t] for t in range(TPD)]
 
     tiles_y = CY // TA
     low_row = (row + 1) // 2
@@ -395,10 +389,10 @@
     part_row = jnp.where(row % 2 == 0, 0.5, 0.0) + 0.5 / R
     part_lane = (lane.astype(F32) + 0.5) / R + 0.5 - low_lane.astype(F32)
 
-    ranks = ranks_of(owner_ref, count, peers)
+    ranks = ranks_of(owners)
     patches = []
     for t in range(TPD):
-        owner = owner_ref[t]
+        owner = owners[t]
         parts = []
         for g, side in enumerate(SIDES):
             begin = (g * CAP + ranks[t]) * 16
@@ -473,13 +467,13 @@
         [jnp.sum(jnp.where(lane // R == b, h, 0.0), axis=1, keepdims=True) for b in range(TA)] for h in pairs
     ]
     for t in range(TPD):
-        place = place_ref[t]
+        place = places[t]
         x_own = place // tiles_y * TA
         y_own = lax.rem(place, tiles_y) * TA
         message = jnp.where(lane == TA, (x_own + row).astype(F32), y_own.astype(F32))
         for b in range(TA):
             message = jnp.where(lane == b, sums[t][b], message)
-        outbox[owner_ref[t], pl.ds(ranks[t] * TA, TA), :] = message[0:TA]
+        outbox[owners[t], pl.ds(ranks[t] * TA, TA), :] = message[0:TA]
     for i in range(TPD // SIDE):
         for copy in results(i):
             copy.wait()
@@ -489,7 +483,7 @@
     tiles = (TPD, S, S)
     return pl.pallas_call(
         functools.partial(fire_kernel, peers, len(waits)),
-        in_specs=[FAR, FAR, LOCAL, LOCAL] + [ANYWHERE] * len(waits),
+        in_specs=[LOCAL] * 4 + [ANYWHERE] * len(waits),
         out_specs=[ANYWHERE, ANYWHERE, LOCAL],
         out_shape=[
             jax.ShapeDtypeStruct(tiles, F32),
@@ -502,10 +496,6 @@
             pltpu.VMEM((TPD, 8, 128), F32),
             pltpu.VMEM(tiles, F32),
             pltpu.VMEM(tiles, F32),
-            pltpu.SMEM((TPD,), jnp.int32),
-            pltpu.SMEM((TPD,), jnp.int32),
-            pltpu.SMEM((peers,), jnp.int32),
-            pltpu.SemaphoreType.DMA((2,)),
             pltpu.SemaphoreType.DMA((2, TPD // SIDE)),
         ],
         name="fire",
@@ -513,7 +503,7 @@
         cost_estimate=pl.CostEstimate(
             flops=50_000_000, bytes_accessed=6_500_000, transcendentals=3_200_000
         ),
-    )(far(owners), far(places), near(winds), near(tiles_near), *waits)
+    )(*(near(a) for a in (owners, places, winds, tiles_near)), *waits)
 
 
 def row_kernel(outbox_ref, one_x_ref, two_x_ref, outbox_out, west_ref, east_ref):

time: 57 us -> 56.5 us (level)
  transfers between devices with their start and end apart: 7 -> 7, of which waited for: 4 -> 4; matrix products, arithmetic and copies ran while one was open for 0% -> 0% of each run, Pallas kernels for 31% -> 30%
where the time goes in v11:
time: 56.5 us; the launch traced here: 56.1 us
  starting transfers between devices  23.7 us (42%)
  Pallas kernels  23.1 us (41%)
  waiting for transfers between devices  8.59 us (15%)
  between operations  0.73 us (1%)
    all_to_all x3, starting transfers between devices, exchange(): return lax.all_to_all(cells, 'gx', split_axis=0, concat_axis=0, tiled=True)  18.6 us
    pallas_call x1, Pallas kernels, fire(): pl.pallas_call(functools.partial(fire_kernel, peers, len(waits)), in_spec...  7.54 us
    all_to_all x3, waiting for transfers between devices, exchange(): return lax.all_to_all(cells, 'gx', split_axis=0, concat_axis=0, tiled=True)  6.99 us
    pallas_call x1, Pallas kernels, advect(): pl.pallas_call(advect_kernel, in_specs=[FAR] * 3 + [LOCAL] * 4, out_specs...  4.93 us
    ppermute x2, starting transfers between devices, swapped_y(): return (lax.ppermute(one, 'gy', pairs), lax.ppermute(two, 'gy', others))  3.2 us
    pallas_call x1, Pallas kernels, prepare_tiles(): pl.pallas_call(tile_kernel, in_specs=[ANYWHERE, FAR, FAR, FAR], out_specs...  2.27 us
    pallas_call x1, Pallas kernels, finish(): pl.pallas_call(final_kernel, in_specs=[LOCAL, LOCAL], out_specs=ANYWHERE,...  2.08 us
    pallas_call x1, Pallas kernels, make_edges(): pl.pallas_call(edge_kernel, in_specs=[LOCAL, LOCAL, FAR], out_specs=[LOCA...  2.06 us
  transfers between devices with their start and end apart: 7, of which 4 were waited for; matrix products, arithmetic and copies ran while one was open for 0% of the time, Pallas kernels for 30%

profile of v11, /device:TPU:0, one launch (start us, length us, event | category | flops | bytes accessed | tf_op | source)
XLA Modules:
  0.0 56.1 jit_solution(16940195812512386303)
XLA Ops:
  0.6 1.8 %make_requests.1 = (s32[16,8,128]{2,1,0:T(8,128)}, f32[24,64,128]{2,1,0:T(8,128)S(1)}, f32[128,128]{1,0:T(8,128)S(1)}) custom-call(s32[16]{0:T(128)} %bitcast.7, s32[16]{0:T(128)} %bitcast.9, f32[80,64,128]{2,1,0:T(8,128)} %theta_ref.5, f32[80,64,128]{2,1,0:T(8,128)} %u_ref.3, f32[80,64,128]{2,1,0:T(8,128)} %v_ref.3), custom_call_target="tpu_custom_call" | custom-call | tf_op jit(solution)/shard_map/make_requests/pallas_call | solution.py:97
  2.5 8.0 %all-to-all-start = ((s32[16,8,128]{2,1,0:T(8,128)}), s32[16,8,128]{2,1,0:T(8,128)S(1)}, u32[]{:S(2)}, u32[]{:S(2)}) async-start(s32[16,8,128]{2,1,0:T(8,128)} %get-tuple-element.19), calls=%async_computation | async-start | bytes 131072 | tf_op jit(solution)/shard_map/all_to_all | solution.py:598
  10.5 2.1 %edges.1 = (f32[80,128]{1,0:T(8,128)S(1)}, f32[80,128]{1,0:T(8,128)S(1)}, f32[64,128]{1,0:T(8,128)S(1)}, f32[64,128]{1,0:T(8,128)S(1)}) custom-call(f32[24,64,128]{2,1,0:T(8,128)S(1)} %get-tuple-element.21.head_ref, f32[128,128]{1,0:T(8,128)S(1)} %get-tuple-element.20.block_ref, f32[80,64,128]{2,1,0:T(8,128)} %theta_ref.5), custom_call_target="tpu_custom_call" | custom-call | flops 4000000 | bytes 2700000 | tf_op jit(solution)/shard_map/edges/pallas_call | solution.py:159
  12.5 0.1 collective-permute-start
  12.6 3.1 %collective-permute-start.1 = (f32[64,128]{1,0:T(8,128)S(1)}, f32[64,128]{1,0:T(8,128)S(1)}, u32[]{:S(2)}, u32[]{:S(2)}) collective-permute-start(f32[64,128]{1,0:T(8,128)S(1)} %get-tuple-element.23), channel_id=1, source_target_pairs={{1,2},{2,1},{3,4},{4,3},{5,6},{6,5},{7,0},{0,7},{9,10},{10,9},{11,... | collective-permute-start | bytes 98312 | tf_op jit(solution)/shard_map/ppermute | solution.py:583
  15.7 0.0 collective-permute-done.one_y_ref
  15.7 1.6 %collective-permute-done.1.two_y_ref = f32[64,128]{1,0:T(8,128)S(1)} collective-permute-done((f32[64,128]{1,0:T(8,128)S(1)}, f32[64,128]{1,0:T(8,128)S(1)}, u32[]{:S(2)}, u32[]{:S(2)}) %collective-permute-start.1) | collective-permute-done | bytes 32800 | tf_op jit(solution)/shard_map/ppermute | solution.py:583
  17.3 0.8 %all-to-all-done.asked_far = s32[16,8,128]{2,1,0:T(8,128)S(1)} async-done(((s32[16,8,128]{2,1,0:T(8,128)}), s32[16,8,128]{2,1,0:T(8,128)S(1)}, u32[]{:S(2)}, u32[]{:S(2)}) %all-to-all-start) | async-done | bytes 65568 | tf_op jit(solution)/shard_map/all_to_all | solution.py:598
  18.1 1.7 %cut_patches.1 = (f32[16,8,128]{2,1,0:T(8,128)}, f32[80,128]{1,0:T(8,128)S(1)}, f32[80,128]{1,0:T(8,128)S(1)}) custom-call(s32[16,8,128]{2,1,0:T(8,128)S(1)} %all-to-all-done.asked_far, f32[128,128]{1,0:T(8,128)S(1)} %get-tuple-element.20.block_ref, f32[64,128]{1,0:T(8,128)S(1)} %collective-permute-done.one_y_ref, ...), custom_call_target="tpu_custom_call" | custom-call | tf_op jit(solution)/shard_map/cut_patches/pallas_call | solution.py:230
  19.8 6.4 %all-to-all-start.1 = ((f32[16,8,128]{2,1,0:T(8,128)}), f32[16,8,128]{2,1,0:T(8,128)S(1)}, u32[]{:S(2)}, u32[]{:S(2)}) async-start(f32[16,8,128]{2,1,0:T(8,128)} %get-tuple-element.26.after_ref), calls=%async_computation.1 | async-start | bytes 131072 | tf_op jit(solution)/shard_map/all_to_all | solution.py:598
  26.3 1.9 %collective-permute-start.2 = (f32[80,128]{1,0:T(8,128)S(1)}, f32[80,128]{1,0:T(8,128)S(1)}, u32[]{:S(2)}, u32[]{:S(2)}) collective-permute-start(f32[80,128]{1,0:T(8,128)S(1)} %get-tuple-element.28), channel_id=1, source_target_pairs={{0,8},{8,0},{16,24},{24,16},{32,40},{40,32},{48,56},{56,48},{64,72... | collective-permute-start | bytes 122888 | tf_op jit(solution)/shard_map/ppermute | solution.py:594
  28.2 0.0 collective-permute-start.3
  28.2 0.0 copy-start
  28.2 0.0 copy-start.1
  28.2 2.3 %prepare_tiles.1.tile_ref = f32[16,49,8,128]{3,2,1,0:T(8,128)S(1)} custom-call(f32[16,8,128]{2,1,0:T(8,128)} %get-tuple-element.26.after_ref, f32[16,128,128]{2,1,0:T(8,128)} %bitcast.11, f32[16,128,128]{2,1,0:T(8,128)} %bitcast.12, f32[16,128,128]{2,1,0:T(8,128)} %bitcast.13), custom_call_target="tpu_custom_call" | custom-call | flops 300000 | bytes 3200000 | tf_op jit(solution)/shard_map/prepare_tiles/pallas_call | solution.py:352
  30.5 3.5 %all-to-all-done.1.winds_ref = f32[16,8,128]{2,1,0:T(8,128)S(1)} async-done(((f32[16,8,128]{2,1,0:T(8,128)}), f32[16,8,128]{2,1,0:T(8,128)S(1)}, u32[]{:S(2)}, u32[]{:S(2)}) %all-to-all-start.1) | async-done | bytes 65568 | tf_op jit(solution)/shard_map/all_to_all | solution.py:598
  34.0 0.0 copy-done
  34.0 0.0 copy-done.1
  34.0 7.5 %fire.1 = (f32[16,128,128]{2,1,0:T(8,128)}, f32[16,128,128]{2,1,0:T(8,128)}, f32[16,8,128]{2,1,0:T(8,128)S(1)}) custom-call(s32[16]{0:T(128)S(1)} %bitcast.8, s32[16]{0:T(128)S(1)} %bitcast.10, f32[16,8,128]{2,1,0:T(8,128)S(1)} %all-to-all-done.1.winds_ref, f32[16,49,8,128]{3,2,1,0:T(8,128)S(1)} %prepare_tiles.1.tile_ref), custom_call_target="tpu_custom_call" | custom-call | flops 50000000 | bytes 6500000 | tf_op jit(solution)/shard_map/fire/pallas_call | solution.py:484
  41.5 0.0 collective-permute-done.2.one_x_ref
  41.5 0.0 collective-permute-done.3.two_x_ref
  41.6 0.6 %sort_rows.1 = (f32[16,8,128]{2,1,0:T(8,128)}, f32[80,128]{1,0:T(8,128)S(1)}, f32[80,128]{1,0:T(8,128)S(1)}) custom-call(f32[16,8,128]{2,1,0:T(8,128)S(1)} %get-tuple-element.27.outbox_ref, f32[80,128]{1,0:T(8,128)S(1)} %collective-permute-done.2.one_x_ref, f32[80,128]{1,0:T(8,128)S(1)} %collective-permute-done.3.two_x_ref), custom_call_target="tpu_custom_call" | custom-call | tf_op jit(solution)/shard_map/sort_rows/pallas_call | solution.py:518
  42.2 4.2 %all-to-all-start.2 = ((f32[16,8,128]{2,1,0:T(8,128)}), f32[16,8,128]{2,1,0:T(8,128)S(1)}, u32[]{:S(2)}, u32[]{:S(2)}) async-start(f32[16,8,128]{2,1,0:T(8,128)} %get-tuple-element.30), calls=%async_computation.2 | async-start | bytes 131072 | tf_op jit(solution)/shard_map/all_to_all | solution.py:598
  46.4 4.9 %advect.1.part_ref = f32[80,64,128]{2,1,0:T(8,128)S(1)} custom-call(f32[80,64,128]{2,1,0:T(8,128)} %theta_ref.5, f32[80,64,128]{2,1,0:T(8,128)} %u_ref.3, f32[80,64,128]{2,1,0:T(8,128)} %v_ref.3, f32[80,128]{1,0:T(8,128)S(1)} %get-tuple-element.31.west_ref, f32[80,128]{1,0:T(8,128)S(1)} %get-tuple-element.32.east_ref, ...), custom_call_target="tpu_custom_call" | custom-call | flops 14000000 | bytes 8000000 | tf_op jit(solution)/shard_map/advect/pallas_call | solution.py:304
  51.3 2.7 %all-to-all-done.2.inbox_ref = f32[16,8,128]{2,1,0:T(8,128)S(1)} async-done(((f32[16,8,128]{2,1,0:T(8,128)}), f32[16,8,128]{2,1,0:T(8,128)S(1)}, u32[]{:S(2)}, u32[]{:S(2)}) %all-to-all-start.2) | async-done | bytes 65568 | tf_op jit(solution)/shard_map/all_to_all | solution.py:598
  54.1 2.1 %finish.1 = f32[80,64,128]{2,1,0:T(8,128)} custom-call(f32[16,8,128]{2,1,0:T(8,128)S(1)} %all-to-all-done.2.inbox_ref, f32[80,64,128]{2,1,0:T(8,128)S(1)} %advect.1.part_ref), custom_call_target="tpu_custom_call" | custom-call | flops 3000000 | bytes 2700000 | tf_op jit(solution)/shard_map/finish/pallas_call | solution.py:563
Async XLA Ops:
  2.5 15.6 %all-to-all-start = ((s32[16,8,128]{2,1,0:T(8,128)}), s32[16,8,128]{2,1,0:T(8,128)S(1)}, u32[]{:S(2)}, u32[]{:S(2)}) async-start(s32[16,8,128]{2,1,0:T(8,128)} %get-tuple-element.19), calls=%async_computation | async-start | bytes 131072 | tf_op jit(solution)/shard_map/all_to_all | solution.py:598
  12.5 3.2 %collective-permute-start = (f32[64,128]{1,0:T(8,128)S(1)}, f32[64,128]{1,0:T(8,128)S(1)}, u32[]{:S(2)}, u32[]{:S(2)}) collective-permute-start(f32[64,128]{1,0:T(8,128)S(1)} %get-tuple-element.22), channel_id=1, source_target_pairs={{0,1},{1,0},{2,3},{3,2},{4,5},{5,4},{6,7},{7,6},{8,9},{9,8},{10,11... | collective-permute-start | bytes 98312 | tf_op jit(solution)/shard_map/ppermute | solution.py:583
  12.6 4.7 %collective-permute-start.1 = (f32[64,128]{1,0:T(8,128)S(1)}, f32[64,128]{1,0:T(8,128)S(1)}, u32[]{:S(2)}, u32[]{:S(2)}) collective-permute-start(f32[64,128]{1,0:T(8,128)S(1)} %get-tuple-element.23), channel_id=1, source_target_pairs={{1,2},{2,1},{3,4},{4,3},{5,6},{6,5},{7,0},{0,7},{9,10},{10,9},{11,... | collective-permute-start | bytes 98312 | tf_op jit(solution)/shard_map/ppermute | solution.py:583
  19.8 14.1 %all-to-all-start.1 = ((f32[16,8,128]{2,1,0:T(8,128)}), f32[16,8,128]{2,1,0:T(8,128)S(1)}, u32[]{:S(2)}, u32[]{:S(2)}) async-start(f32[16,8,128]{2,1,0:T(8,128)} %get-tuple-element.26.after_ref), calls=%async_computation.1 | async-start | bytes 131072 | tf_op jit(solution)/shard_map/all_to_all | solution.py:598
  26.3 15.2 %collective-permute-start.2 = (f32[80,128]{1,0:T(8,128)S(1)}, f32[80,128]{1,0:T(8,128)S(1)}, u32[]{:S(2)}, u32[]{:S(2)}) collective-permute-start(f32[80,128]{1,0:T(8,128)S(1)} %get-tuple-element.28), channel_id=1, source_target_pairs={{0,8},{8,0},{16,24},{24,16},{32,40},{40,32},{48,56},{56,48},{64,72... | collective-permute-start | bytes 122888 | tf_op jit(solution)/shard_map/ppermute | solution.py:594
  28.2 13.3 %collective-permute-start.3 = (f32[80,128]{1,0:T(8,128)S(1)}, f32[80,128]{1,0:T(8,128)S(1)}, u32[]{:S(2)}, u32[]{:S(2)}) collective-permute-start(f32[80,128]{1,0:T(8,128)S(1)} %get-tuple-element.29), channel_id=1, source_target_pairs={{0,1},{1,0},{2,3},{3,2},{4,5},{5,4},{6,7},{7,6},{8,16},{9,17},{10,... | collective-permute-start | bytes 122888 | tf_op jit(solution)/shard_map/ppermute | solution.py:594
  28.2 5.8 %copy-start = (s32[1,1,16]{2,1,0:T(1,128)S(1)}, s32[1,1,16]{2,1,0:T(1,128)}, u32[]{:S(2)}) copy-start(s32[1,1,16]{2,1,0:T(1,128)} %param.14) | copy-start | bytes 196
  28.2 5.8 %copy-start.1 = (s32[1,1,16]{2,1,0:T(1,128)S(1)}, s32[1,1,16]{2,1,0:T(1,128)}, u32[]{:S(2)}) copy-start(s32[1,1,16]{2,1,0:T(1,128)} %param.15) | copy-start | bytes 196
  42.2 11.9 %all-to-all-start.2 = ((f32[16,8,128]{2,1,0:T(8,128)}), f32[16,8,128]{2,1,0:T(8,128)S(1)}, u32[]{:S(2)}, u32[]{:S(2)}) async-start(f32[16,8,128]{2,1,0:T(8,128)} %get-tuple-element.30), calls=%async_computation.2 | async-start | bytes 131072 | tf_op jit(solution)/shard_map/all_to_all | solution.py:598

commit v12 on v11

--- a/solution.py
+++ b/solution.py
@@ -245,8 +245,8 @@
 
 
 def advect_kernel(
-    theta_ref, u_ref, v_ref, west_ref, east_ref, one_y_ref, two_y_ref,
-    out_ref, theta, wind_u, wind_v, sems,
+    theta_ref, u_ref, v_ref, one_x_ref, two_x_ref, one_y_ref, two_y_ref,
+    out_ref, theta, wind_u, wind_v, west_ref, east_ref, sems,
 ):
     def copies(g):
         part = pl.ds(g * GROUP, GROUP)
@@ -259,6 +259,9 @@
     for g in range(GROUPS):
         for copy in copies(g):
             copy.start()
+    even, _ = place_on("gx")
+    west_ref[...] = jnp.where(even, two_x_ref[...], one_x_ref[...])
+    east_ref[...] = jnp.where(even, one_x_ref[...], two_x_ref[...])
     even, _ = place_on("gy")
     south = jnp.where(even, two_y_ref[...], one_y_ref[...])
     north = jnp.where(even, one_y_ref[...], two_y_ref[...])
@@ -310,6 +313,8 @@
             whole,
             whole,
             whole,
+            pltpu.VMEM((LZ, 128), F32),
+            pltpu.VMEM((LZ, 128), F32),
             pltpu.SemaphoreType.DMA((3, GROUPS)),
         ],
         name="advect",
@@ -506,23 +511,19 @@
     )(*(near(a) for a in (owners, places, winds, tiles_near)), *waits)
 
 
-def row_kernel(outbox_ref, one_x_ref, two_x_ref, outbox_out, west_ref, east_ref):
+def pass_kernel(outbox_ref, one_x_ref, two_x_ref, outbox_out):
     outbox_out[...] = outbox_ref[...]
-    even, _ = place_on("gx")
-    west_ref[...] = jnp.where(even, two_x_ref[...], one_x_ref[...])
-    east_ref[...] = jnp.where(even, one_x_ref[...], two_x_ref[...])
-
-
-def sort_rows(outbox, one_x, two_x):
-    row = pltpu.VMEM((LZ, 128), F32)
-    return pl.pallas_call(
-        row_kernel,
-        in_specs=[LOCAL] * 3,
-        out_specs=[LOCAL] * 3,
-        out_shape=[pltpu.VMEM(outbox.shape, F32), row, row],
-        name="sort_rows",
+
+
+def pass_on(outbox, one_x, two_x):
+    return pl.pallas_call(
+        pass_kernel,
+        in_specs=[LOCAL, ANYWHERE, ANYWHERE],
+        out_specs=LOCAL,
+        out_shape=pltpu.VMEM(outbox.shape, F32),
+        name="pass_on",
         compiler_params=params(4),
-    )(near(outbox), near(one_x), near(two_x))
+    )(near(outbox), one_x, two_x)
 
 
 def final_kernel(inbox_ref, part_ref, out_ref, field, result, sems):
@@ -545,16 +546,13 @@
         part = pl.ds(g * GROUP, GROUP)
         return pltpu.make_async_copy(result.at[part], out_ref.at[part], sems.at[g])
 
-    def one(g, carry):
+    for g in range(GROUPS):
         for k in range(GROUP):
             z = g * GROUP + k
             height = jnp.full((8, 128), z, jnp.int32).astype(F32)
             gain = heat_gain * jnp.exp((height + 0.5) * (-4.0 / LZ))
             result[z] = part_ref[z] + field[...] * jnp.concatenate([gain] * (CX // 8), axis=0)
         copy(g).start()
-        return carry
-
-    lax.fori_loop(0, GROUPS, one, 0)
     for g in range(GROUPS):
         copy(g).wait()
 
@@ -613,8 +611,8 @@
 
     tiles_near = prepare_tiles(patches, level_set[0, 0], fuel_load[0, 0], spread_base[0, 0])
     level_out, fuel_out, outbox = fire(owners, places, winds, tiles_near, peers, ())
-    outbox, west, east = sort_rows(outbox, *rims_x)
-    part = advect(theta, wind_u, wind_v, west, east, *rims_y)
+    outbox = pass_on(outbox, *rims_x)
+    part = advect(theta, wind_u, wind_v, *rims_x, *rims_y)
     inbox = exchange(outbox)
     theta_next = finish(inbox, part)
     return (theta_next, level_out[None, None], fuel_out[None, None])

time: 56.5 us -> 56.5 us (level)
  no operation moved by 1% of the time
where the time goes in v12:
time: 56.5 us; the launch traced here: 56.1 us
  starting transfers between devices  23.7 us (42%)
  Pallas kernels  23.1 us (41%)
  waiting for transfers between devices  8.58 us (15%)
  between operations  0.73 us (1%)
    all_to_all x3, starting transfers between devices, exchange(): return lax.all_to_all(cells, 'gx', split_axis=0, concat_axis=0, tiled=True)  18.6 us
    pallas_call x1, Pallas kernels, fire(): pl.pallas_call(functools.partial(fire_kernel, peers, len(waits)), in_spec...  7.54 us
    all_to_all x3, waiting for transfers between devices, exchange(): return lax.all_to_all(cells, 'gx', split_axis=0, concat_axis=0, tiled=True)  6.98 us
    pallas_call x1, Pallas kernels, advect(): pl.pallas_call(advect_kernel, in_specs=[FAR] * 3 + [LOCAL] * 4, out_specs...  4.94 us
    ppermute x2, starting transfers between devices, swapped_y(): return (lax.ppermute(one, 'gy', pairs), lax.ppermute(two, 'gy', others))  3.2 us
    pallas_call x1, Pallas kernels, prepare_tiles(): pl.pallas_call(tile_kernel, in_specs=[ANYWHERE, FAR, FAR, FAR], out_specs...  2.27 us
    pallas_call x1, Pallas kernels, make_edges(): pl.pallas_call(edge_kernel, in_specs=[LOCAL, LOCAL, FAR], out_specs=[LOCA...  2.06 us
    pallas_call x1, Pallas kernels, finish(): pl.pallas_call(final_kernel, in_specs=[LOCAL, LOCAL], out_specs=ANYWHERE,...  2.06 us
  transfers between devices with their start and end apart: 7, of which 4 were waited for; matrix products, arithmetic and copies ran while one was open for 0% of the time, Pallas kernels for 30%

profile of v12, /device:TPU:0, one launch (start us, length us, event | category | flops | bytes accessed | tf_op | source)
XLA Modules:
  0.0 56.1 jit_solution(4516448110942323340)
XLA Ops:
  0.6 1.8 %make_requests.1 = (s32[16,8,128]{2,1,0:T(8,128)}, f32[24,64,128]{2,1,0:T(8,128)S(1)}, f32[128,128]{1,0:T(8,128)S(1)}) custom-call(s32[16]{0:T(128)} %bitcast.7, s32[16]{0:T(128)} %bitcast.9, f32[80,64,128]{2,1,0:T(8,128)} %theta_ref.5, f32[80,64,128]{2,1,0:T(8,128)} %u_ref.3, f32[80,64,128]{2,1,0:T(8,128)} %v_ref.3), custom_call_target="tpu_custom_call" | custom-call | tf_op jit(solution)/shard_map/make_requests/pallas_call | solution.py:97
  2.5 8.0 %all-to-all-start = ((s32[16,8,128]{2,1,0:T(8,128)}), s32[16,8,128]{2,1,0:T(8,128)S(1)}, u32[]{:S(2)}, u32[]{:S(2)}) async-start(s32[16,8,128]{2,1,0:T(8,128)} %get-tuple-element.16), calls=%async_computation | async-start | bytes 131072 | tf_op jit(solution)/shard_map/all_to_all | solution.py:596
  10.5 2.1 %edges.1 = (f32[80,128]{1,0:T(8,128)S(1)}, f32[80,128]{1,0:T(8,128)S(1)}, f32[64,128]{1,0:T(8,128)S(1)}, f32[64,128]{1,0:T(8,128)S(1)}) custom-call(f32[24,64,128]{2,1,0:T(8,128)S(1)} %get-tuple-element.18.head_ref, f32[128,128]{1,0:T(8,128)S(1)} %get-tuple-element.17.block_ref, f32[80,64,128]{2,1,0:T(8,128)} %theta_ref.5), custom_call_target="tpu_custom_call" | custom-call | flops 4000000 | bytes 2700000 | tf_op jit(solution)/shard_map/edges/pallas_call | solution.py:159
  12.5 0.1 collective-permute-start
  12.6 3.1 %collective-permute-start.1 = (f32[64,128]{1,0:T(8,128)S(1)}, f32[64,128]{1,0:T(8,128)S(1)}, u32[]{:S(2)}, u32[]{:S(2)}) collective-permute-start(f32[64,128]{1,0:T(8,128)S(1)} %get-tuple-element.20), channel_id=1, source_target_pairs={{1,2},{2,1},{3,4},{4,3},{5,6},{6,5},{7,0},{0,7},{9,10},{10,9},{11,... | collective-permute-start | bytes 98312 | tf_op jit(solution)/shard_map/ppermute | solution.py:581
  15.7 0.0 collective-permute-done.one_y_ref
  15.7 1.6 %collective-permute-done.1.two_y_ref = f32[64,128]{1,0:T(8,128)S(1)} collective-permute-done((f32[64,128]{1,0:T(8,128)S(1)}, f32[64,128]{1,0:T(8,128)S(1)}, u32[]{:S(2)}, u32[]{:S(2)}) %collective-permute-start.1) | collective-permute-done | bytes 32800 | tf_op jit(solution)/shard_map/ppermute | solution.py:581
  17.3 0.8 %all-to-all-done.asked_far = s32[16,8,128]{2,1,0:T(8,128)S(1)} async-done(((s32[16,8,128]{2,1,0:T(8,128)}), s32[16,8,128]{2,1,0:T(8,128)S(1)}, u32[]{:S(2)}, u32[]{:S(2)}) %all-to-all-start) | async-done | bytes 65568 | tf_op jit(solution)/shard_map/all_to_all | solution.py:596
  18.1 1.7 %cut_patches.1 = (f32[16,8,128]{2,1,0:T(8,128)}, f32[80,128]{1,0:T(8,128)S(1)}, f32[80,128]{1,0:T(8,128)S(1)}) custom-call(s32[16,8,128]{2,1,0:T(8,128)S(1)} %all-to-all-done.asked_far, f32[128,128]{1,0:T(8,128)S(1)} %get-tuple-element.17.block_ref, f32[64,128]{1,0:T(8,128)S(1)} %collective-permute-done.one_y_ref, ...), custom_call_target="tpu_custom_call" | custom-call | tf_op jit(solution)/shard_map/cut_patches/pallas_call | solution.py:230
  19.8 6.4 %all-to-all-start.1 = ((f32[16,8,128]{2,1,0:T(8,128)}), f32[16,8,128]{2,1,0:T(8,128)S(1)}, u32[]{:S(2)}, u32[]{:S(2)}) async-start(f32[16,8,128]{2,1,0:T(8,128)} %get-tuple-element.23.after_ref), calls=%async_computation.1 | async-start | bytes 131072 | tf_op jit(solution)/shard_map/all_to_all | solution.py:596
  26.3 1.9 %collective-permute-start.2 = (f32[80,128]{1,0:T(8,128)S(1)}, f32[80,128]{1,0:T(8,128)S(1)}, u32[]{:S(2)}, u32[]{:S(2)}) collective-permute-start(f32[80,128]{1,0:T(8,128)S(1)} %get-tuple-element.25), channel_id=1, source_target_pairs={{0,8},{8,0},{16,24},{24,16},{32,40},{40,32},{48,56},{56,48},{64,72... | collective-permute-start | bytes 122888 | tf_op jit(solution)/shard_map/ppermute | solution.py:592
  28.2 0.0 collective-permute-start.3
  28.2 0.0 copy-start
  28.2 0.0 copy-start.1
  28.2 2.3 %prepare_tiles.1.tile_ref = f32[16,49,8,128]{3,2,1,0:T(8,128)S(1)} custom-call(f32[16,8,128]{2,1,0:T(8,128)} %get-tuple-element.23.after_ref, f32[16,128,128]{2,1,0:T(8,128)} %bitcast.11, f32[16,128,128]{2,1,0:T(8,128)} %bitcast.12, f32[16,128,128]{2,1,0:T(8,128)} %bitcast.13), custom_call_target="tpu_custom_call" | custom-call | flops 300000 | bytes 3200000 | tf_op jit(solution)/shard_map/prepare_tiles/pallas_call | solution.py:357
  30.5 3.5 %all-to-all-done.1.winds_ref = f32[16,8,128]{2,1,0:T(8,128)S(1)} async-done(((f32[16,8,128]{2,1,0:T(8,128)}), f32[16,8,128]{2,1,0:T(8,128)S(1)}, u32[]{:S(2)}, u32[]{:S(2)}) %all-to-all-start.1) | async-done | bytes 65568 | tf_op jit(solution)/shard_map/all_to_all | solution.py:596
  34.0 0.0 copy-done
  34.0 0.0 copy-done.1
  34.0 7.5 %fire.1 = (f32[16,128,128]{2,1,0:T(8,128)}, f32[16,128,128]{2,1,0:T(8,128)}, f32[16,8,128]{2,1,0:T(8,128)S(1)}) custom-call(s32[16]{0:T(128)S(1)} %bitcast.8, s32[16]{0:T(128)S(1)} %bitcast.10, f32[16,8,128]{2,1,0:T(8,128)S(1)} %all-to-all-done.1.winds_ref, f32[16,49,8,128]{3,2,1,0:T(8,128)S(1)} %prepare_tiles.1.tile_ref), custom_call_target="tpu_custom_call" | custom-call | flops 50000000 | bytes 6500000 | tf_op jit(solution)/shard_map/fire/pallas_call | solution.py:489
  41.5 0.0 collective-permute-done.2.one_x_ref
  41.5 0.0 collective-permute-done.3.two_x_ref
  41.6 0.6 %pass_on.1 = f32[16,8,128]{2,1,0:T(8,128)} custom-call(f32[16,8,128]{2,1,0:T(8,128)S(1)} %get-tuple-element.24.outbox_ref, f32[80,128]{1,0:T(8,128)S(1)} %collective-permute-done.2.one_x_ref, f32[80,128]{1,0:T(8,128)S(1)} %collective-permute-done.3.two_x_ref), custom_call_target="tpu_custom_call" | custom-call | tf_op jit(solution)/shard_map/pass_on/pallas_call | solution.py:519
  42.2 4.2 %all-to-all-start.2 = ((f32[16,8,128]{2,1,0:T(8,128)}), f32[16,8,128]{2,1,0:T(8,128)S(1)}, u32[]{:S(2)}, u32[]{:S(2)}) async-start(f32[16,8,128]{2,1,0:T(8,128)} %pass_on.1), calls=%async_computation.2 | async-start | bytes 131072 | tf_op jit(solution)/shard_map/all_to_all | solution.py:596
  46.4 4.9 %advect.1.part_ref = f32[80,64,128]{2,1,0:T(8,128)S(1)} custom-call(f32[80,64,128]{2,1,0:T(8,128)} %theta_ref.5, f32[80,64,128]{2,1,0:T(8,128)} %u_ref.3, f32[80,64,128]{2,1,0:T(8,128)} %v_ref.3, f32[80,128]{1,0:T(8,128)S(1)} %collective-permute-done.2.one_x_ref, f32[80,128]{1,0:T(8,128)S(1)} %collective-permute-done.3.two_x_ref, ...), custom_call_target="tpu_custom_call" | custom-call | flops 14000000 | bytes 8000000 | tf_op jit(solution)/shard_map/advect/pallas_call | solution.py:307
  51.3 2.7 %all-to-all-done.2.inbox_ref = f32[16,8,128]{2,1,0:T(8,128)S(1)} async-done(((f32[16,8,128]{2,1,0:T(8,128)}), f32[16,8,128]{2,1,0:T(8,128)S(1)}, u32[]{:S(2)}, u32[]{:S(2)}) %all-to-all-start.2) | async-done | bytes 65568 | tf_op jit(solution)/shard_map/all_to_all | solution.py:596
  54.1 2.1 %finish.1 = f32[80,64,128]{2,1,0:T(8,128)} custom-call(f32[16,8,128]{2,1,0:T(8,128)S(1)} %all-to-all-done.2.inbox_ref, f32[80,64,128]{2,1,0:T(8,128)S(1)} %advect.1.part_ref), custom_call_target="tpu_custom_call" | custom-call | flops 3000000 | bytes 2700000 | tf_op jit(solution)/shard_map/finish/pallas_call | solution.py:561
Async XLA Ops:
  2.5 15.6 %all-to-all-start = ((s32[16,8,128]{2,1,0:T(8,128)}), s32[16,8,128]{2,1,0:T(8,128)S(1)}, u32[]{:S(2)}, u32[]{:S(2)}) async-start(s32[16,8,128]{2,1,0:T(8,128)} %get-tuple-element.16), calls=%async_computation | async-start | bytes 131072 | tf_op jit(solution)/shard_map/all_to_all | solution.py:596
  12.5 3.2 %collective-permute-start = (f32[64,128]{1,0:T(8,128)S(1)}, f32[64,128]{1,0:T(8,128)S(1)}, u32[]{:S(2)}, u32[]{:S(2)}) collective-permute-start(f32[64,128]{1,0:T(8,128)S(1)} %get-tuple-element.19), channel_id=1, source_target_pairs={{0,1},{1,0},{2,3},{3,2},{4,5},{5,4},{6,7},{7,6},{8,9},{9,8},{10,11... | collective-permute-start | bytes 98312 | tf_op jit(solution)/shard_map/ppermute | solution.py:581
  12.6 4.7 %collective-permute-start.1 = (f32[64,128]{1,0:T(8,128)S(1)}, f32[64,128]{1,0:T(8,128)S(1)}, u32[]{:S(2)}, u32[]{:S(2)}) collective-permute-start(f32[64,128]{1,0:T(8,128)S(1)} %get-tuple-element.20), channel_id=1, source_target_pairs={{1,2},{2,1},{3,4},{4,3},{5,6},{6,5},{7,0},{0,7},{9,10},{10,9},{11,... | collective-permute-start | bytes 98312 | tf_op jit(solution)/shard_map/ppermute | solution.py:581
  19.8 14.1 %all-to-all-start.1 = ((f32[16,8,128]{2,1,0:T(8,128)}), f32[16,8,128]{2,1,0:T(8,128)S(1)}, u32[]{:S(2)}, u32[]{:S(2)}) async-start(f32[16,8,128]{2,1,0:T(8,128)} %get-tuple-element.23.after_ref), calls=%async_computation.1 | async-start | bytes 131072 | tf_op jit(solution)/shard_map/all_to_all | solution.py:596
  26.3 15.2 %collective-permute-start.2 = (f32[80,128]{1,0:T(8,128)S(1)}, f32[80,128]{1,0:T(8,128)S(1)}, u32[]{:S(2)}, u32[]{:S(2)}) collective-permute-start(f32[80,128]{1,0:T(8,128)S(1)} %get-tuple-element.25), channel_id=1, source_target_pairs={{0,8},{8,0},{16,24},{24,16},{32,40},{40,32},{48,56},{56,48},{64,72... | collective-permute-start | bytes 122888 | tf_op jit(solution)/shard_map/ppermute | solution.py:592
  28.2 13.3 %collective-permute-start.3 = (f32[80,128]{1,0:T(8,128)S(1)}, f32[80,128]{1,0:T(8,128)S(1)}, u32[]{:S(2)}, u32[]{:S(2)}) collective-permute-start(f32[80,128]{1,0:T(8,128)S(1)} %get-tuple-element.26), channel_id=1, source_target_pairs={{0,1},{1,0},{2,3},{3,2},{4,5},{5,4},{6,7},{7,6},{8,16},{9,17},{10,... | collective-permute-start | bytes 122888 | tf_op jit(solution)/shard_map/ppermute | solution.py:592
  28.2 5.8 %copy-start = (s32[1,1,16]{2,1,0:T(1,128)S(1)}, s32[1,1,16]{2,1,0:T(1,128)}, u32[]{:S(2)}) copy-start(s32[1,1,16]{2,1,0:T(1,128)} %param.14) | copy-start | bytes 196
  28.2 5.8 %copy-start.1 = (s32[1,1,16]{2,1,0:T(1,128)S(1)}, s32[1,1,16]{2,1,0:T(1,128)}, u32[]{:S(2)}) copy-start(s32[1,1,16]{2,1,0:T(1,128)} %param.15) | copy-start | bytes 196
  42.2 11.9 %all-to-all-start.2 = ((f32[16,8,128]{2,1,0:T(8,128)}), f32[16,8,128]{2,1,0:T(8,128)S(1)}, u32[]{:S(2)}, u32[]{:S(2)}) async-start(f32[16,8,128]{2,1,0:T(8,128)} %pass_on.1), calls=%async_computation.2 | async-start | bytes 131072 | tf_op jit(solution)/shard_map/all_to_all | solution.py:596
